TPU v7x, 32 devices: a whole 2x2x4 slice. The times are simulated.
32 devices in a mesh: replica: 2 (over y), expert: 4 (over z), dp: 4 (over x, core).
Axes of the slice: x: 2, y: 2, z: 4, core: 2. Of those that a mesh axis runs over, the one named last changes fastest.
Arguments:
- queries: bfloat16 [192, 2, 4096], P(('replica', 'expert', 'dp')), parts along dimension 0, may hold values from -128 to 128
- new_keys: bfloat16 [192, 2, 256], P(('replica', 'expert', 'dp')), parts along dimension 0, may hold values from -6 to 6
- new_values: bfloat16 [192, 2, 256], P(('replica', 'expert', 'dp')), parts along dimension 0, may hold values from -6 to 6
- cache_keys: bfloat16 [192, 32, 256], P(('replica', 'expert', 'dp')), parts along dimension 0, may hold values from -6 to 6
- cache_values: bfloat16 [192, 32, 256], P(('replica', 'expert', 'dp')), parts along dimension 0, may hold values from -6 to 6
- lengths: int32 [192], P(('replica', 'expert', 'dp')), parts along dimension 0, may hold values from 18 to 32, as said below
- image_grid: int32 [192, 2], P(('replica', 'expert', 'dp')), parts along dimension 0, may hold values from 1 to 4
- residual: bfloat16 [192, 2, 4096], P(('replica', 'expert', 'dp')), parts along dimension 0, may hold values from -6 to 6
- norm_gain: bfloat16 [4096], replicated, may hold values from 0.5 to 2
- routes: int32 [192, 2, 8], P(('replica', 'expert', 'dp')), parts along dimension 0, may hold values from 0 to 63, all different within a row; in each aligned block of 12 rows (0 to 11, 12 to 23, ..., all dimensions but the last counted through in order) at most 2 rows name the same one
- route_gains: float32 [192, 2, 8], P(('replica', 'expert', 'dp')), parts along dimension 0, may hold values from 0.1 to 1
- w_gate: bfloat16 [64, 4096, 768], P('expert', None, 'dp'), may hold values from -0.09375 to 0.09375
- w_up: bfloat16 [64, 4096, 768], P('expert', None, 'dp'), may hold values from -0.09375 to 0.09375
- w_down: bfloat16 [64, 768, 4096], P('expert', 'dp'), may hold values from -0.21875 to 0.21875
Outputs:
- layer_out: bfloat16 [192, 2, 4096], P(('replica', 'expert', 'dp')), parts along dimension 0
There are 2 independent parts, one for each index of `replica`. A program takes and returns all parts, laid end to end along the dimension named above; an argument that names none is the same for every part. Nothing has to cross between parts.
Inputs may be any that keep to these rules, and one draw needn't show every extreme that they name: `routes`: each row names 8 different experts at each step. In the rows of one device (aligned blocks of 6 rows, both steps together) no expert is named more than 2 times. `lengths`: every row's cache holds its image tokens and at least two more live positions.
All inputs are finite; a program needn't handle non-finite values.
Results may differ from a plain program's by a relative error of at most 0.008.
Values may be sent and summed in bfloat16 or wider, within the bound.
No kernel may reach another device: no remote copies, remote signals or barrier semaphores. Data moves between devices by JAX's collectives and lax.ppermute only.
A program may use at most 192 MiB of HBM per device.

v0:
```python
import math

import jax
import jax.numpy as jnp
from jax import lax
from jax.sharding import PartitionSpec as P

HEAD_DIM = 128
TOP = 8
CAP = 2


THETA = 5000000.0
EPS = 1e-06
MASKED = -1e30


def rotate(vectors, where):
    half = vectors.shape[-1] // 2
    freq = THETA ** (-2.0 * jnp.arange(half, dtype=jnp.float32) / vectors.shape[-1])
    angle = where[..., None] * freq
    cosine = jnp.cos(angle)
    sine = jnp.sin(angle)
    first = vectors[..., :half]
    second = vectors[..., half:]
    return jnp.concatenate(
        [first * cosine - second * sine, second * cosine + first * sine], axis=-1
    )


def attend(queries, new_keys, new_values, cache_keys, cache_values, lengths, image_grid):
    count = queries.shape[0]
    steps = queries.shape[1]
    ctx = cache_keys.shape[1]
    kv_count = cache_keys.shape[2] // HEAD_DIM
    group = queries.shape[2] // HEAD_DIM // kv_count
    base = (
        lengths
        - image_grid[:, 0] * image_grid[:, 1]
        + jnp.maximum(image_grid[:, 0], image_grid[:, 1])
    )
    where = (base[:, None] + jnp.arange(steps, dtype=jnp.int32)[None, :]).astype(jnp.float32)
    query = rotate(
        queries.astype(jnp.float32).reshape(count, steps, kv_count, group, HEAD_DIM),
        where[:, :, None, None],
    )
    fresh = rotate(
        new_keys.astype(jnp.float32).reshape(count, steps, kv_count, HEAD_DIM), where[:, :, None]
    )
    cached = cache_keys.astype(jnp.float32).reshape(count, ctx, kv_count, HEAD_DIM)
    scale = 1.0 / math.sqrt(HEAD_DIM)
    old_scores = (
        jnp.einsum("rsgqd,rcgd->rsgqc", query, cached, precision=lax.Precision.HIGHEST) * scale
    )
    new_scores = (
        jnp.einsum("rsgqd,rtgd->rsgqt", query, fresh, precision=lax.Precision.HIGHEST) * scale
    )
    live = jnp.arange(ctx, dtype=jnp.int32)[None, :] < lengths[:, None]
    old_scores = jnp.where(live[:, None, None, None, :], old_scores, MASKED)
    causal = (
        jnp.arange(steps, dtype=jnp.int32)[None, :] <= jnp.arange(steps, dtype=jnp.int32)[:, None]
    )
    new_scores = jnp.where(causal[None, :, None, None, :], new_scores, MASKED)
    scores = jnp.concatenate([old_scores, new_scores], axis=-1)
    top = jnp.max(scores, axis=-1, keepdims=True)
    weights = jnp.exp(scores - top)
    probs = (weights / jnp.sum(weights, axis=-1, keepdims=True)).astype(jnp.bfloat16)
    values = jnp.concatenate(
        [
            cache_values.reshape(count, ctx, kv_count, HEAD_DIM),
            new_values.reshape(count, steps, kv_count, HEAD_DIM),
        ],
        axis=1,
    )
    out = jnp.einsum("rsgqc,rcgd->rsgqd", probs, values, preferred_element_type=jnp.float32)
    return out.astype(jnp.bfloat16).reshape(count, steps, -1)


def shards(
    queries,
    new_keys,
    new_values,
    cache_keys,
    cache_values,
    lengths,
    image_grid,
    residual,
    norm_gain,
    routes,
    route_gains,
    w_gate,
    w_up,
    w_down,
):
    rows, steps, width = residual.shape
    attended = attend(queries, new_keys, new_values, cache_keys, cache_values, lengths, image_grid)
    mixed = residual.astype(jnp.float32) + attended.astype(jnp.float32)
    normed = (
        mixed
        * lax.rsqrt(jnp.mean(mixed * mixed, axis=-1, keepdims=True) + EPS)
        * norm_gain.astype(jnp.float32)
    ).astype(jnp.bfloat16)
    shares = (route_gains / jnp.sum(route_gains, axis=-1, keepdims=True)).astype(jnp.bfloat16)
    members = lax.axis_size("expert")
    local = w_gate.shape[0]
    places = members * CAP * local
    picks = routes.reshape(-1)
    onehot = (picks[:, None] == jnp.arange(members * local, dtype=jnp.int32)[None, :]).astype(
        jnp.int32
    )
    earlier = jnp.sum((jnp.cumsum(onehot, axis=0) - onehot) * onehot, axis=1)
    target = picks // local * (CAP * local) + earlier * local + picks % local
    placed = (target[:, None] == jnp.arange(places, dtype=jnp.int32)[None, :]).reshape(
        rows * steps, TOP, places
    )
    chooser = jnp.sum(placed.astype(jnp.float32), axis=1).astype(jnp.bfloat16)
    weigher = jnp.sum(
        jnp.where(
            placed, shares.reshape(rows * steps, TOP, 1).astype(jnp.float32), jnp.float32(0.0)
        ),
        axis=1,
    ).astype(jnp.bfloat16)
    outgoing = jnp.einsum(
        "jp,jd->pd",
        chooser,
        normed.reshape(rows * steps, width),
        preferred_element_type=jnp.float32,
    )
    outgoing = outgoing.astype(jnp.bfloat16).reshape(members, CAP, local, width)
    incoming = lax.all_to_all(outgoing, "expert", split_axis=0, concat_axis=0, tiled=True)
    flat = incoming.reshape(-1, local, width)
    piece = lax.all_gather(flat, "dp", axis=0, tiled=True)
    gate = jnp.einsum("red,edh->reh", piece, w_gate, preferred_element_type=jnp.float32)
    upper = jnp.einsum("red,edh->reh", piece, w_up, preferred_element_type=jnp.float32)
    hidden = (jax.nn.silu(gate) * upper).astype(jnp.bfloat16)
    piece = hidden
    result = lax.psum_scatter(
        jnp.einsum("reh,ehd->red", piece, w_down, preferred_element_type=jnp.float32).astype(
            jnp.bfloat16
        ),
        "dp",
        scatter_dimension=0,
        tiled=True,
    )
    returned = lax.all_to_all(
        result.reshape(incoming.shape), "expert", split_axis=0, concat_axis=0, tiled=True
    )
    routed = jnp.dot(weigher, returned.reshape(places, width), preferred_element_type=jnp.float32)
    layer_out = mixed.reshape(rows * steps, width) + routed
    return layer_out.astype(jnp.bfloat16).reshape(rows, steps, width)


def solution(mesh):
    placed = (
        P(("replica", "expert", "dp"), None, None),
        P(("replica", "expert", "dp"), None, None),
        P(("replica", "expert", "dp"), None, None),
        P(("replica", "expert", "dp"), None, None),
        P(("replica", "expert", "dp"), None, None),
        P(("replica", "expert", "dp")),
        P(("replica", "expert", "dp"), None),
        P(("replica", "expert", "dp"), None, None),
        P(),
        P(("replica", "expert", "dp"), None, None),
        P(("replica", "expert", "dp"), None, None),
        P("expert", None, "dp"),
        P("expert", None, "dp"),
        P("expert", "dp", None),
    )
    return jax.shard_map(
        shards,
        mesh=mesh,
        in_specs=placed,
        out_specs=P(("replica", "expert", "dp"), None, None),
        check_vma=False,
    )
```

profile of v0, /device:TPU:0, one launch (start us, length us, event | category | flops | bytes accessed | tf_op | source)
XLA Modules:
  0.0 213.3 jit_solution(7096348705756631557)
XLA Ops:
  6.6 0.8 eq.31
  7.4 0.7 reshape.252
  8.1 0.7 iota_compare_fusion.2
  8.8 0.8 bitcast_add_fusion
  9.6 1.0 reshape.260
  10.7 0.7 bitcast_convert_fusion
  11.4 0.9 reshape.248
  12.3 0.2 multiply_cosine_fusion
  12.7 1.5 fusion.23
  14.3 0.2 copy.47
  14.6 0.4 fusion.45
  15.0 0.3 fusion.26
  15.3 1.0 fusion.8
  16.5 1.1 multiply_reduce_fusion
  17.6 0.7 convert_element_type.94
  18.3 0.2 multiply_convert_fusion
  18.6 0.1 reduce_window_sum.11
  18.8 0.2 select_reduce_fusion.1
  19.0 0.9 fusion.11
  20.1 0.5 convolution_convert_fusion.1
  20.5 31.8 %all_to_all.10 = bf16[4,2,16,4096]{3,2,1,0:T(8,128)(2,1)S(1)} all-to-all(bf16[4,2,16,4096]{3,2,1,0:T(8,128)(2,1)S(1)} %bitcast.67), channel_id=1, replica_groups=mesh['replica'=2,'expert'=4,'dp'=4] {'expert'}, dimensions={0} | all-to-all | bytes 2097152 | tf_op jit(solution)/shard_map/all_to_all | solution.py:130
  52.4 1.6 copy.56
  54.0 33.7 %all-gather.2.cloned.1.call-done = bf16[32,16,4096]{2,0,1:T(8,128)(2,1)} async-done(((bf16[8,16,4096]{2,0,1:T(8,128)(2,1)}), bf16[32,16,4096]{2,0,1:T(8,128)(2,1)}) %all-gather.2.cloned.1.call-update) | async-done | bytes 4194320 | tf_op jit(solution)/shard_map/all_gather | solution.py:132
  87.7 13.4 %convolution_bitcast_fusion.1 = f32[32,16,192]{2,0,1:T(8,128)S(1)} fusion(bf16[32,16,4096]{2,0,1:T(8,128)(2,1)} %all-gather.2.cloned.1.call-done, bf16[16,4096,192]{1,2,0:T(8,128)(2,1)} %param.25), kind=kOutput, calls=%fused_computation.7 | convolution fusion | flops 805306368 | bytes 29753344 | tf_op jit(solution)/shard_map/red,edh->reh/dot_general | solution.py:133
  101.1 22.0 %fusion.1 = bf16[16,4,8,4096]{3,2,1,0:T(8,128)(2,1)} fusion(bf16[16,192,4096]{2,1,0:T(8,128)(2,1)} %param.27, bf16[32,16,4096]{2,0,1:T(8,128)(2,1)} %all-gather.2.cloned.1.call-done, bf16[16,4096,192]{1,2,0:T(8,128)(2,1)} %param.26, f32[32,16,192]{2,0,1:T(8,128)S(1)} %convolution_bitcast_fusion.1), kind=kOutput, calls=%fused_computation.2 | convolution fusion | flops 1613299712 | bytes 59113472 | tf_op jit(solution)/shard_map/reh,ehd->red/dot_general | solution.py:138
  123.1 4.6 %copy.62 = bf16[16,4,8,4096]{3,2,0,1:T(8,128)(2,1)} copy(bf16[16,4,8,4096]{3,2,1,0:T(8,128)(2,1)} %fusion.1) | data formatting | bytes 8388608
  127.7 44.7 %reduce-scatter.4.cloned.1.call-done = bf16[8,65536]{1,0:T(8,128)(2,1)} async-done(((bf16[32,65536]{1,0:T(8,128)(2,1)}), bf16[8,65536]{1,0:T(8,128)(2,1)}) %reduce-scatter.4.cloned.1.call-update) | async-done | bytes 1048592
  172.4 2.8 %copy.50 = bf16[8,16,4096]{2,1,0:T(8,128)(2,1)} copy(bf16[8,16,4096]{2,0,1:T(8,128)(2,1)} %bitcast.69) | data formatting | bytes 2097152 | tf_op jit(solution)/shard_map/reduce_scatter | solution.py:137
  175.2 4.6 %all-to-all-start.1 = ((bf16[4,2,16,4096]{3,2,1,0:T(8,128)(2,1)}), bf16[4,2,16,4096]{3,2,1,0:T(8,128)(2,1)S(1)}, u32[]{:S(2)}, u32[]{:S(2)}) async-start(bf16[4,2,16,4096]{3,2,1,0:T(8,128)(2,1)} %bitcast.18), calls=%async_computation.1 | async-start | bytes 2097152 | tf_op jit(solution)/shard_map/all_to_all | solution.py:145
  179.9 25.6 %all-to-all-done.1 = bf16[4,2,16,4096]{3,2,1,0:T(8,128)(2,1)S(1)} async-done(((bf16[4,2,16,4096]{3,2,1,0:T(8,128)(2,1)}), bf16[4,2,16,4096]{3,2,1,0:T(8,128)(2,1)S(1)}, u32[]{:S(2)}, u32[]{:S(2)}) %all-to-all-start.1) | async-done | bytes 1048608 | tf_op jit(solution)/shard_map/all_to_all | solution.py:145
  205.5 0.3 fusion.2
  205.8 0.7 reshape.258
  (26 shorter events, 1.2 us)
Async XLA Ops:
  6.5 8.0 %copy-start = (bf16[6,32,256]{2,1,0:T(8,128)(2,1)S(1)}, bf16[6,32,256]{2,1,0:T(8,128)(2,1)}, u32[]{:S(2)}) copy-start(bf16[6,32,256]{2,1,0:T(8,128)(2,1)} %param.18) | copy-start | bytes 294916
  6.5 81.2 %all-gather.2.cloned.1.call-start = ((), (), s32[]{:S(2)}) async-start(), calls=%async_computation.3 | async-start | bytes 5242880 | tf_op jit(solution)/shard_map/all_gather | solution.py:132
  53.9 118.4 %reduce-scatter.4.cloned.1.call-start = ((), (), s32[]{:S(2)}) async-start(), calls=%async_computation.4 | async-start | bytes 5242880
  175.2 30.3 %all-to-all-start.1 = ((bf16[4,2,16,4096]{3,2,1,0:T(8,128)(2,1)}), bf16[4,2,16,4096]{3,2,1,0:T(8,128)(2,1)S(1)}, u32[]{:S(2)}, u32[]{:S(2)}) async-start(bf16[4,2,16,4096]{3,2,1,0:T(8,128)(2,1)} %bitcast.18), calls=%async_computation.1 | async-start | bytes 2097152 | tf_op jit(solution)/shard_map/all_to_all | solution.py:145
Sparse Core Ops, SparseCore 0:
  54.1 33.5 all-gather.1
  127.8 44.4 reduce-scatter.3
where the time goes:
time: 214 us; the launch traced here: 213 us
  waiting for transfers between devices  104 us (49%)
  matrix products  39.1 us (18%)
  blocking collectives  31.8 us (15%)
  local copies, waits for them, and re-layouts  13.8 us (6%)
  between operations  13.6 us (6%)
  other arithmetic  6.38 us (3%)
  starting transfers between devices  4.64 us (2%)
    unnamed x3, waiting for transfers between devices  44.7 us
    all_gather x1, waiting for transfers between devices, shards(): piece = lax.all_gather(flat, 'dp', axis=0, tiled=True)  33.7 us
    all_to_all x1, blocking collectives, shards(): lax.all_to_all(outgoing, 'expert', split_axis=0, concat_axis=0, tiled=True)  31.8 us
    all_to_all x1, waiting for transfers between devices, shards(): lax.all_to_all(result.reshape(incoming.shape), 'expert', split_axis=0, co...  25.6 us
    dot_general x1, matrix products, shards(): jnp.einsum('reh,ehd->red', piece, w_down, preferred_element_type=jnp.floa...  22 us
    dot_general x1, matrix products, shards(): jnp.einsum('red,edh->reh', piece, w_gate, preferred_element_type=jnp.floa...  13.4 us
    unnamed x3, local copies, waits for them, and re-layouts  4.61 us
    all_to_all x1, starting transfers between devices, shards(): lax.all_to_all(result.reshape(incoming.shape), 'expert', split_axis=0, co...  4.6 us
  transfers between devices with their start and end apart: 3, of which 3 were waited for; matrix products, arithmetic and copies ran while one was open for 0% of the time, Pallas kernels for 0%

commit v1 on v0

--- a/solution.py
+++ b/solution.py
@@ -1,8 +1,11 @@
+import functools
 import math
 
 import jax
 import jax.numpy as jnp
 from jax import lax
+from jax.experimental import pallas as pl
+from jax.experimental.pallas import tpu as pltpu
 from jax.sharding import PartitionSpec as P
 
 HEAD_DIM = 128
@@ -150,6 +153,266 @@
     return layer_out.astype(jnp.bfloat16).reshape(rows, steps, width)
 
 
+VMEM = pl.BlockSpec(memory_space=pltpu.VMEM)
+SMEM = pl.BlockSpec(memory_space=pltpu.SMEM)
+LANES = 128
+MAIN = 8
+
+
+def stack(parts, axis=0):
+    return jnp.concatenate(parts, axis=axis)
+
+
+def front_kernel(
+    q_ref, nk_ref, nv_ref, ck_ref, cv_ref, len_ref, grid_ref, res_ref, gain_ref, routes_ref,
+    gains_ref, pay_ref, mixed_ref,
+):
+    rows, steps, width = q_ref.shape
+    ctx = ck_ref.shape[1]
+    kv_count = ck_ref.shape[2] // HEAD_DIM
+    group = width // HEAD_DIM // kv_count
+    half = HEAD_DIM // 2
+    tall = group * steps
+    fresh_pad = 8
+    keys = ctx + fresh_pad
+    lane = lax.broadcasted_iota(jnp.int32, (8, HEAD_DIM), 1)
+    freq = jnp.exp((lane % half).astype(jnp.float32) * (-2.0 * math.log(THETA) / HEAD_DIM))
+    sub = lax.broadcasted_iota(jnp.int32, (8, HEAD_DIM), 0)
+    flip = jnp.where(lane < half, -1.0, 1.0)
+    head_step = lax.broadcasted_iota(jnp.int32, (tall, keys), 0) % steps
+    column = lax.broadcasted_iota(jnp.int32, (tall, keys), 1)
+    fresh_live = (column >= ctx) & (column - ctx <= head_step)
+    scale = 1.0 / math.sqrt(HEAD_DIM)
+
+    def turn(vectors, cosine, sine):
+        return vectors * cosine + pltpu.roll(vectors, half, 1) * sine
+
+    normed = []
+    for r in range(rows):
+        length = len_ref[r]
+        high, wide = grid_ref[r, 0], grid_ref[r, 1]
+        base = length - high * wide + jnp.maximum(high, wide)
+        angle = (base + sub % steps).astype(jnp.float32) * freq
+        cosine = jnp.cos(angle)
+        sine = jnp.sin(angle) * flip
+        cosines = stack([cosine] * (tall // 8))
+        sines = stack([sine] * (tall // 8))
+        live = (column < jnp.minimum(length, ctx)) | fresh_live
+        q_r = q_ref[r].astype(jnp.float32)
+        nk_r = nk_ref[r].astype(jnp.float32)
+        nv_r = nv_ref[r].astype(jnp.float32)
+        ck_r = ck_ref[r].astype(jnp.float32)
+        cv_r = cv_ref[r].astype(jnp.float32)
+        blank = jnp.zeros((fresh_pad - steps, HEAD_DIM), jnp.float32)
+        pieces = []
+        for g in range(kv_count):
+            cols = slice(g * HEAD_DIM, (g + 1) * HEAD_DIM)
+            first = g * group
+            query = stack(
+                [q_r[:, (first + h) * HEAD_DIM : (first + h + 1) * HEAD_DIM] for h in range(group)]
+            )
+            query = turn(query, cosines, sines)
+            fresh = turn(stack([nk_r[:, cols], blank]), cosine, sine)
+            key = stack([ck_r[:, cols], fresh])
+            scores = (
+                lax.dot_general(
+                    query, key, (((1,), (1,)), ((), ())),
+                    precision=lax.Precision.HIGHEST, preferred_element_type=jnp.float32,
+                )
+                * scale
+            )
+            scores = jnp.where(live, scores, MASKED)
+            top = jnp.max(scores, axis=-1, keepdims=True)
+            weights = jnp.exp(scores - top)
+            probs = (weights / jnp.sum(weights, axis=-1, keepdims=True)).astype(jnp.bfloat16)
+            value = stack([cv_r[:, cols], nv_r[:, cols], blank]).astype(jnp.bfloat16)
+            out = jnp.dot(probs, value, preferred_element_type=jnp.float32)
+            out = out.astype(jnp.bfloat16).astype(jnp.float32)
+            pieces += [out[h * steps : (h + 1) * steps] for h in range(group)]
+        mixed = res_ref[r].astype(jnp.float32) + stack(pieces, axis=1)
+        mixed_ref[r] = mixed
+        mean = jnp.mean(mixed * mixed, axis=-1, keepdims=True)
+        normed.append(mixed * lax.rsqrt(mean + EPS) * gain_ref[...].astype(jnp.float32))
+
+    whole = MAIN // steps
+    fold = width // 2
+    pay_ref[:, :width] = stack(normed[:whole]).astype(pay_ref.dtype)
+    late = normed[whole:]
+    pay_ref[:, width : width + fold] = stack(
+        [n[:, :fold] for n in late] + [n[:, fold:] for n in late]
+    ).astype(pay_ref.dtype)
+
+    place = lax.broadcasted_iota(jnp.int32, (steps, LANES), 1)
+    spread = []
+    for r in range(rows):
+        gains = gains_ref[r]
+        shares = gains / jnp.sum(gains, axis=-1, keepdims=True)
+        picks = routes_ref[r] + (0 if r < whole else LANES // 2)
+        dense = jnp.zeros((steps, LANES), jnp.float32)
+        for k in range(TOP):
+            dense = jnp.where(place == picks[:, k : k + 1], shares[:, k : k + 1], dense)
+        spread.append(dense)
+    early = stack(spread[:whole])
+    late = stack(spread[whole:] + [jnp.zeros((MAIN - (rows - whole) * steps, LANES), jnp.float32)])
+    pay_ref[:, width + fold :] = (early + late).astype(pay_ref.dtype)
+
+
+def front(queries, new_keys, new_values, cache_keys, cache_values, lengths, image_grid, residual,
+          norm_gain, routes, route_gains):
+    rows, steps, width = queries.shape
+    return pl.pallas_call(
+        front_kernel,
+        out_shape=(
+            jax.ShapeDtypeStruct((MAIN, width + width // 2 + LANES), jnp.bfloat16),
+            jax.ShapeDtypeStruct((rows, steps, width), jnp.float32),
+        ),
+        in_specs=[VMEM] * 5 + [SMEM] * 2 + [VMEM] * 4,
+        out_specs=(VMEM, VMEM),
+        cost_estimate=pl.CostEstimate(flops=10**7, bytes_accessed=10**6, transcendentals=10**4),
+    )(queries, new_keys, new_values, cache_keys, cache_values, lengths, image_grid, residual,
+      norm_gain.reshape(1, width), routes, route_gains)
+
+
+def experts_kernel(blocks, local, axis, *refs):
+    pays = refs[:blocks]
+    gate_ref, up_ref, down_ref, near_ref, far_ref, x_ref, share_ref, total_ref = refs[blocks:]
+    step = pl.program_id(0)
+    count, quarter, width = gate_ref.shape
+    fold = width // 2
+    rest = 4
+    tokens = blocks * (MAIN + rest)
+
+    @pl.when(step == 0)
+    def _():
+        for i in range(0, blocks, 2):
+            pair = [pays[i + j][...].astype(jnp.float32) for j in range(2)]
+            x_ref[i * MAIN : (i + 2) * MAIN] = stack([p[:, :width] for p in pair]).astype(x_ref.dtype)
+            share_ref[i * MAIN : (i + 2) * MAIN] = stack([p[:, width + fold :] for p in pair])
+        for i in range(0, blocks, 4):
+            start = blocks * MAIN + i * rest
+            four = [pays[i + j][...].astype(jnp.float32) for j in range(4)]
+            left = stack([p[:rest, width : width + fold] for p in four])
+            right = stack([p[rest:, width : width + fold] for p in four])
+            x_ref[start : start + 4 * rest, :fold] = left.astype(x_ref.dtype)
+            x_ref[start : start + 4 * rest, fold:] = right.astype(x_ref.dtype)
+            share_ref[start : start + 4 * rest] = stack([p[:rest, width + fold :] for p in four])
+        total_ref[...] = jnp.zeros_like(total_ref)
+
+    first = lax.axis_index(axis) * local + step * count
+    lane = lax.broadcasted_iota(jnp.int32, (tokens, LANES), 1)
+    row = lax.broadcasted_iota(jnp.int32, (tokens, LANES), 0)
+    offset = jnp.where(row < blocks * MAIN, 0, LANES // 2)
+    shares = share_ref[...]
+    flat = (((1,), (1,)), ((), ()))
+    gate = lax.dot_general(
+        x_ref[...], gate_ref[...].reshape(count * quarter, width), flat,
+        preferred_element_type=jnp.float32,
+    )
+    upper = lax.dot_general(
+        x_ref[...], up_ref[...].reshape(count * quarter, width), flat,
+        preferred_element_type=jnp.float32,
+    )
+    hidden = jax.nn.silu(gate) * upper
+    unit = lax.broadcasted_iota(jnp.int32, hidden.shape, 1)
+    weight = jnp.zeros_like(hidden)
+    for e in range(count):
+        share = jnp.sum(jnp.where(lane == first + e + offset, shares, 0.0), axis=1, keepdims=True)
+        weight = jnp.where((unit >= e * quarter) & (unit < (e + 1) * quarter), share, weight)
+    hidden = (hidden * weight).astype(jnp.bfloat16)
+    total_ref[...] += jnp.dot(
+        hidden, down_ref[...].reshape(count * quarter, width), preferred_element_type=jnp.float32
+    )
+
+    @pl.when(step == pl.num_programs(0) - 1)
+    def _():
+        for b in range(blocks):
+            out = near_ref if b < blocks // 2 else far_ref
+            at = b % (blocks // 2)
+            out[at, :, :width] = total_ref[b * MAIN : (b + 1) * MAIN].astype(out.dtype)
+            start = blocks * MAIN + b * rest
+            late = total_ref[start : start + rest]
+            out[at, :, width:] = stack([late[:, :fold], late[:, fold:]]).astype(out.dtype)
+
+
+def experts(pays, w_gate, w_up, w_down, axis, count):
+    blocks = len(pays)
+    local, quarter, width = w_down.shape
+    tokens = blocks * 12
+    packed = width + width // 2
+    weights = pl.BlockSpec((count, quarter, width), lambda i: (i, 0, 0))
+    half = jax.ShapeDtypeStruct((blocks // 2, MAIN, packed), jnp.bfloat16)
+    return pl.pallas_call(
+        functools.partial(experts_kernel, blocks, local, axis),
+        grid=(local // count,),
+        out_shape=(half, half),
+        in_specs=[VMEM] * blocks + [weights] * 3,
+        out_specs=(VMEM, VMEM),
+        scratch_shapes=[
+            pltpu.VMEM((tokens, width), jnp.bfloat16),
+            pltpu.VMEM((tokens, LANES), jnp.float32),
+            pltpu.VMEM((tokens, width), jnp.float32),
+        ],
+        compiler_params=pltpu.CompilerParams(vmem_limit_bytes=60 * 2**20),
+        cost_estimate=pl.CostEstimate(
+            flops=6 * tokens * local * quarter * width,
+            bytes_accessed=6 * local * quarter * width,
+            transcendentals=tokens * local * quarter,
+        ),
+    )(*pays, jnp.swapaxes(w_gate, 1, 2), jnp.swapaxes(w_up, 1, 2), w_down)
+
+
+def final_kernel(mixed_ref, *refs):
+    parts, out_ref = refs[:-1], refs[-1]
+    rows, steps, width = mixed_ref.shape
+    fold = width // 2
+    total = parts[0][...].astype(jnp.float32)
+    for part in parts[1:]:
+        total = total + part[...].astype(jnp.float32)
+    for r in range(rows):
+        at = r * steps
+        if at < MAIN:
+            routed = total[at : at + steps, :width]
+        else:
+            at -= MAIN
+            low = total[at : at + steps, width:]
+            at += MAIN // 2
+            routed = stack([low, total[at : at + steps, width:]], axis=1)
+        out_ref[r] = (mixed_ref[r] + routed).astype(out_ref.dtype)
+
+
+def gathered(
+    queries, new_keys, new_values, cache_keys, cache_values, lengths, image_grid, residual,
+    norm_gain, routes, route_gains, w_gate, w_up, w_down,
+):
+    members = lax.axis_size("expert")
+    pay, mixed = front(
+        queries, new_keys, new_values, cache_keys, cache_values, lengths, image_grid, residual,
+        norm_gain, routes, route_gains,
+    )
+    twin = [(0, 1), (1, 0), (2, 3), (3, 2)]
+    side = [(0, 2), (2, 0), (1, 3), (3, 1)]
+    shifts = (2, 1, 3)
+    ahead = {k: [(i, (i + k) % members) for i in range(members)] for k in shifts}
+    back = {k: [(i, (i - k) % members) for i in range(members)] for k in shifts}
+    line = [pay] + [lax.ppermute(pay, "expert", ahead[k]) for k in shifts]
+    pays = line + [lax.ppermute(p, "dp", side) for p in line]
+    pays = pays + [lax.ppermute(p, "dp", twin) for p in pays]
+    near, far = experts(pays, w_gate, w_up, w_down, "expert", 4)
+    far = lax.ppermute(far, "dp", twin)
+    near = (near.astype(jnp.float32) + far.astype(jnp.float32)).astype(jnp.bfloat16)
+    peer = lax.ppermute(near[members:], "dp", side)
+    near = (near[:members].astype(jnp.float32) + peer.astype(jnp.float32)).astype(jnp.bfloat16)
+    parts = [near[0]] + [
+        lax.ppermute(near[i + 1], "expert", back[k]) for i, k in enumerate(shifts)
+    ]
+    return pl.pallas_call(
+        final_kernel,
+        out_shape=jax.ShapeDtypeStruct(residual.shape, jnp.bfloat16),
+        in_specs=[VMEM] * (1 + members),
+        out_specs=VMEM,
+    )(mixed, *parts)
+
+
 def solution(mesh):
     placed = (
         P(("replica", "expert", "dp"), None, None),
@@ -167,8 +430,9 @@
         P("expert", None, "dp"),
         P("expert", "dp", None),
     )
+    near = mesh.shape["expert"] == 4 and mesh.shape["dp"] == 4
     return jax.shard_map(
-        shards,
+        gathered if near else shards,
         mesh=mesh,
         in_specs=placed,
         out_specs=P(("replica", "expert", "dp"), None, None),

time: 214 us -> 96.7 us (0.45)
  waiting for transfers between devices: 104 us -> 33.5 us
  Pallas kernels: 0 us -> 42.4 us
  matrix products: 39.1 us -> 0 us
  blocking collectives: 31.8 us -> 0 us
  between operations: 13.6 us -> 0.22 us
  starting transfers between devices: 4.64 us -> 14.4 us
  local copies, waits for them, and re-layouts: 13.8 us -> 4.55 us
  other arithmetic: 6.38 us -> 1.41 us
    unnamed x3 -> x0, waiting for transfers between devices: 44.7 us -> none
    pallas_call x0 -> x3, Pallas kernels: none -> 42.4 us  [the longest x1 33.9 us: experts(): pl.pallas_call(functools.partial(experts_kernel, blocks, local, axis), gr...]
    dot_general x7 -> x0, matrix products: 39.1 us -> none  [the longest x1 22 us: shards(): jnp.einsum('reh,ehd->red', piece, w_down, preferred_element_type=jnp.floa...]
    all_gather x1 -> x0, waiting for transfers between devices: 33.7 us -> none  [shards(): piece = lax.all_gather(flat, 'dp', axis=0, tiled=True)]
    ppermute x0 -> x20, waiting for transfers between devices: none -> 33.5 us  [the longest x1 10.6 us: gathered(): peer = lax.ppermute(near[members:], 'dp', side)]
    all_to_all x1 -> x0, blocking collectives: 31.8 us -> none  [shards(): lax.all_to_all(outgoing, 'expert', split_axis=0, concat_axis=0, tiled=True)]
    all_to_all x1 -> x0, waiting for transfers between devices: 25.6 us -> none  [shards(): lax.all_to_all(result.reshape(incoming.shape), 'expert', split_axis=0, co...]
    ppermute x0 -> x20, starting transfers between devices: none -> 14.4 us  [the longest x3 4.61 us: gathered(): line = [pay] + [lax.ppermute(pay, 'expert', ahead[k]) for k in shifts]]
  transfers between devices with their start and end apart: 3 -> 20, of which waited for: 3 -> 10; matrix products, arithmetic and copies ran while one was open for 0% -> 0% of each run, Pallas kernels for 0% -> 0%
where the time goes in v1:
time: 96.7 us; the launch traced here: 96.4 us
  Pallas kernels  42.4 us (44%)
  waiting for transfers between devices  33.5 us (35%)
  starting transfers between devices  14.4 us (15%)
  local copies, waits for them, and re-layouts  4.55 us (5%)
  other arithmetic  1.41 us (1%)
    pallas_call x1, Pallas kernels, experts(): pl.pallas_call(functools.partial(experts_kernel, blocks, local, axis), gr...  33.9 us
    ppermute x1, waiting for transfers between devices, gathered(): peer = lax.ppermute(near[members:], 'dp', side)  10.6 us
    ppermute x3, waiting for transfers between devices, gathered(): line = [pay] + [lax.ppermute(pay, 'expert', ahead[k]) for k in shifts]  8.49 us
    ppermute x3, waiting for transfers between devices, gathered(): lax.ppermute(near[i + 1], 'expert', back[k])  7.26 us
    pallas_call x1, Pallas kernels, front(): pl.pallas_call(front_kernel, out_shape=(jax.ShapeDtypeStruct((MAIN, width...  6.59 us
    ppermute x3, starting transfers between devices, gathered(): line = [pay] + [lax.ppermute(pay, 'expert', ahead[k]) for k in shifts]  4.61 us
    ppermute x4, starting transfers between devices, gathered(): pays = line + [lax.ppermute(p, 'dp', side) for p in line]  4.61 us
    ppermute x3, starting transfers between devices, gathered(): lax.ppermute(near[i + 1], 'expert', back[k])  3.83 us
  transfers between devices with their start and end apart: 20, of which 10 were waited for; matrix products, arithmetic and copies ran while one was open for 0% of the time, Pallas kernels for 0%

profile of v1, /device:TPU:0, one launch (start us, length us, event | category | flops | bytes accessed | tf_op | source)
XLA Modules:
  0.0 96.4 jit_solution(6137719930212519751)
XLA Ops:
  0.0 1.4 %copy.15.grid_ref = s32[6,2]{1,0:T(8,128)} copy(s32[6,2]{0,1:T(2,128)} %param.20) | data formatting | bytes 96 | tf_op args[6]
  1.4 1.3 %reshape.3.gain_ref = bf16[1,4096]{1,0:T(2,128)(2,1)} reshape(bf16[4096]{0:T(1024)(128)(2,1)} %param.22) | data formatting | bytes 16384 | tf_op jit(solution)/shard_map/reshape | solution.py:273
  2.7 6.6 %shard_map.136 = (bf16[8,6272]{1,0:T(8,128)(2,1)}, f32[6,2,4096]{2,1,0:T(2,128)}) custom-call(bf16[6,2,4096]{2,1,0:T(2,128)(2,1)} %q_ref.1, bf16[6,2,256]{2,1,0:T(2,128)(2,1)} %nk_ref.1, bf16[6,2,256]{2,1,0:T(2,128)(2,1)} %nv_ref.1, bf16[6,32,256]{2,1,0:T(8,128)(2,1)} %ck_ref.1, bf16[6,32,256]{2,1,0:T(8,128)(2,1)} %cv_ref.1, s32[6]{0:T(128)} %len_ref.1, ...), custom_call_target="tpu_custom_call" | custom-call | flops 10000000 | bytes 1000000 | tf_op jit(solution)/shard_map/pallas_call | solution.py:263
  9.3 2.9 %collective-permute-start.3 = (bf16[8,6272]{1,0:T(8,128)(2,1)}, bf16[8,6272]{1,0:T(8,128)(2,1)S(1)}, u32[]{:S(2)}, u32[]{:S(2)}) collective-permute-start(bf16[8,6272]{1,0:T(8,128)(2,1)} %get-tuple-element.10.refs_0_), channel_id=1, source_target_pairs={{0,2},{2,0},{1,3},{3,1},{4,6},{6,4},{5,7},{7,5},{8,10},{10,8},{9,1... | collective-permute-start | bytes 301064 | tf_op jit(solution)/shard_map/ppermute | solution.py:398
  12.2 3.6 %collective-permute-start.2 = (bf16[8,6272]{1,0:T(8,128)(2,1)}, bf16[8,6272]{1,0:T(8,128)(2,1)S(1)}, u32[]{:S(2)}, u32[]{:S(2)}) collective-permute-start(bf16[8,6272]{1,0:T(8,128)(2,1)} %get-tuple-element.10.refs_0_), channel_id=1, source_target_pairs={{0,12},{4,0},{8,4},{12,8},{1,13},{5,1},{9,5},{13,9},{2,14},{6,2},{... | collective-permute-start | bytes 301064 | tf_op jit(solution)/shard_map/ppermute | solution.py:397
  15.8 0.0 collective-permute-start.7
  15.8 1.0 %collective-permute-start = (bf16[8,6272]{1,0:T(8,128)(2,1)}, bf16[8,6272]{1,0:T(8,128)(2,1)S(1)}, u32[]{:S(2)}, u32[]{:S(2)}) collective-permute-start(bf16[8,6272]{1,0:T(8,128)(2,1)} %get-tuple-element.10.refs_0_), channel_id=1, source_target_pairs={{0,8},{4,12},{8,0},{12,4},{1,9},{5,13},{9,1},{13,5},{2,10},{6,14},... | collective-permute-start | bytes 301064 | tf_op jit(solution)/shard_map/ppermute | solution.py:397
  16.8 2.5 %collective-permute-done.2.refs_3_ = bf16[8,6272]{1,0:T(8,128)(2,1)S(1)} collective-permute-done((bf16[8,6272]{1,0:T(8,128)(2,1)}, bf16[8,6272]{1,0:T(8,128)(2,1)S(1)}, u32[]{:S(2)}, u32[]{:S(2)}) %collective-permute-start.2) | collective-permute-done | bytes 100384 | tf_op jit(solution)/shard_map/ppermute | solution.py:397
  19.4 0.6 collective-permute-start.6
  20.0 3.6 %collective-permute-done.1.refs_2_ = bf16[8,6272]{1,0:T(8,128)(2,1)S(1)} collective-permute-done((bf16[8,6272]{1,0:T(8,128)(2,1)}, bf16[8,6272]{1,0:T(8,128)(2,1)S(1)}, u32[]{:S(2)}, u32[]{:S(2)}) %collective-permute-start.1) | collective-permute-done | bytes 100384 | tf_op jit(solution)/shard_map/ppermute | solution.py:397
  23.5 0.5 collective-permute-start.5
  24.1 2.4 %collective-permute-done.refs_1_ = bf16[8,6272]{1,0:T(8,128)(2,1)S(1)} collective-permute-done((bf16[8,6272]{1,0:T(8,128)(2,1)}, bf16[8,6272]{1,0:T(8,128)(2,1)S(1)}, u32[]{:S(2)}, u32[]{:S(2)}) %collective-permute-start) | collective-permute-done | bytes 100384 | tf_op jit(solution)/shard_map/ppermute | solution.py:397
  26.5 0.5 collective-permute-start.4
  27.0 0.5 collective-permute-start.8
  27.5 0.1 collective-permute-start.14
  27.6 0.6 collective-permute-done.5.refs_6_
  28.2 2.9 %collective-permute-done.4.refs_5_ = bf16[8,6272]{1,0:T(8,128)(2,1)S(1)} collective-permute-done((bf16[8,6272]{1,0:T(8,128)(2,1)S(1)}, bf16[8,6272]{1,0:T(8,128)(2,1)S(1)}, u32[]{:S(2)}, u32[]{:S(2)}) %collective-permute-start.4) | collective-permute-done | bytes 100384 | tf_op jit(solution)/shard_map/ppermute | solution.py:398
  31.2 1.2 %collective-permute-done.12.refs_13_ = bf16[8,6272]{1,0:T(8,128)(2,1)S(1)} collective-permute-done((bf16[8,6272]{1,0:T(8,128)(2,1)S(1)}, bf16[8,6272]{1,0:T(8,128)(2,1)S(1)}, u32[]{:S(2)}, u32[]{:S(2)}) %collective-permute-start.12) | collective-permute-done | bytes 100384 | tf_op jit(solution)/shard_map/ppermute | solution.py:399
  32.5 0.5 copy-done.14
  33.0 33.9 %shard_map.137 = (bf16[8,8,6144]{2,1,0:T(8,128)(2,1)}, bf16[8,8,6144]{2,1,0:T(8,128)(2,1)}) custom-call(bf16[8,6272]{1,0:T(8,128)(2,1)} %get-tuple-element.10.refs_0_, bf16[8,6272]{1,0:T(8,128)(2,1)} %copy-done.4, bf16[8,6272]{1,0:T(8,128)(2,1)} %copy-done.3, bf16[8,6272]{1,0:T(8,128)(2,1)} %copy-done.1, bf16[8,6272]{1,0:T(8,128)(2,1)} %copy-done, ...), custom_call_target="tpu_custom_call" | custom-call | flops 14495514624 | bytes 75497472 | tf_op jit(solution)/shard_map/pallas_call | solution.py:344
  66.9 0.2 collective-permute-start.15
  67.1 2.3 %collective-permute-done.15 = bf16[8,8,6144]{2,1,0:T(8,128)(2,1)S(1)} collective-permute-done((bf16[8,8,6144]{2,1,0:T(8,128)(2,1)}, bf16[8,8,6144]{2,1,0:T(8,128)(2,1)S(1)}, u32[]{:S(2)}, u32[]{:S(2)}) %collective-permute-start.15) | collective-permute-done | bytes 786464 | tf_op jit(solution)/shard_map/ppermute | solution.py:401
  69.4 1.3 %add_convert_fusion = bf16[8,8,6144]{2,1,0:T(8,128)(2,1)S(1)} fusion(bf16[8,8,6144]{2,1,0:T(8,128)(2,1)S(1)} %collective-permute-done.15, bf16[8,8,6144]{2,1,0:T(8,128)(2,1)} %get-tuple-element.11), kind=kLoop, calls=%fused_computation | loop fusion | flops 1572864 | bytes 2359296 | tf_op jit(solution)/shard_map/convert_element_type | solution.py:402
  70.7 0.6 collective-permute-start.16
  71.4 10.6 %collective-permute-done.16 = bf16[4,8,6144]{2,1,0:T(8,128)(2,1)S(1)} collective-permute-done((bf16[4,8,6144]{2,1,0:T(8,128)(2,1)S(1)}, bf16[4,8,6144]{2,1,0:T(8,128)(2,1)S(1)}, u32[]{:S(2)}, u32[]{:S(2)}) %collective-permute-start.16) | collective-permute-done | bytes 393248 | tf_op jit(solution)/shard_map/ppermute | solution.py:403
  82.0 0.1 add_convert_fusion.1
  82.1 0.7 slice_bitcast_fusion
  82.8 3.8 %collective-permute-start.18 = (bf16[8,6144]{1,0:T(8,128)(2,1)S(1)}, bf16[8,6144]{1,0:T(8,128)(2,1)S(1)}, u32[]{:S(2)}, u32[]{:S(2)}) collective-permute-start(bf16[8,6144]{1,0:T(8,128)(2,1)S(1)} %get-tuple-element.14), channel_id=1, source_target_pairs={{0,12},{4,0},{8,4},{12,8},{1,13},{5,1},{9,5},{13,9},{2,14},{6,2},{... | collective-permute-start | bytes 294920 | tf_op jit(solution)/shard_map/ppermute | solution.py:406
  86.6 3.8 %collective-permute-done.19.refs_3_ = bf16[8,6144]{1,0:T(8,128)(2,1)S(1)} collective-permute-done((bf16[8,6144]{1,0:T(8,128)(2,1)S(1)}, bf16[8,6144]{1,0:T(8,128)(2,1)S(1)}, u32[]{:S(2)}, u32[]{:S(2)}) %collective-permute-start.19) | collective-permute-done | bytes 98336 | tf_op jit(solution)/shard_map/ppermute | solution.py:406
  90.4 3.5 %collective-permute-done.17.refs_1_ = bf16[8,6144]{1,0:T(8,128)(2,1)S(1)} collective-permute-done((bf16[8,6144]{1,0:T(8,128)(2,1)S(1)}, bf16[8,6144]{1,0:T(8,128)(2,1)S(1)}, u32[]{:S(2)}, u32[]{:S(2)}) %collective-permute-start.17) | collective-permute-done | bytes 98336 | tf_op jit(solution)/shard_map/ppermute | solution.py:406
  93.8 0.6 copy-done.17
  94.5 1.9 %shard_map.138 = bf16[6,2,4096]{2,1,0:T(2,128)(2,1)} custom-call(f32[6,2,4096]{2,1,0:T(2,128)} %get-tuple-element.9.mixed_ref, bf16[8,6144]{1,0:T(8,128)(2,1)} %get-tuple-element.16.refs_0_, bf16[8,6144]{1,0:T(8,128)(2,1)} %copy-done.17, bf16[8,6144]{1,0:T(8,128)(2,1)} %copy-done.16, bf16[8,6144]{1,0:T(8,128)(2,1)} %copy-done.15), custom_call_target="tpu_custom_call" | custom-call | tf_op jit(solution)/shard_map/pallas_call | solution.py:408
  (53 shorter events, 0.1 us)
Async XLA Ops:
  9.3 7.6 %collective-permute-start.3 = (bf16[8,6272]{1,0:T(8,128)(2,1)}, bf16[8,6272]{1,0:T(8,128)(2,1)S(1)}, u32[]{:S(2)}, u32[]{:S(2)}) collective-permute-start(bf16[8,6272]{1,0:T(8,128)(2,1)} %get-tuple-element.10.refs_0_), channel_id=1, source_target_pairs={{0,2},{2,0},{1,3},{3,1},{4,6},{6,4},{5,7},{7,5},{8,10},{10,8},{9,1... | collective-permute-start | bytes 301064 | tf_op jit(solution)/shard_map/ppermute | solution.py:398
  12.2 7.1 %collective-permute-start.2 = (bf16[8,6272]{1,0:T(8,128)(2,1)}, bf16[8,6272]{1,0:T(8,128)(2,1)S(1)}, u32[]{:S(2)}, u32[]{:S(2)}) collective-permute-start(bf16[8,6272]{1,0:T(8,128)(2,1)} %get-tuple-element.10.refs_0_), channel_id=1, source_target_pairs={{0,12},{4,0},{8,4},{12,8},{1,13},{5,1},{9,5},{13,9},{2,14},{6,2},{... | collective-permute-start | bytes 301064 | tf_op jit(solution)/shard_map/ppermute | solution.py:397
  15.8 3.6 %collective-permute-start.7 = (bf16[8,6272]{1,0:T(8,128)(2,1)}, bf16[8,6272]{1,0:T(8,128)(2,1)S(1)}, u32[]{:S(2)}, u32[]{:S(2)}) collective-permute-start(bf16[8,6272]{1,0:T(8,128)(2,1)} %get-tuple-element.10.refs_0_), channel_id=1, source_target_pairs={{0,1},{1,0},{2,3},{3,2},{4,5},{5,4},{6,7},{7,6},{8,9},{9,8},{10,11... | collective-permute-start | bytes 301064 | tf_op jit(solution)/shard_map/ppermute | solution.py:399
  15.8 7.7 %collective-permute-start.1 = (bf16[8,6272]{1,0:T(8,128)(2,1)}, bf16[8,6272]{1,0:T(8,128)(2,1)S(1)}, u32[]{:S(2)}, u32[]{:S(2)}) collective-permute-start(bf16[8,6272]{1,0:T(8,128)(2,1)} %get-tuple-element.10.refs_0_), channel_id=1, source_target_pairs={{0,4},{4,8},{8,12},{12,0},{1,5},{5,9},{9,13},{13,1},{2,6},{6,10},{... | collective-permute-start | bytes 301064 | tf_op jit(solution)/shard_map/ppermute | solution.py:397
  15.8 10.7 %collective-permute-start = (bf16[8,6272]{1,0:T(8,128)(2,1)}, bf16[8,6272]{1,0:T(8,128)(2,1)S(1)}, u32[]{:S(2)}, u32[]{:S(2)}) collective-permute-start(bf16[8,6272]{1,0:T(8,128)(2,1)} %get-tuple-element.10.refs_0_), channel_id=1, source_target_pairs={{0,8},{4,12},{8,0},{12,4},{1,9},{5,13},{9,1},{13,5},{2,10},{6,14},... | collective-permute-start | bytes 301064 | tf_op jit(solution)/shard_map/ppermute | solution.py:397
  16.8 15.6 %copy-start = (bf16[8,6272]{1,0:T(8,128)(2,1)}, bf16[8,6272]{1,0:T(8,128)(2,1)S(1)}, u32[]{:S(2)}) copy-start(bf16[8,6272]{1,0:T(8,128)(2,1)S(1)} %collective-permute-done.3.refs_4_) | copy-start | bytes 301060
  16.8 10.2 %collective-permute-start.11 = (bf16[8,6272]{1,0:T(8,128)(2,1)S(1)}, bf16[8,6272]{1,0:T(8,128)(2,1)S(1)}, u32[]{:S(2)}, u32[]{:S(2)}) collective-permute-start(bf16[8,6272]{1,0:T(8,128)(2,1)S(1)} %collective-permute-done.3.refs_4_), channel_id=1, source_target_pairs={{0,1},{1,0},{2,3},{3,2},{4,5},{5,4},{6,7},{7,6},{8,9},{9,8},{10,11... | collective-permute-start | bytes 301064 | tf_op jit(solution)/shard_map/ppermute | solution.py:399
  19.3 13.1 %copy-start.1 = (bf16[8,6272]{1,0:T(8,128)(2,1)}, bf16[8,6272]{1,0:T(8,128)(2,1)S(1)}, u32[]{:S(2)}) copy-start(bf16[8,6272]{1,0:T(8,128)(2,1)S(1)} %collective-permute-done.2.refs_3_) | copy-start | bytes 301060
  19.3 7.7 %collective-permute-start.10 = (bf16[8,6272]{1,0:T(8,128)(2,1)S(1)}, bf16[8,6272]{1,0:T(8,128)(2,1)S(1)}, u32[]{:S(2)}, u32[]{:S(2)}) collective-permute-start(bf16[8,6272]{1,0:T(8,128)(2,1)S(1)} %collective-permute-done.2.refs_3_), channel_id=1, source_target_pairs={{0,1},{1,0},{2,3},{3,2},{4,5},{5,4},{6,7},{7,6},{8,9},{9,8},{10,11... | collective-permute-start | bytes 301064 | tf_op jit(solution)/shard_map/ppermute | solution.py:399
  19.3 13.1 %copy-start.2 = (bf16[8,6272]{1,0:T(8,128)(2,1)}, bf16[8,6272]{1,0:T(8,128)(2,1)S(1)}, u32[]{:S(2)}) copy-start(bf16[8,6272]{1,0:T(8,128)(2,1)S(1)} %collective-permute-done.7.refs_8_) | copy-start | bytes 301060
  19.4 8.2 %collective-permute-start.6 = (bf16[8,6272]{1,0:T(8,128)(2,1)S(1)}, bf16[8,6272]{1,0:T(8,128)(2,1)S(1)}, u32[]{:S(2)}, u32[]{:S(2)}) collective-permute-start(bf16[8,6272]{1,0:T(8,128)(2,1)S(1)} %collective-permute-done.2.refs_3_), channel_id=1, source_target_pairs={{0,2},{2,0},{1,3},{3,1},{4,6},{6,4},{5,7},{7,5},{8,10},{10,8},{9,1... | collective-permute-start | bytes 301064 | tf_op jit(solution)/shard_map/ppermute | solution.py:398
  23.5 8.9 %copy-start.3 = (bf16[8,6272]{1,0:T(8,128)(2,1)}, bf16[8,6272]{1,0:T(8,128)(2,1)S(1)}, u32[]{:S(2)}) copy-start(bf16[8,6272]{1,0:T(8,128)(2,1)S(1)} %collective-permute-done.1.refs_2_) | copy-start | bytes 301060
  23.5 4.6 %collective-permute-start.5 = (bf16[8,6272]{1,0:T(8,128)(2,1)S(1)}, bf16[8,6272]{1,0:T(8,128)(2,1)S(1)}, u32[]{:S(2)}, u32[]{:S(2)}) collective-permute-start(bf16[8,6272]{1,0:T(8,128)(2,1)S(1)} %collective-permute-done.1.refs_2_), channel_id=1, source_target_pairs={{0,2},{2,0},{1,3},{3,1},{4,6},{6,4},{5,7},{7,5},{8,10},{10,8},{9,1... | collective-permute-start | bytes 301064 | tf_op jit(solution)/shard_map/ppermute | solution.py:398
  26.5 6.0 %copy-start.4 = (bf16[8,6272]{1,0:T(8,128)(2,1)}, bf16[8,6272]{1,0:T(8,128)(2,1)S(1)}, u32[]{:S(2)}) copy-start(bf16[8,6272]{1,0:T(8,128)(2,1)S(1)} %collective-permute-done.refs_1_) | copy-start | bytes 301060
  26.5 4.6 %collective-permute-start.4 = (bf16[8,6272]{1,0:T(8,128)(2,1)S(1)}, bf16[8,6272]{1,0:T(8,128)(2,1)S(1)}, u32[]{:S(2)}, u32[]{:S(2)}) collective-permute-start(bf16[8,6272]{1,0:T(8,128)(2,1)S(1)} %collective-permute-done.refs_1_), channel_id=1, source_target_pairs={{0,2},{2,0},{1,3},{3,1},{4,6},{6,4},{5,7},{7,5},{8,10},{10,8},{9,1... | collective-permute-start | bytes 301064 | tf_op jit(solution)/shard_map/ppermute | solution.py:398
  27.0 5.4 %copy-start.5 = (bf16[8,6272]{1,0:T(8,128)(2,1)}, bf16[8,6272]{1,0:T(8,128)(2,1)S(1)}, u32[]{:S(2)}) copy-start(bf16[8,6272]{1,0:T(8,128)(2,1)S(1)} %collective-permute-done.11.refs_12_) | copy-start | bytes 301060
  27.0 4.1 %collective-permute-start.9 = (bf16[8,6272]{1,0:T(8,128)(2,1)S(1)}, bf16[8,6272]{1,0:T(8,128)(2,1)S(1)}, u32[]{:S(2)}, u32[]{:S(2)}) collective-permute-start(bf16[8,6272]{1,0:T(8,128)(2,1)S(1)} %collective-permute-done.1.refs_2_), channel_id=1, source_target_pairs={{0,1},{1,0},{2,3},{3,2},{4,5},{5,4},{6,7},{7,6},{8,9},{9,8},{10,11... | collective-permute-start | bytes 301064 | tf_op jit(solution)/shard_map/ppermute | solution.py:399
  27.0 5.4 %copy-start.6 = (bf16[8,6272]{1,0:T(8,128)(2,1)}, bf16[8,6272]{1,0:T(8,128)(2,1)S(1)}, u32[]{:S(2)}) copy-start(bf16[8,6272]{1,0:T(8,128)(2,1)S(1)} %collective-permute-done.10.refs_11_) | copy-start | bytes 301060
  27.0 4.1 %collective-permute-start.8 = (bf16[8,6272]{1,0:T(8,128)(2,1)S(1)}, bf16[8,6272]{1,0:T(8,128)(2,1)S(1)}, u32[]{:S(2)}, u32[]{:S(2)}) collective-permute-start(bf16[8,6272]{1,0:T(8,128)(2,1)S(1)} %collective-permute-done.refs_1_), channel_id=1, source_target_pairs={{0,1},{1,0},{2,3},{3,2},{4,5},{5,4},{6,7},{7,6},{8,9},{9,8},{10,11... | collective-permute-start | bytes 301064 | tf_op jit(solution)/shard_map/ppermute | solution.py:399
  27.5 4.9 %copy-start.7 = (bf16[8,6272]{1,0:T(8,128)(2,1)}, bf16[8,6272]{1,0:T(8,128)(2,1)S(1)}, u32[]{:S(2)}) copy-start(bf16[8,6272]{1,0:T(8,128)(2,1)S(1)} %collective-permute-done.6.refs_7_) | copy-start | bytes 301060
  27.5 3.6 %collective-permute-start.14 = (bf16[8,6272]{1,0:T(8,128)(2,1)S(1)}, bf16[8,6272]{1,0:T(8,128)(2,1)S(1)}, u32[]{:S(2)}, u32[]{:S(2)}) collective-permute-start(bf16[8,6272]{1,0:T(8,128)(2,1)S(1)} %collective-permute-done.6.refs_7_), channel_id=1, source_target_pairs={{0,1},{1,0},{2,3},{3,2},{4,5},{5,4},{6,7},{7,6},{8,9},{9,8},{10,11... | collective-permute-start | bytes 301064 | tf_op jit(solution)/shard_map/ppermute | solution.py:399
  28.2 4.3 %copy-start.8 = (bf16[8,6272]{1,0:T(8,128)(2,1)}, bf16[8,6272]{1,0:T(8,128)(2,1)S(1)}, u32[]{:S(2)}) copy-start(bf16[8,6272]{1,0:T(8,128)(2,1)S(1)} %collective-permute-done.5.refs_6_) | copy-start | bytes 301060
  28.2 3.0 %collective-permute-start.13 = (bf16[8,6272]{1,0:T(8,128)(2,1)S(1)}, bf16[8,6272]{1,0:T(8,128)(2,1)S(1)}, u32[]{:S(2)}, u32[]{:S(2)}) collective-permute-start(bf16[8,6272]{1,0:T(8,128)(2,1)S(1)} %collective-permute-done.5.refs_6_), channel_id=1, source_target_pairs={{0,1},{1,0},{2,3},{3,2},{4,5},{5,4},{6,7},{7,6},{8,9},{9,8},{10,11... | collective-permute-start | bytes 301064 | tf_op jit(solution)/shard_map/ppermute | solution.py:399
  31.1 1.4 %copy-start.9 = (bf16[8,6272]{1,0:T(8,128)(2,1)}, bf16[8,6272]{1,0:T(8,128)(2,1)S(1)}, u32[]{:S(2)}) copy-start(bf16[8,6272]{1,0:T(8,128)(2,1)S(1)} %collective-permute-done.4.refs_5_) | copy-start | bytes 301060
  31.1 1.3 %collective-permute-start.12 = (bf16[8,6272]{1,0:T(8,128)(2,1)S(1)}, bf16[8,6272]{1,0:T(8,128)(2,1)S(1)}, u32[]{:S(2)}, u32[]{:S(2)}) collective-permute-start(bf16[8,6272]{1,0:T(8,128)(2,1)S(1)} %collective-permute-done.4.refs_5_), channel_id=1, source_target_pairs={{0,1},{1,0},{2,3},{3,2},{4,5},{5,4},{6,7},{7,6},{8,9},{9,8},{10,11... | collective-permute-start | bytes 301064 | tf_op jit(solution)/shard_map/ppermute | solution.py:399
  66.9 2.5 %collective-permute-start.15 = (bf16[8,8,6144]{2,1,0:T(8,128)(2,1)}, bf16[8,8,6144]{2,1,0:T(8,128)(2,1)S(1)}, u32[]{:S(2)}, u32[]{:S(2)}) collective-permute-start(bf16[8,8,6144]{2,1,0:T(8,128)(2,1)} %get-tuple-element.12), channel_id=1, source_target_pairs={{0,1},{1,0},{2,3},{3,2},{4,5},{5,4},{6,7},{7,6},{8,9},{9,8},{10,11... | collective-permute-start | bytes 2359304 | tf_op jit(solution)/shard_map/ppermute | solution.py:401
  70.7 11.2 %collective-permute-start.16 = (bf16[4,8,6144]{2,1,0:T(8,128)(2,1)S(1)}, bf16[4,8,6144]{2,1,0:T(8,128)(2,1)S(1)}, u32[]{:S(2)}, u32[]{:S(2)}) collective-permute-start(bf16[4,8,6144]{2,1,0:T(8,128)(2,1)S(1)} %slice.25), channel_id=1, source_target_pairs={{0,2},{2,0},{1,3},{3,1},{4,6},{6,4},{5,7},{7,5},{8,10},{10,8},{9,1... | collective-permute-start | bytes 1179656 | tf_op jit(solution)/shard_map/ppermute | solution.py:403
  82.7 7.6 %collective-permute-start.19 = (bf16[8,6144]{1,0:T(8,128)(2,1)S(1)}, bf16[8,6144]{1,0:T(8,128)(2,1)S(1)}, u32[]{:S(2)}, u32[]{:S(2)}) collective-permute-start(bf16[8,6144]{1,0:T(8,128)(2,1)S(1)} %get-tuple-element.13), channel_id=1, source_target_pairs={{0,4},{4,8},{8,12},{12,0},{1,5},{5,9},{9,13},{13,1},{2,6},{6,10},{... | collective-permute-start | bytes 294920 | tf_op jit(solution)/shard_map/ppermute | solution.py:406
  82.8 7.6 %collective-permute-start.18 = (bf16[8,6144]{1,0:T(8,128)(2,1)S(1)}, bf16[8,6144]{1,0:T(8,128)(2,1)S(1)}, u32[]{:S(2)}, u32[]{:S(2)}) collective-permute-start(bf16[8,6144]{1,0:T(8,128)(2,1)S(1)} %get-tuple-element.14), channel_id=1, source_target_pairs={{0,12},{4,0},{8,4},{12,8},{1,13},{5,1},{9,5},{13,9},{2,14},{6,2},{... | collective-permute-start | bytes 294920 | tf_op jit(solution)/shard_map/ppermute | solution.py:406
  86.6 7.3 %collective-permute-start.17 = (bf16[8,6144]{1,0:T(8,128)(2,1)S(1)}, bf16[8,6144]{1,0:T(8,128)(2,1)S(1)}, u32[]{:S(2)}, u32[]{:S(2)}) collective-permute-start(bf16[8,6144]{1,0:T(8,128)(2,1)S(1)} %get-tuple-element.15), channel_id=1, source_target_pairs={{0,8},{4,12},{8,0},{12,4},{1,9},{5,13},{9,1},{13,5},{2,10},{6,14},... | collective-permute-start | bytes 294920 | tf_op jit(solution)/shard_map/ppermute | solution.py:406
  90.4 3.5 %copy-start.15 = (bf16[8,6144]{1,0:T(8,128)(2,1)}, bf16[8,6144]{1,0:T(8,128)(2,1)S(1)}, u32[]{:S(2)}) copy-start(bf16[8,6144]{1,0:T(8,128)(2,1)S(1)} %collective-permute-done.19.refs_3_) | copy-start | bytes 294916
  90.4 3.5 %copy-start.16 = (bf16[8,6144]{1,0:T(8,128)(2,1)}, bf16[8,6144]{1,0:T(8,128)(2,1)S(1)}, u32[]{:S(2)}) copy-start(bf16[8,6144]{1,0:T(8,128)(2,1)S(1)} %collective-permute-done.18.refs_2_) | copy-start | bytes 294916
  (6 other events, 6.7 us)

commit v2 on v1

--- a/solution.py
+++ b/solution.py
@@ -156,6 +156,7 @@
 VMEM = pl.BlockSpec(memory_space=pltpu.VMEM)
 SMEM = pl.BlockSpec(memory_space=pltpu.SMEM)
 LANES = 128
+VMEM_BYTES = 34 * 2**20
 MAIN = 8
 
 
@@ -187,10 +188,11 @@
     def turn(vectors, cosine, sine):
         return vectors * cosine + pltpu.roll(vectors, half, 1) * sine
 
+    gain = gain_ref[...].astype(jnp.float32).reshape(1, width)
     normed = []
     for r in range(rows):
         length = len_ref[r]
-        high, wide = grid_ref[r, 0], grid_ref[r, 1]
+        high, wide = grid_ref[0, r], grid_ref[1, r]
         base = length - high * wide + jnp.maximum(high, wide)
         angle = (base + sub % steps).astype(jnp.float32) * freq
         cosine = jnp.cos(angle)
@@ -232,7 +234,7 @@
         mixed = res_ref[r].astype(jnp.float32) + stack(pieces, axis=1)
         mixed_ref[r] = mixed
         mean = jnp.mean(mixed * mixed, axis=-1, keepdims=True)
-        normed.append(mixed * lax.rsqrt(mean + EPS) * gain_ref[...].astype(jnp.float32))
+        normed.append(mixed * lax.rsqrt(mean + EPS) * gain)
 
     whole = MAIN // steps
     fold = width // 2
@@ -269,96 +271,177 @@
         in_specs=[VMEM] * 5 + [SMEM] * 2 + [VMEM] * 4,
         out_specs=(VMEM, VMEM),
         cost_estimate=pl.CostEstimate(flops=10**7, bytes_accessed=10**6, transcendentals=10**4),
-    )(queries, new_keys, new_values, cache_keys, cache_values, lengths, image_grid, residual,
-      norm_gain.reshape(1, width), routes, route_gains)
-
-
-def experts_kernel(blocks, local, axis, *refs):
+    )(queries, new_keys, new_values, cache_keys, cache_values, lengths, image_grid.T, residual,
+      norm_gain, routes, route_gains)
+
+
+GROUP = 4
+CUT = 256
+
+
+def fetch_kernel(parts, *refs):
+    sources, (_, *outs, sem) = refs[:parts], refs[parts:]
+    copies = [
+        pltpu.make_async_copy(source.at[e], out.at[e], sem.at[p, e])
+        for p, (source, out) in enumerate(zip(sources, outs))
+        for e in range(out.shape[0])
+    ]
+    for copy in copies:
+        copy.start()
+    for copy in copies:
+        copy.wait()
+
+
+def fetch(weights, count, after):
+    size = weights[0].size * 2 // weights[0].shape[0] * count * len(weights)
+    place = pl.BlockSpec(memory_space=pl.ANY)
+    shape = (count, *weights[0].shape[1:])
+    return pl.pallas_call(
+        functools.partial(fetch_kernel, len(weights)),
+        out_shape=[pltpu.VMEM(shape, jnp.bfloat16)] * len(weights),
+        in_specs=[place] * (len(weights) + 1),
+        out_specs=[VMEM] * len(weights),
+        scratch_shapes=[pltpu.SemaphoreType.DMA((len(weights), count))],
+        compiler_params=pltpu.CompilerParams(vmem_limit_bytes=2**20),
+        cost_estimate=pl.CostEstimate(flops=0, bytes_accessed=size, transcendentals=0),
+    )(*[pltpu.with_memory_space_constraint(w, pltpu.HBM) for w in weights], after)
+
+
+def experts_kernel(blocks, axis, *refs):
     pays = refs[:blocks]
-    gate_ref, up_ref, down_ref, near_ref, far_ref, x_ref, share_ref, total_ref = refs[blocks:]
-    step = pl.program_id(0)
-    count, quarter, width = gate_ref.shape
+    (
+        early_gate, early_up, early_down, gate_hbm, up_hbm, down_hbm, near_ref, far_ref, held_ref,
+        x_ref, share_ref, hidden_ref, held_sem,
+    ) = refs[blocks:]
+    local, quarter, width = gate_hbm.shape
     fold = width // 2
     rest = 4
     tokens = blocks * (MAIN + rest)
-
-    @pl.when(step == 0)
-    def _():
-        for i in range(0, blocks, 2):
-            pair = [pays[i + j][...].astype(jnp.float32) for j in range(2)]
-            x_ref[i * MAIN : (i + 2) * MAIN] = stack([p[:, :width] for p in pair]).astype(x_ref.dtype)
-            share_ref[i * MAIN : (i + 2) * MAIN] = stack([p[:, width + fold :] for p in pair])
-        for i in range(0, blocks, 4):
-            start = blocks * MAIN + i * rest
-            four = [pays[i + j][...].astype(jnp.float32) for j in range(4)]
-            left = stack([p[:rest, width : width + fold] for p in four])
-            right = stack([p[rest:, width : width + fold] for p in four])
-            x_ref[start : start + 4 * rest, :fold] = left.astype(x_ref.dtype)
-            x_ref[start : start + 4 * rest, fold:] = right.astype(x_ref.dtype)
-            share_ref[start : start + 4 * rest] = stack([p[:rest, width + fold :] for p in four])
-        total_ref[...] = jnp.zeros_like(total_ref)
-
-    first = lax.axis_index(axis) * local + step * count
-    lane = lax.broadcasted_iota(jnp.int32, (tokens, LANES), 1)
-    row = lax.broadcasted_iota(jnp.int32, (tokens, LANES), 0)
-    offset = jnp.where(row < blocks * MAIN, 0, LANES // 2)
-    shares = share_ref[...]
-    flat = (((1,), (1,)), ((), ()))
-    gate = lax.dot_general(
-        x_ref[...], gate_ref[...].reshape(count * quarter, width), flat,
-        preferred_element_type=jnp.float32,
-    )
-    upper = lax.dot_general(
-        x_ref[...], up_ref[...].reshape(count * quarter, width), flat,
-        preferred_element_type=jnp.float32,
-    )
-    hidden = jax.nn.silu(gate) * upper
-    unit = lax.broadcasted_iota(jnp.int32, hidden.shape, 1)
-    weight = jnp.zeros_like(hidden)
-    for e in range(count):
-        share = jnp.sum(jnp.where(lane == first + e + offset, shares, 0.0), axis=1, keepdims=True)
-        weight = jnp.where((unit >= e * quarter) & (unit < (e + 1) * quarter), share, weight)
-    hidden = (hidden * weight).astype(jnp.bfloat16)
-    total_ref[...] += jnp.dot(
-        hidden, down_ref[...].reshape(count * quarter, width), preferred_element_type=jnp.float32
-    )
-
-    @pl.when(step == pl.num_programs(0) - 1)
-    def _():
+    tall = GROUP * quarter
+    groups = local // GROUP
+    half = local // 2
+
+    def load(g):
+        slot = g % 2
+        copies = []
+        for k in range(GROUP):
+            if g < groups:
+                e = g * GROUP + k
+                pair = gate_hbm.at[e], up_hbm.at[e]
+            else:
+                pair = down_hbm.at[half + k], down_hbm.at[half + GROUP + k]
+            for p in range(2):
+                copies.append(
+                    pltpu.make_async_copy(
+                        pair[p], held_ref.at[slot, p, k], held_sem.at[slot, p, k]
+                    )
+                )
+        return copies
+
+    for g in (1, 2):
+        for copy in load(g):
+            copy.start()
+
+    spread = []
+    for i in range(0, blocks, 2):
+        pair = [pays[i + j][...].astype(jnp.float32) for j in range(2)]
+        x_ref[i * MAIN : (i + 2) * MAIN] = stack([p[:, :width] for p in pair]).astype(x_ref.dtype)
+        spread += [p[:, width + fold :] for p in pair]
+    for i in range(0, blocks, 4):
+        start = blocks * MAIN + i * rest
+        four = [pays[i + j][...].astype(jnp.float32) for j in range(4)]
+        left = stack([p[:rest, width : width + fold] for p in four])
+        right = stack([p[rest:, width : width + fold] for p in four])
+        x_ref[start : start + 4 * rest, :fold] = left.astype(x_ref.dtype)
+        x_ref[start : start + 4 * rest, fold:] = right.astype(x_ref.dtype)
+        spread += [p[:rest, width + fold :] for p in four]
+    shares = stack(spread).T
+    column = lax.broadcasted_iota(jnp.int32, (LANES // 2, tokens), 1)
+    share_ref[...] = jnp.where(
+        column < blocks * MAIN, shares[: LANES // 2], shares[LANES // 2 :]
+    )
+    first = lax.axis_index(axis) * local
+
+    for g in range(groups):
+        if g == 0:
+            gate_w, up_w = early_gate[...], early_up[...]
+        else:
+            for copy in load(g):
+                copy.wait()
+            gate_w, up_w = held_ref[g % 2, 0], held_ref[g % 2, 1]
+        flat = (((1,), (1,)), ((), ()))
+        gate = lax.dot_general(
+            gate_w.reshape(tall, width), x_ref[...], flat, preferred_element_type=jnp.float32
+        )
+        upper = lax.dot_general(
+            up_w.reshape(tall, width), x_ref[...], flat, preferred_element_type=jnp.float32
+        )
+        hidden = jax.nn.silu(gate) * upper
+        weight = stack(
+            [
+                jnp.broadcast_to(share_ref[pl.ds(first + g * GROUP + k, 1)], (quarter, tokens))
+                for k in range(GROUP)
+            ]
+        )
+        hidden_ref[:, g * tall : (g + 1) * tall] = (hidden * weight).T.astype(hidden_ref.dtype)
+        if 1 <= g < groups - 1:
+            for copy in load(g + 2):
+                copy.start()
+
+    for copy in load(groups):
+        copy.wait()
+    deep = half * quarter
+    slot = groups % 2
+    for at in range(0, fold, CUT):
+        low, high = [
+            jnp.dot(
+                hidden_ref[:, :deep], early_down[:, :, c : c + CUT].reshape(deep, CUT),
+                preferred_element_type=jnp.float32,
+            )
+            + jnp.dot(
+                hidden_ref[:, deep:], held_ref[slot, :, :, :, c : c + CUT].reshape(deep, CUT),
+                preferred_element_type=jnp.float32,
+            )
+            for c in (at, fold + at)
+        ]
         for b in range(blocks):
             out = near_ref if b < blocks // 2 else far_ref
-            at = b % (blocks // 2)
-            out[at, :, :width] = total_ref[b * MAIN : (b + 1) * MAIN].astype(out.dtype)
+            to = b % (blocks // 2)
+            main = slice(b * MAIN, (b + 1) * MAIN)
+            out[to, :, at : at + CUT] = low[main].astype(out.dtype)
+            out[to, :, fold + at : fold + at + CUT] = high[main].astype(out.dtype)
             start = blocks * MAIN + b * rest
-            late = total_ref[start : start + rest]
-            out[at, :, width:] = stack([late[:, :fold], late[:, fold:]]).astype(out.dtype)
-
-
-def experts(pays, w_gate, w_up, w_down, axis, count):
+            late = stack([low[start : start + rest], high[start : start + rest]])
+            out[to, :, width + at : width + at + CUT] = late.astype(out.dtype)
+
+
+def experts(pays, early, w_gate, w_up, w_down, axis):
     blocks = len(pays)
     local, quarter, width = w_down.shape
     tokens = blocks * 12
     packed = width + width // 2
-    weights = pl.BlockSpec((count, quarter, width), lambda i: (i, 0, 0))
     half = jax.ShapeDtypeStruct((blocks // 2, MAIN, packed), jnp.bfloat16)
+    place = pl.BlockSpec(memory_space=pl.ANY)
+    held = [pltpu.with_memory_space_constraint(a, pltpu.VMEM) for a in (*pays, *early)]
     return pl.pallas_call(
-        functools.partial(experts_kernel, blocks, local, axis),
-        grid=(local // count,),
+        functools.partial(experts_kernel, blocks, axis),
         out_shape=(half, half),
-        in_specs=[VMEM] * blocks + [weights] * 3,
+        in_specs=[VMEM] * len(held) + [place] * 3,
         out_specs=(VMEM, VMEM),
         scratch_shapes=[
+            pltpu.VMEM((2, 2, GROUP, quarter, width), jnp.bfloat16),
             pltpu.VMEM((tokens, width), jnp.bfloat16),
-            pltpu.VMEM((tokens, LANES), jnp.float32),
-            pltpu.VMEM((tokens, width), jnp.float32),
+            pltpu.VMEM((LANES // 2, tokens), jnp.float32),
+            pltpu.VMEM((tokens, local * quarter), jnp.bfloat16),
+            pltpu.SemaphoreType.DMA((2, 2, GROUP)),
         ],
-        compiler_params=pltpu.CompilerParams(vmem_limit_bytes=60 * 2**20),
+        compiler_params=pltpu.CompilerParams(vmem_limit_bytes=VMEM_BYTES),
         cost_estimate=pl.CostEstimate(
             flops=6 * tokens * local * quarter * width,
-            bytes_accessed=6 * local * quarter * width,
+            bytes_accessed=4 * local * quarter * width,
             transcendentals=tokens * local * quarter,
         ),
-    )(*pays, jnp.swapaxes(w_gate, 1, 2), jnp.swapaxes(w_up, 1, 2), w_down)
+    )(*held, *[pltpu.with_memory_space_constraint(w, pltpu.HBM) for w in (w_gate, w_up, w_down)])
 
 
 def final_kernel(mixed_ref, *refs):
@@ -395,9 +478,14 @@
     ahead = {k: [(i, (i + k) % members) for i in range(members)] for k in shifts}
     back = {k: [(i, (i - k) % members) for i in range(members)] for k in shifts}
     line = [pay] + [lax.ppermute(pay, "expert", ahead[k]) for k in shifts]
+    gate, up = jnp.swapaxes(w_gate, 1, 2), jnp.swapaxes(w_up, 1, 2)
+    pair = fetch((gate, up), GROUP, pay)
+    line[1], *pair = lax.optimization_barrier((line[1], *pair))
     pays = line + [lax.ppermute(p, "dp", side) for p in line]
+    (down,) = fetch((w_down,), w_down.shape[0] // 2, line[-1])
+    pays[5], down = lax.optimization_barrier((pays[5], down))
     pays = pays + [lax.ppermute(p, "dp", twin) for p in pays]
-    near, far = experts(pays, w_gate, w_up, w_down, "expert", 4)
+    near, far = experts(pays, (*pair, down), gate, up, w_down, "expert")
     far = lax.ppermute(far, "dp", twin)
     near = (near.astype(jnp.float32) + far.astype(jnp.float32)).astype(jnp.bfloat16)
     peer = lax.ppermute(near[members:], "dp", side)

time: 96.7 us -> 90.2 us (0.933)
  waiting for transfers between devices: 33.5 us -> 25.3 us
  local copies, waits for them, and re-layouts: 4.55 us -> 2.27 us
  starting transfers between devices: 14.4 us -> 16.6 us
  Pallas kernels: 42.4 us -> 44.3 us
    ppermute x3, waiting for transfers between devices: 8.49 us -> 0.01 us  [gathered(): line = [pay] + [lax.ppermute(pay, 'expert', ahead[k]) for k in shifts]]
    pallas_call x1 -> x3, Pallas kernels: 33.9 us -> 35.7 us  [the longest x1 26.3 us: experts(): pl.pallas_call(functools.partial(experts_kernel, blocks, axis), out_shape...]
    ppermute x8, starting transfers between devices: 0.59 us -> 2.1 us  [gathered(): pays = pays + [lax.ppermute(p, 'dp', twin) for p in pays]]
    ppermute x3, starting transfers between devices: 4.61 us -> 6.06 us  [gathered(): line = [pay] + [lax.ppermute(pay, 'expert', ahead[k]) for k in shifts]]
    reshape x1 -> x0, local copies, waits for them, and re-layouts: 1.31 us -> none  [front(): norm_gain.reshape(1, width)]
    ppermute x3, waiting for transfers between devices: 7.26 us -> 8.41 us  [gathered(): lax.ppermute(near[i + 1], 'expert', back[k])]
    ppermute x4, waiting for transfers between devices: 3.49 us -> 2.48 us  [gathered(): pays = line + [lax.ppermute(p, 'dp', side) for p in line]]
    unnamed x37 -> x10, local copies, waits for them, and re-layouts: 2.55 us -> 1.57 us
  transfers between devices with their start and end apart: 20 -> 20, of which waited for: 10 -> 10; matrix products, arithmetic and copies ran while one was open for 0% -> 0% of each run, Pallas kernels for 0% -> 10%
where the time goes in v2:
time: 90.2 us; the launch traced here: 90 us
  Pallas kernels  44.3 us (49%)
  waiting for transfers between devices  25.3 us (28%)
  starting transfers between devices  16.6 us (18%)
  local copies, waits for them, and re-layouts  2.27 us (3%)
  other arithmetic  1.41 us (2%)
    pallas_call x1, Pallas kernels, experts(): pl.pallas_call(functools.partial(experts_kernel, blocks, axis), out_shape...  26.3 us
    ppermute x1, waiting for transfers between devices, gathered(): peer = lax.ppermute(near[members:], 'dp', side)  11.4 us
    pallas_call x2, Pallas kernels, fetch(): pl.pallas_call(functools.partial(fetch_kernel, len(weights)), out_shape=[...  9.42 us
    ppermute x3, waiting for transfers between devices, gathered(): lax.ppermute(near[i + 1], 'expert', back[k])  8.41 us
    pallas_call x1, Pallas kernels, front(): pl.pallas_call(front_kernel, out_shape=(jax.ShapeDtypeStruct((MAIN, width...  6.6 us
    ppermute x3, starting transfers between devices, gathered(): line = [pay] + [lax.ppermute(pay, 'expert', ahead[k]) for k in shifts]  6.06 us
    ppermute x4, starting transfers between devices, gathered(): pays = line + [lax.ppermute(p, 'dp', side) for p in line]  4.12 us
    ppermute x3, starting transfers between devices, gathered(): lax.ppermute(near[i + 1], 'expert', back[k])  3.83 us
  transfers between devices with their start and end apart: 20, of which 10 were waited for; matrix products, arithmetic and copies ran while one was open for 0% of the time, Pallas kernels for 10%

profile of v2, /device:TPU:0, one launch (start us, length us, event | category | flops | bytes accessed | tf_op | source)
XLA Modules:
  0.0 90.0 jit_solution(2362978775878315849)
XLA Ops:
  0.0 6.6 %shard_map.136 = (bf16[8,6272]{1,0:T(8,128)(2,1)}, f32[6,2,4096]{2,1,0:T(2,128)}) custom-call(bf16[6,2,4096]{2,1,0:T(2,128)(2,1)} %q_ref.1, bf16[6,2,256]{2,1,0:T(2,128)(2,1)} %nk_ref.1, bf16[6,2,256]{2,1,0:T(2,128)(2,1)} %nv_ref.1, bf16[6,32,256]{2,1,0:T(8,128)(2,1)} %ck_ref.1, bf16[6,32,256]{2,1,0:T(8,128)(2,1)} %cv_ref.1, s32[6]{0:T(128)} %len_ref.1, ...), custom_call_target="tpu_custom_call" | custom-call | flops 10000000 | bytes 1000000 | tf_op jit(solution)/shard_map/pallas_call | solution.py:265
  6.6 4.0 %collective-permute-start = (bf16[8,6272]{1,0:T(8,128)(2,1)}, bf16[8,6272]{1,0:T(8,128)(2,1)S(1)}, u32[]{:S(2)}, u32[]{:S(2)}) collective-permute-start(bf16[8,6272]{1,0:T(8,128)(2,1)} %get-tuple-element.17.refs_2_.refs_0_), channel_id=1, source_target_pairs={{0,8},{4,12},{8,0},{12,4},{1,9},{5,13},{9,1},{13,5},{2,10},{6,14},... | collective-permute-start | bytes 301064 | tf_op jit(solution)/shard_map/ppermute | solution.py:480
  10.6 1.5 %collective-permute-start.3 = (bf16[8,6272]{1,0:T(8,128)(2,1)}, bf16[8,6272]{1,0:T(8,128)(2,1)S(1)}, u32[]{:S(2)}, u32[]{:S(2)}) collective-permute-start(bf16[8,6272]{1,0:T(8,128)(2,1)} %get-tuple-element.17.refs_2_.refs_0_), channel_id=1, source_target_pairs={{0,2},{2,0},{1,3},{3,1},{4,6},{6,4},{5,7},{7,5},{8,10},{10,8},{9,1... | collective-permute-start | bytes 301064 | tf_op jit(solution)/shard_map/ppermute | solution.py:484
  12.1 1.3 %collective-permute-start.2 = (bf16[8,6272]{1,0:T(8,128)(2,1)}, bf16[8,6272]{1,0:T(8,128)(2,1)S(1)}, u32[]{:S(2)}, u32[]{:S(2)}) collective-permute-start(bf16[8,6272]{1,0:T(8,128)(2,1)} %get-tuple-element.17.refs_2_.refs_0_), channel_id=1, source_target_pairs={{0,12},{4,0},{8,4},{12,8},{1,13},{5,1},{9,5},{13,9},{2,14},{6,2},{... | collective-permute-start | bytes 301064 | tf_op jit(solution)/shard_map/ppermute | solution.py:480
  13.5 0.7 collective-permute-start.1
  14.2 0.9 %copy-done = bf16[8,6272]{1,0:T(8,128)(2,1)S(1)} copy-done((bf16[8,6272]{1,0:T(8,128)(2,1)S(1)}, bf16[8,6272]{1,0:T(8,128)(2,1)}, u32[]{:S(2)}) %copy-start) | copy-done | bytes 100376
  15.1 4.7 %shard_map.137 = (bf16[4,192,4096]{2,1,0:T(8,128)(2,1)S(1)}, bf16[4,192,4096]{2,1,0:T(8,128)(2,1)S(1)}) custom-call(bf16[16,192,4096]{2,1,0:T(8,128)(2,1)} %bitcast.11, bf16[16,192,4096]{2,1,0:T(8,128)(2,1)} %bitcast.13, bf16[8,6272]{1,0:T(8,128)(2,1)S(1)} %copy-done), custom_call_target="tpu_custom_call" | custom-call | bytes 12582912 | tf_op jit(solution)/shard_map/pallas_call | solution.py:299
  19.8 0.6 collective-permute-start.4
  20.4 0.5 collective-permute-start.11
  21.0 1.5 %collective-permute-start.6 = (bf16[8,6272]{1,0:T(8,128)(2,1)S(1)}, bf16[8,6272]{1,0:T(8,128)(2,1)S(1)}, u32[]{:S(2)}, u32[]{:S(2)}) collective-permute-start(bf16[8,6272]{1,0:T(8,128)(2,1)S(1)} %collective-permute-done.2.refs_1_.refs_3_), channel_id=1, source_target_pairs={{0,2},{2,0},{1,3},{3,1},{4,6},{6,4},{5,7},{7,5},{8,10},{10,8},{9,1... | collective-permute-start | bytes 301064 | tf_op jit(solution)/shard_map/ppermute | solution.py:484
  22.4 0.5 collective-permute-start.5
  23.0 2.5 %collective-permute-done.4.refs_5_ = bf16[8,6272]{1,0:T(8,128)(2,1)S(1)} collective-permute-done((bf16[8,6272]{1,0:T(8,128)(2,1)S(1)}, bf16[8,6272]{1,0:T(8,128)(2,1)S(1)}, u32[]{:S(2)}, u32[]{:S(2)}) %collective-permute-start.4) | collective-permute-done | bytes 100384 | tf_op jit(solution)/shard_map/ppermute | solution.py:484
  25.5 4.7 %shard_map.138.refs_18_ = bf16[8,192,4096]{2,1,0:T(8,128)(2,1)S(1)} custom-call(bf16[16,192,4096]{2,1,0:T(8,128)(2,1)} %refs_21_.1, bf16[8,6272]{1,0:T(8,128)(2,1)S(1)} %collective-permute-done.2.refs_1_.refs_3_), custom_call_target="tpu_custom_call" | custom-call | bytes 12582912 | tf_op jit(solution)/shard_map/pallas_call | solution.py:299
  30.2 0.6 collective-permute-start.8
  30.8 0.4 collective-permute-start.14
  31.4 0.4 collective-permute-start.12
  31.8 0.3 collective-permute-done.9.refs_10_
  32.1 0.2 collective-permute-done.14.refs_15_
  32.2 0.4 collective-permute-done.13.refs_14_
  32.6 0.2 collective-permute-done.12.refs_13_
  32.7 26.3 %shard_map.139 = (bf16[8,8,6144]{2,1,0:T(8,128)(2,1)}, bf16[8,8,6144]{2,1,0:T(8,128)(2,1)}) custom-call(bf16[8,6272]{1,0:T(8,128)(2,1)S(1)} %copy-done.1, bf16[8,6272]{1,0:T(8,128)(2,1)S(1)} %collective-permute-done.refs_1_, bf16[8,6272]{1,0:T(8,128)(2,1)S(1)} %collective-permute-done.1.refs_2_, bf16[8,6272]{1,0:T(8,128)(2,1)S(1)} %collective-permute-done.2.refs_1_.refs_3_, ...), custom_call_target="tpu_custom_call" | custom-call | flops 14495514624 | bytes 50331648 | tf_op jit(solution)/shard_map/pallas_call | solution.py:426
  59.1 0.4 collective-permute-start.15
  59.5 2.1 %collective-permute-done.15 = bf16[8,8,6144]{2,1,0:T(8,128)(2,1)S(1)} collective-permute-done((bf16[8,8,6144]{2,1,0:T(8,128)(2,1)}, bf16[8,8,6144]{2,1,0:T(8,128)(2,1)S(1)}, u32[]{:S(2)}, u32[]{:S(2)}) %collective-permute-start.15) | collective-permute-done | bytes 786464 | tf_op jit(solution)/shard_map/ppermute | solution.py:489
  61.6 1.3 %add_convert_fusion = bf16[8,8,6144]{2,1,0:T(8,128)(2,1)S(1)} fusion(bf16[8,8,6144]{2,1,0:T(8,128)(2,1)S(1)} %collective-permute-done.15, bf16[8,8,6144]{2,1,0:T(8,128)(2,1)} %get-tuple-element.25), kind=kLoop, calls=%fused_computation | loop fusion | flops 1572864 | bytes 2359296 | tf_op jit(solution)/shard_map/convert_element_type | solution.py:490
  63.1 11.4 %collective-permute-done.16 = bf16[4,8,6144]{2,1,0:T(8,128)(2,1)S(1)} collective-permute-done((bf16[4,8,6144]{2,1,0:T(8,128)(2,1)S(1)}, bf16[4,8,6144]{2,1,0:T(8,128)(2,1)S(1)}, u32[]{:S(2)}, u32[]{:S(2)}) %collective-permute-start.16) | collective-permute-done | bytes 393248 | tf_op jit(solution)/shard_map/ppermute | solution.py:491
  74.5 0.7 slice_bitcast_fusion
  75.2 1.6 %collective-permute-start.19 = (bf16[8,6144]{1,0:T(8,128)(2,1)S(1)}, bf16[8,6144]{1,0:T(8,128)(2,1)S(1)}, u32[]{:S(2)}, u32[]{:S(2)}) collective-permute-start(bf16[8,6144]{1,0:T(8,128)(2,1)S(1)} %get-tuple-element.27), channel_id=1, source_target_pairs={{0,4},{4,8},{8,12},{12,0},{1,5},{5,9},{9,13},{13,1},{2,6},{6,10},{... | collective-permute-start | bytes 294920 | tf_op jit(solution)/shard_map/ppermute | solution.py:494
  76.8 2.3 %collective-permute-start.18 = (bf16[8,6144]{1,0:T(8,128)(2,1)S(1)}, bf16[8,6144]{1,0:T(8,128)(2,1)S(1)}, u32[]{:S(2)}, u32[]{:S(2)}) collective-permute-start(bf16[8,6144]{1,0:T(8,128)(2,1)S(1)} %get-tuple-element.28), channel_id=1, source_target_pairs={{0,12},{4,0},{8,4},{12,8},{1,13},{5,1},{9,5},{13,9},{2,14},{6,2},{... | collective-permute-start | bytes 294920 | tf_op jit(solution)/shard_map/ppermute | solution.py:494
  79.0 3.7 %collective-permute-done.19.refs_3_ = bf16[8,6144]{1,0:T(8,128)(2,1)S(1)} collective-permute-done((bf16[8,6144]{1,0:T(8,128)(2,1)S(1)}, bf16[8,6144]{1,0:T(8,128)(2,1)S(1)}, u32[]{:S(2)}, u32[]{:S(2)}) %collective-permute-start.19) | collective-permute-done | bytes 98336 | tf_op jit(solution)/shard_map/ppermute | solution.py:494
  82.8 4.6 %collective-permute-done.17.refs_1_ = bf16[8,6144]{1,0:T(8,128)(2,1)S(1)} collective-permute-done((bf16[8,6144]{1,0:T(8,128)(2,1)S(1)}, bf16[8,6144]{1,0:T(8,128)(2,1)S(1)}, u32[]{:S(2)}, u32[]{:S(2)}) %collective-permute-start.17) | collective-permute-done | bytes 98336 | tf_op jit(solution)/shard_map/ppermute | solution.py:494
  87.4 0.6 copy-done.4
  88.1 1.9 %shard_map.140 = bf16[6,2,4096]{2,1,0:T(2,128)(2,1)} custom-call(f32[6,2,4096]{2,1,0:T(2,128)} %get-tuple-element.16.mixed_ref, bf16[8,6144]{1,0:T(8,128)(2,1)} %get-tuple-element.30.refs_0_, bf16[8,6144]{1,0:T(8,128)(2,1)} %copy-done.4, bf16[8,6144]{1,0:T(8,128)(2,1)} %copy-done.3, bf16[8,6144]{1,0:T(8,128)(2,1)} %copy-done.2), custom_call_target="tpu_custom_call" | custom-call | tf_op jit(solution)/shard_map/pallas_call | solution.py:496
  (27 shorter events, 0.5 us)
Async XLA Ops:
  6.6 13.2 %collective-permute-start = (bf16[8,6272]{1,0:T(8,128)(2,1)}, bf16[8,6272]{1,0:T(8,128)(2,1)S(1)}, u32[]{:S(2)}, u32[]{:S(2)}) collective-permute-start(bf16[8,6272]{1,0:T(8,128)(2,1)} %get-tuple-element.17.refs_2_.refs_0_), channel_id=1, source_target_pairs={{0,8},{4,12},{8,0},{12,4},{1,9},{5,13},{9,1},{13,5},{2,10},{6,14},... | collective-permute-start | bytes 301064 | tf_op jit(solution)/shard_map/ppermute | solution.py:480
  10.6 9.8 %collective-permute-start.3 = (bf16[8,6272]{1,0:T(8,128)(2,1)}, bf16[8,6272]{1,0:T(8,128)(2,1)S(1)}, u32[]{:S(2)}, u32[]{:S(2)}) collective-permute-start(bf16[8,6272]{1,0:T(8,128)(2,1)} %get-tuple-element.17.refs_2_.refs_0_), channel_id=1, source_target_pairs={{0,2},{2,0},{1,3},{3,1},{4,6},{6,4},{5,7},{7,5},{8,10},{10,8},{9,1... | collective-permute-start | bytes 301064 | tf_op jit(solution)/shard_map/ppermute | solution.py:484
  12.1 8.8 %collective-permute-start.2 = (bf16[8,6272]{1,0:T(8,128)(2,1)}, bf16[8,6272]{1,0:T(8,128)(2,1)S(1)}, u32[]{:S(2)}, u32[]{:S(2)}) collective-permute-start(bf16[8,6272]{1,0:T(8,128)(2,1)} %get-tuple-element.17.refs_2_.refs_0_), channel_id=1, source_target_pairs={{0,12},{4,0},{8,4},{12,8},{1,13},{5,1},{9,5},{13,9},{2,14},{6,2},{... | collective-permute-start | bytes 301064 | tf_op jit(solution)/shard_map/ppermute | solution.py:480
  13.5 9.0 %collective-permute-start.1 = (bf16[8,6272]{1,0:T(8,128)(2,1)}, bf16[8,6272]{1,0:T(8,128)(2,1)S(1)}, u32[]{:S(2)}, u32[]{:S(2)}) collective-permute-start(bf16[8,6272]{1,0:T(8,128)(2,1)} %get-tuple-element.17.refs_2_.refs_0_), channel_id=1, source_target_pairs={{0,4},{4,8},{8,12},{12,0},{1,5},{5,9},{9,13},{13,1},{2,6},{6,10},{... | collective-permute-start | bytes 301064 | tf_op jit(solution)/shard_map/ppermute | solution.py:480
  14.2 0.9 %copy-start = (bf16[8,6272]{1,0:T(8,128)(2,1)S(1)}, bf16[8,6272]{1,0:T(8,128)(2,1)}, u32[]{:S(2)}) copy-start(bf16[8,6272]{1,0:T(8,128)(2,1)} %get-tuple-element.17.refs_2_.refs_0_) | copy-start | bytes 301060
  15.1 5.3 %copy-start.1 = (bf16[8,6272]{1,0:T(8,128)(2,1)S(1)}, bf16[8,6272]{1,0:T(8,128)(2,1)}, u32[]{:S(2)}) copy-start(bf16[8,6272]{1,0:T(8,128)(2,1)} %get-tuple-element.17.refs_2_.refs_0_) | copy-start | bytes 301060
  19.8 5.6 %collective-permute-start.4 = (bf16[8,6272]{1,0:T(8,128)(2,1)S(1)}, bf16[8,6272]{1,0:T(8,128)(2,1)S(1)}, u32[]{:S(2)}, u32[]{:S(2)}) collective-permute-start(bf16[8,6272]{1,0:T(8,128)(2,1)S(1)} %collective-permute-done.refs_1_), channel_id=1, source_target_pairs={{0,2},{2,0},{1,3},{3,1},{4,6},{6,4},{5,7},{7,5},{8,10},{10,8},{9,1... | collective-permute-start | bytes 301064 | tf_op jit(solution)/shard_map/ppermute | solution.py:484
  20.4 9.7 %collective-permute-start.7 = (bf16[8,6272]{1,0:T(8,128)(2,1)S(1)}, bf16[8,6272]{1,0:T(8,128)(2,1)S(1)}, u32[]{:S(2)}, u32[]{:S(2)}) collective-permute-start(bf16[8,6272]{1,0:T(8,128)(2,1)S(1)} %copy-done.1), channel_id=1, source_target_pairs={{0,1},{1,0},{2,3},{3,2},{4,5},{5,4},{6,7},{7,6},{8,9},{9,8},{10,11... | collective-permute-start | bytes 301064 | tf_op jit(solution)/shard_map/ppermute | solution.py:487
  20.4 10.3 %collective-permute-start.11 = (bf16[8,6272]{1,0:T(8,128)(2,1)S(1)}, bf16[8,6272]{1,0:T(8,128)(2,1)S(1)}, u32[]{:S(2)}, u32[]{:S(2)}) collective-permute-start(bf16[8,6272]{1,0:T(8,128)(2,1)S(1)} %collective-permute-done.3.refs_4_), channel_id=1, source_target_pairs={{0,1},{1,0},{2,3},{3,2},{4,5},{5,4},{6,7},{7,6},{8,9},{9,8},{10,11... | collective-permute-start | bytes 301064 | tf_op jit(solution)/shard_map/ppermute | solution.py:487
  21.0 9.9 %collective-permute-start.6 = (bf16[8,6272]{1,0:T(8,128)(2,1)S(1)}, bf16[8,6272]{1,0:T(8,128)(2,1)S(1)}, u32[]{:S(2)}, u32[]{:S(2)}) collective-permute-start(bf16[8,6272]{1,0:T(8,128)(2,1)S(1)} %collective-permute-done.2.refs_1_.refs_3_), channel_id=1, source_target_pairs={{0,2},{2,0},{1,3},{3,1},{4,6},{6,4},{5,7},{7,5},{8,10},{10,8},{9,1... | collective-permute-start | bytes 301064 | tf_op jit(solution)/shard_map/ppermute | solution.py:484
  22.4 8.8 %collective-permute-start.5 = (bf16[8,6272]{1,0:T(8,128)(2,1)S(1)}, bf16[8,6272]{1,0:T(8,128)(2,1)S(1)}, u32[]{:S(2)}, u32[]{:S(2)}) collective-permute-start(bf16[8,6272]{1,0:T(8,128)(2,1)S(1)} %collective-permute-done.1.refs_2_), channel_id=1, source_target_pairs={{0,2},{2,0},{1,3},{3,1},{4,6},{6,4},{5,7},{7,5},{8,10},{10,8},{9,1... | collective-permute-start | bytes 301064 | tf_op jit(solution)/shard_map/ppermute | solution.py:484
  25.5 5.9 %collective-permute-start.10 = (bf16[8,6272]{1,0:T(8,128)(2,1)S(1)}, bf16[8,6272]{1,0:T(8,128)(2,1)S(1)}, u32[]{:S(2)}, u32[]{:S(2)}) collective-permute-start(bf16[8,6272]{1,0:T(8,128)(2,1)S(1)} %collective-permute-done.2.refs_1_.refs_3_), channel_id=1, source_target_pairs={{0,1},{1,0},{2,3},{3,2},{4,5},{5,4},{6,7},{7,6},{8,9},{9,8},{10,11... | collective-permute-start | bytes 301064 | tf_op jit(solution)/shard_map/ppermute | solution.py:487
  30.2 1.9 %collective-permute-start.8 = (bf16[8,6272]{1,0:T(8,128)(2,1)S(1)}, bf16[8,6272]{1,0:T(8,128)(2,1)S(1)}, u32[]{:S(2)}, u32[]{:S(2)}) collective-permute-start(bf16[8,6272]{1,0:T(8,128)(2,1)S(1)} %collective-permute-done.refs_1_), channel_id=1, source_target_pairs={{0,1},{1,0},{2,3},{3,2},{4,5},{5,4},{6,7},{7,6},{8,9},{9,8},{10,11... | collective-permute-start | bytes 301064 | tf_op jit(solution)/shard_map/ppermute | solution.py:487
  30.7 1.3 %collective-permute-start.9 = (bf16[8,6272]{1,0:T(8,128)(2,1)S(1)}, bf16[8,6272]{1,0:T(8,128)(2,1)S(1)}, u32[]{:S(2)}, u32[]{:S(2)}) collective-permute-start(bf16[8,6272]{1,0:T(8,128)(2,1)S(1)} %collective-permute-done.1.refs_2_), channel_id=1, source_target_pairs={{0,1},{1,0},{2,3},{3,2},{4,5},{5,4},{6,7},{7,6},{8,9},{9,8},{10,11... | collective-permute-start | bytes 301064 | tf_op jit(solution)/shard_map/ppermute | solution.py:487
  30.8 1.4 %collective-permute-start.14 = (bf16[8,6272]{1,0:T(8,128)(2,1)S(1)}, bf16[8,6272]{1,0:T(8,128)(2,1)S(1)}, u32[]{:S(2)}, u32[]{:S(2)}) collective-permute-start(bf16[8,6272]{1,0:T(8,128)(2,1)S(1)} %collective-permute-done.6.refs_7_), channel_id=1, source_target_pairs={{0,1},{1,0},{2,3},{3,2},{4,5},{5,4},{6,7},{7,6},{8,9},{9,8},{10,11... | collective-permute-start | bytes 301064 | tf_op jit(solution)/shard_map/ppermute | solution.py:487
  31.3 1.3 %collective-permute-start.13 = (bf16[8,6272]{1,0:T(8,128)(2,1)S(1)}, bf16[8,6272]{1,0:T(8,128)(2,1)S(1)}, u32[]{:S(2)}, u32[]{:S(2)}) collective-permute-start(bf16[8,6272]{1,0:T(8,128)(2,1)S(1)} %collective-permute-done.5.refs_6_), channel_id=1, source_target_pairs={{0,1},{1,0},{2,3},{3,2},{4,5},{5,4},{6,7},{7,6},{8,9},{9,8},{10,11... | collective-permute-start | bytes 301064 | tf_op jit(solution)/shard_map/ppermute | solution.py:487
  31.4 1.4 %collective-permute-start.12 = (bf16[8,6272]{1,0:T(8,128)(2,1)S(1)}, bf16[8,6272]{1,0:T(8,128)(2,1)S(1)}, u32[]{:S(2)}, u32[]{:S(2)}) collective-permute-start(bf16[8,6272]{1,0:T(8,128)(2,1)S(1)} %collective-permute-done.4.refs_5_), channel_id=1, source_target_pairs={{0,1},{1,0},{2,3},{3,2},{4,5},{5,4},{6,7},{7,6},{8,9},{9,8},{10,11... | collective-permute-start | bytes 301064 | tf_op jit(solution)/shard_map/ppermute | solution.py:487
  59.1 2.6 %collective-permute-start.15 = (bf16[8,8,6144]{2,1,0:T(8,128)(2,1)}, bf16[8,8,6144]{2,1,0:T(8,128)(2,1)S(1)}, u32[]{:S(2)}, u32[]{:S(2)}) collective-permute-start(bf16[8,8,6144]{2,1,0:T(8,128)(2,1)} %get-tuple-element.26), channel_id=1, source_target_pairs={{0,1},{1,0},{2,3},{3,2},{4,5},{5,4},{6,7},{7,6},{8,9},{9,8},{10,11... | collective-permute-start | bytes 2359304 | tf_op jit(solution)/shard_map/ppermute | solution.py:489
  63.0 11.4 %collective-permute-start.16 = (bf16[4,8,6144]{2,1,0:T(8,128)(2,1)S(1)}, bf16[4,8,6144]{2,1,0:T(8,128)(2,1)S(1)}, u32[]{:S(2)}, u32[]{:S(2)}) collective-permute-start(bf16[4,8,6144]{2,1,0:T(8,128)(2,1)S(1)} %slice.25), channel_id=1, source_target_pairs={{0,2},{2,0},{1,3},{3,1},{4,6},{6,4},{5,7},{7,5},{8,10},{10,8},{9,1... | collective-permute-start | bytes 1179656 | tf_op jit(solution)/shard_map/ppermute | solution.py:491
  75.2 7.6 %collective-permute-start.19 = (bf16[8,6144]{1,0:T(8,128)(2,1)S(1)}, bf16[8,6144]{1,0:T(8,128)(2,1)S(1)}, u32[]{:S(2)}, u32[]{:S(2)}) collective-permute-start(bf16[8,6144]{1,0:T(8,128)(2,1)S(1)} %get-tuple-element.27), channel_id=1, source_target_pairs={{0,4},{4,8},{8,12},{12,0},{1,5},{5,9},{9,13},{13,1},{2,6},{6,10},{... | collective-permute-start | bytes 294920 | tf_op jit(solution)/shard_map/ppermute | solution.py:494
  76.8 6.1 %collective-permute-start.18 = (bf16[8,6144]{1,0:T(8,128)(2,1)S(1)}, bf16[8,6144]{1,0:T(8,128)(2,1)S(1)}, u32[]{:S(2)}, u32[]{:S(2)}) collective-permute-start(bf16[8,6144]{1,0:T(8,128)(2,1)S(1)} %get-tuple-element.28), channel_id=1, source_target_pairs={{0,12},{4,0},{8,4},{12,8},{1,13},{5,1},{9,5},{13,9},{2,14},{6,2},{... | collective-permute-start | bytes 294920 | tf_op jit(solution)/shard_map/ppermute | solution.py:494
  79.0 8.4 %collective-permute-start.17 = (bf16[8,6144]{1,0:T(8,128)(2,1)S(1)}, bf16[8,6144]{1,0:T(8,128)(2,1)S(1)}, u32[]{:S(2)}, u32[]{:S(2)}) collective-permute-start(bf16[8,6144]{1,0:T(8,128)(2,1)S(1)} %get-tuple-element.29), channel_id=1, source_target_pairs={{0,8},{4,12},{8,0},{12,4},{1,9},{5,13},{9,1},{13,5},{2,10},{6,14},... | collective-permute-start | bytes 294920 | tf_op jit(solution)/shard_map/ppermute | solution.py:494
  82.8 4.7 %copy-start.2 = (bf16[8,6144]{1,0:T(8,128)(2,1)}, bf16[8,6144]{1,0:T(8,128)(2,1)S(1)}, u32[]{:S(2)}) copy-start(bf16[8,6144]{1,0:T(8,128)(2,1)S(1)} %collective-permute-done.19.refs_3_) | copy-start | bytes 294916
  82.8 4.6 %copy-start.3 = (bf16[8,6144]{1,0:T(8,128)(2,1)}, bf16[8,6144]{1,0:T(8,128)(2,1)S(1)}, u32[]{:S(2)}) copy-start(bf16[8,6144]{1,0:T(8,128)(2,1)S(1)} %collective-permute-done.18.refs_2_) | copy-start | bytes 294916
  87.4 0.6 copy-start.4

commit v3 on v2

--- a/solution.py
+++ b/solution.py
@@ -276,13 +276,13 @@
 
 
 GROUP = 4
-CUT = 256
-
-
-def fetch_kernel(parts, *refs):
+CUT = 512
+
+
+def fetch_kernel(parts, start, *refs):
     sources, (_, *outs, sem) = refs[:parts], refs[parts:]
     copies = [
-        pltpu.make_async_copy(source.at[e], out.at[e], sem.at[p, e])
+        pltpu.make_async_copy(source.at[start + e], out.at[e], sem.at[p, e])
         for p, (source, out) in enumerate(zip(sources, outs))
         for e in range(out.shape[0])
     ]
@@ -292,12 +292,12 @@
         copy.wait()
 
 
-def fetch(weights, count, after):
+def fetch(weights, start, count, after):
     size = weights[0].size * 2 // weights[0].shape[0] * count * len(weights)
     place = pl.BlockSpec(memory_space=pl.ANY)
     shape = (count, *weights[0].shape[1:])
     return pl.pallas_call(
-        functools.partial(fetch_kernel, len(weights)),
+        functools.partial(fetch_kernel, len(weights), start),
         out_shape=[pltpu.VMEM(shape, jnp.bfloat16)] * len(weights),
         in_specs=[place] * (len(weights) + 1),
         out_specs=[VMEM] * len(weights),
@@ -310,35 +310,41 @@
 def experts_kernel(blocks, axis, *refs):
     pays = refs[:blocks]
     (
-        early_gate, early_up, early_down, gate_hbm, up_hbm, down_hbm, near_ref, far_ref, held_ref,
-        x_ref, share_ref, hidden_ref, held_sem,
+        _, _, _, _, gate_hbm, up_hbm, down_hbm, near_ref, far_ref, gate_a, up_a, gate_b, up_b,
+        held_ref, x_ref, share_ref, hidden_ref, held_sem, down_sem,
     ) = refs[blocks:]
+    early = (gate_a, up_a, gate_b, up_b)
     local, quarter, width = gate_hbm.shape
     fold = width // 2
     rest = 4
     tokens = blocks * (MAIN + rest)
     tall = GROUP * quarter
     groups = local // GROUP
-    half = local // 2
+    ready = len(early) // 2
 
     def load(g):
-        slot = g % 2
-        copies = []
-        for k in range(GROUP):
-            if g < groups:
-                e = g * GROUP + k
-                pair = gate_hbm.at[e], up_hbm.at[e]
-            else:
-                pair = down_hbm.at[half + k], down_hbm.at[half + GROUP + k]
-            for p in range(2):
-                copies.append(
-                    pltpu.make_async_copy(
-                        pair[p], held_ref.at[slot, p, k], held_sem.at[slot, p, k]
-                    )
-                )
-        return copies
-
-    for g in (1, 2):
+        return [
+            pltpu.make_async_copy(
+                source.at[g * GROUP + k], held_ref.at[g - ready, p, k], held_sem.at[g - ready, p, k]
+            )
+            for p, source in enumerate((gate_hbm, up_hbm))
+            for k in range(GROUP)
+        ]
+
+    cuts = fold // CUT
+
+    def load_down(c):
+        return [
+            pltpu.make_async_copy(
+                down_hbm.at[pl.ds(q * GROUP, GROUP), :, pl.ds(side * fold + c * CUT, CUT)],
+                early[q].at[:, :, pl.ds(side * fold + c * CUT, CUT)],
+                down_sem.at[c, q, side],
+            )
+            for q in range(groups)
+            for side in range(2)
+        ]
+
+    for g in range(ready, groups):
         for copy in load(g):
             copy.start()
 
@@ -362,20 +368,9 @@
     )
     first = lax.axis_index(axis) * local
 
-    for g in range(groups):
-        if g == 0:
-            gate_w, up_w = early_gate[...], early_up[...]
-        else:
-            for copy in load(g):
-                copy.wait()
-            gate_w, up_w = held_ref[g % 2, 0], held_ref[g % 2, 1]
-        flat = (((1,), (1,)), ((), ()))
-        gate = lax.dot_general(
-            gate_w.reshape(tall, width), x_ref[...], flat, preferred_element_type=jnp.float32
-        )
-        upper = lax.dot_general(
-            up_w.reshape(tall, width), x_ref[...], flat, preferred_element_type=jnp.float32
-        )
+    flat = (((1,), (1,)), ((), ()))
+
+    def finish(g, gate, upper):
         hidden = jax.nn.silu(gate) * upper
         weight = stack(
             [
@@ -384,23 +379,43 @@
             ]
         )
         hidden_ref[:, g * tall : (g + 1) * tall] = (hidden * weight).T.astype(hidden_ref.dtype)
-        if 1 <= g < groups - 1:
-            for copy in load(g + 2):
-                copy.start()
-
-    for copy in load(groups):
-        copy.wait()
-    deep = half * quarter
-    slot = groups % 2
-    for at in range(0, fold, CUT):
+
+    made = None
+    for g in range(groups):
+        if g >= ready:
+            for copy in load(g):
+                copy.wait()
+            few = -(-cuts // (groups - ready))
+            for c in range((g - ready) * few, min((g - ready + 1) * few, cuts)):
+                for copy in load_down(c):
+                    copy.start()
+        if g < ready:
+            gate_at, up_at = early[2 * g], early[2 * g + 1]
+        else:
+            gate_at, up_at = held_ref.at[g - ready, 0], held_ref.at[g - ready, 1]
+        gate, upper = [
+            lax.dot_general(
+                at[...].reshape(tall, width), x_ref[...], flat, preferred_element_type=jnp.float32
+            )
+            for at in (gate_at, up_at)
+        ]
+        if made is not None:
+            finish(g - 1, *made)
+        made = gate, upper
+    for c in range(cuts):
+        at = c * CUT
+        for copy in load_down(c):
+            copy.wait()
+        if c == 0:
+            finish(groups - 1, *made)
         low, high = [
-            jnp.dot(
-                hidden_ref[:, :deep], early_down[:, :, c : c + CUT].reshape(deep, CUT),
-                preferred_element_type=jnp.float32,
-            )
-            + jnp.dot(
-                hidden_ref[:, deep:], held_ref[slot, :, :, :, c : c + CUT].reshape(deep, CUT),
-                preferred_element_type=jnp.float32,
+            sum(
+                jnp.dot(
+                    hidden_ref[:, q * tall : (q + 1) * tall],
+                    early[q][:, :, c : c + CUT].reshape(tall, CUT),
+                    preferred_element_type=jnp.float32,
+                )
+                for q in range(groups)
             )
             for c in (at, fold + at)
         ]
@@ -425,15 +440,17 @@
     held = [pltpu.with_memory_space_constraint(a, pltpu.VMEM) for a in (*pays, *early)]
     return pl.pallas_call(
         functools.partial(experts_kernel, blocks, axis),
-        out_shape=(half, half),
+        out_shape=[half, half] + [pltpu.VMEM(a.shape, a.dtype) for a in early],
         in_specs=[VMEM] * len(held) + [place] * 3,
-        out_specs=(VMEM, VMEM),
+        out_specs=[VMEM] * (2 + len(early)),
+        input_output_aliases={blocks + i: 2 + i for i in range(len(early))},
         scratch_shapes=[
-            pltpu.VMEM((2, 2, GROUP, quarter, width), jnp.bfloat16),
+            pltpu.VMEM((local // GROUP - 2, 2, GROUP, quarter, width), jnp.bfloat16),
             pltpu.VMEM((tokens, width), jnp.bfloat16),
             pltpu.VMEM((LANES // 2, tokens), jnp.float32),
             pltpu.VMEM((tokens, local * quarter), jnp.bfloat16),
-            pltpu.SemaphoreType.DMA((2, 2, GROUP)),
+            pltpu.SemaphoreType.DMA((local // GROUP - 2, 2, GROUP)),
+            pltpu.SemaphoreType.DMA((width // 2 // CUT, local // GROUP, 2)),
         ],
         compiler_params=pltpu.CompilerParams(vmem_limit_bytes=VMEM_BYTES),
         cost_estimate=pl.CostEstimate(
@@ -441,7 +458,7 @@
             bytes_accessed=4 * local * quarter * width,
             transcendentals=tokens * local * quarter,
         ),
-    )(*held, *[pltpu.with_memory_space_constraint(w, pltpu.HBM) for w in (w_gate, w_up, w_down)])
+    )(*held, *[pltpu.with_memory_space_constraint(w, pltpu.HBM) for w in (w_gate, w_up, w_down)])[:2]
 
 
 def final_kernel(mixed_ref, *refs):
@@ -479,13 +496,15 @@
     back = {k: [(i, (i - k) % members) for i in range(members)] for k in shifts}
     line = [pay] + [lax.ppermute(pay, "expert", ahead[k]) for k in shifts]
     gate, up = jnp.swapaxes(w_gate, 1, 2), jnp.swapaxes(w_up, 1, 2)
-    pair = fetch((gate, up), GROUP, pay)
+    pair = fetch((gate, up), 0, GROUP, pay)
     line[1], *pair = lax.optimization_barrier((line[1], *pair))
     pays = line + [lax.ppermute(p, "dp", side) for p in line]
-    (down,) = fetch((w_down,), w_down.shape[0] // 2, line[-1])
-    pays[5], down = lax.optimization_barrier((pays[5], down))
+    second = fetch((gate, up), GROUP, GROUP, line[-1])
+    *x_side, first_two, next_two = lax.optimization_barrier((*pays[members:], *second))
+    second = [first_two, next_two]
+    pays = pays[:members] + x_side
     pays = pays + [lax.ppermute(p, "dp", twin) for p in pays]
-    near, far = experts(pays, (*pair, down), gate, up, w_down, "expert")
+    near, far = experts(pays, (*pair, *second), gate, up, w_down, "expert")
     far = lax.ppermute(far, "dp", twin)
     near = (near.astype(jnp.float32) + far.astype(jnp.float32)).astype(jnp.bfloat16)
     peer = lax.ppermute(near[members:], "dp", side)

time: 90.2 us -> 86.8 us (0.962)
  Pallas kernels: 44.3 us -> 40.6 us
  starting transfers between devices: 16.6 us -> 19 us
  waiting for transfers between devices: 25.3 us -> 23.2 us
    pallas_call x1, Pallas kernels: 26.3 us -> 22.6 us  [experts(): pl.pallas_call(functools.partial(experts_kernel, blocks, axis), out_shape...]
    ppermute x4, waiting for transfers between devices: 2.48 us -> 0.01 us  [gathered(): pays = line + [lax.ppermute(p, 'dp', side) for p in line]]
    ppermute x3, waiting for transfers between devices: 0.01 us -> 1.06 us  [gathered(): line = [pay] + [lax.ppermute(pay, 'expert', ahead[k]) for k in shifts]]
    ppermute x4, starting transfers between devices: 4.12 us -> 5.07 us  [gathered(): pays = line + [lax.ppermute(p, 'dp', side) for p in line]]
    ppermute x3, starting transfers between devices: 3.83 us -> 4.77 us  [gathered(): lax.ppermute(near[i + 1], 'expert', back[k])]
  transfers between devices with their start and end apart: 20 -> 20, of which waited for: 10 -> 9; matrix products, arithmetic and copies ran while one was open for 0% -> 0% of each run, Pallas kernels for 10% -> 11%
where the time goes in v3:
time: 86.8 us; the launch traced here: 86.5 us
  Pallas kernels  40.6 us (47%)
  waiting for transfers between devices  23.2 us (27%)
  starting transfers between devices  19 us (22%)
  local copies, waits for them, and re-layouts  2.22 us (3%)
  other arithmetic  1.41 us (2%)
    pallas_call x1, Pallas kernels, experts(): pl.pallas_call(functools.partial(experts_kernel, blocks, axis), out_shape...  22.6 us
    ppermute x1, waiting for transfers between devices, gathered(): peer = lax.ppermute(near[members:], 'dp', side)  10.8 us
    pallas_call x2, Pallas kernels, fetch(): pl.pallas_call(functools.partial(fetch_kernel, len(weights), start), out_...  9.42 us
    ppermute x3, waiting for transfers between devices, gathered(): lax.ppermute(near[i + 1], 'expert', back[k])  8.24 us
    pallas_call x1, Pallas kernels, front(): pl.pallas_call(front_kernel, out_shape=(jax.ShapeDtypeStruct((MAIN, width...  6.6 us
    ppermute x3, starting transfers between devices, gathered(): line = [pay] + [lax.ppermute(pay, 'expert', ahead[k]) for k in shifts]  6.06 us
    ppermute x4, starting transfers between devices, gathered(): pays = line + [lax.ppermute(p, 'dp', side) for p in line]  5.07 us
    ppermute x3, starting transfers between devices, gathered(): lax.ppermute(near[i + 1], 'expert', back[k])  4.77 us
  transfers between devices with their start and end apart: 20, of which 9 were waited for; matrix products, arithmetic and copies ran while one was open for 0% of the time, Pallas kernels for 11%

profile of v3, /device:TPU:0, one launch (start us, length us, event | category | flops | bytes accessed | tf_op | source)
XLA Modules:
  0.0 86.5 jit_solution(14489321488568837991)
XLA Ops:
  0.0 6.6 %shard_map.136 = (bf16[8,6272]{1,0:T(8,128)(2,1)}, f32[6,2,4096]{2,1,0:T(2,128)}) custom-call(bf16[6,2,4096]{2,1,0:T(2,128)(2,1)} %q_ref.1, bf16[6,2,256]{2,1,0:T(2,128)(2,1)} %nk_ref.1, bf16[6,2,256]{2,1,0:T(2,128)(2,1)} %nv_ref.1, bf16[6,32,256]{2,1,0:T(8,128)(2,1)} %ck_ref.1, bf16[6,32,256]{2,1,0:T(8,128)(2,1)} %cv_ref.1, s32[6]{0:T(128)} %len_ref.1, ...), custom_call_target="tpu_custom_call" | custom-call | flops 10000000 | bytes 1000000 | tf_op jit(solution)/shard_map/pallas_call | solution.py:265
  6.6 5.0 %collective-permute-start.2 = (bf16[8,6272]{1,0:T(8,128)(2,1)}, bf16[8,6272]{1,0:T(8,128)(2,1)S(1)}, u32[]{:S(2)}, u32[]{:S(2)}) collective-permute-start(bf16[8,6272]{1,0:T(8,128)(2,1)} %get-tuple-element.23.refs_2_.refs_0_), channel_id=1, source_target_pairs={{0,12},{4,0},{8,4},{12,8},{1,13},{5,1},{9,5},{13,9},{2,14},{6,2},{... | collective-permute-start | bytes 301064 | tf_op jit(solution)/shard_map/ppermute | solution.py:497
  11.7 1.0 %collective-permute-start.1 = (bf16[8,6272]{1,0:T(8,128)(2,1)}, bf16[8,6272]{1,0:T(8,128)(2,1)S(1)}, u32[]{:S(2)}, u32[]{:S(2)}) collective-permute-start(bf16[8,6272]{1,0:T(8,128)(2,1)} %get-tuple-element.23.refs_2_.refs_0_), channel_id=1, source_target_pairs={{0,4},{4,8},{8,12},{12,0},{1,5},{5,9},{9,13},{13,1},{2,6},{6,10},{... | collective-permute-start | bytes 301064 | tf_op jit(solution)/shard_map/ppermute | solution.py:497
  12.7 1.5 %collective-permute-start.3 = (bf16[8,6272]{1,0:T(8,128)(2,1)}, bf16[8,6272]{1,0:T(8,128)(2,1)S(1)}, u32[]{:S(2)}, u32[]{:S(2)}) collective-permute-start(bf16[8,6272]{1,0:T(8,128)(2,1)} %get-tuple-element.23.refs_2_.refs_0_), channel_id=1, source_target_pairs={{0,2},{2,0},{1,3},{3,1},{4,6},{6,4},{5,7},{7,5},{8,10},{10,8},{9,1... | collective-permute-start | bytes 301064 | tf_op jit(solution)/shard_map/ppermute | solution.py:501
  14.2 1.1 %collective-permute-done.2.refs_2_.refs_3_ = bf16[8,6272]{1,0:T(8,128)(2,1)S(1)} collective-permute-done((bf16[8,6272]{1,0:T(8,128)(2,1)}, bf16[8,6272]{1,0:T(8,128)(2,1)S(1)}, u32[]{:S(2)}, u32[]{:S(2)}) %collective-permute-start.2) | collective-permute-done | bytes 100384 | tf_op jit(solution)/shard_map/ppermute | solution.py:497
  15.2 1.5 %collective-permute-start.6 = (bf16[8,6272]{1,0:T(8,128)(2,1)S(1)}, bf16[8,6272]{1,0:T(8,128)(2,1)S(1)}, u32[]{:S(2)}, u32[]{:S(2)}) collective-permute-start(bf16[8,6272]{1,0:T(8,128)(2,1)S(1)} %collective-permute-done.2.refs_2_.refs_3_), channel_id=1, source_target_pairs={{0,2},{2,0},{1,3},{3,1},{4,6},{6,4},{5,7},{7,5},{8,10},{10,8},{9,1... | collective-permute-start | bytes 301064 | tf_op jit(solution)/shard_map/ppermute | solution.py:501
  16.7 0.9 %copy-done = bf16[8,6272]{1,0:T(8,128)(2,1)S(1)} copy-done((bf16[8,6272]{1,0:T(8,128)(2,1)S(1)}, bf16[8,6272]{1,0:T(8,128)(2,1)}, u32[]{:S(2)}) %copy-start) | copy-done | bytes 100376
  17.6 4.7 %shard_map.137 = (bf16[4,192,4096]{2,1,0:T(8,128)(2,1)S(1)}, bf16[4,192,4096]{2,1,0:T(8,128)(2,1)S(1)}) custom-call(bf16[16,192,4096]{2,1,0:T(8,128)(2,1)} %bitcast.11, bf16[16,192,4096]{2,1,0:T(8,128)(2,1)} %bitcast.14, bf16[8,6272]{1,0:T(8,128)(2,1)S(1)} %copy-done), custom_call_target="tpu_custom_call" | custom-call | bytes 12582912 | tf_op jit(solution)/shard_map/pallas_call | solution.py:299
  22.4 0.6 collective-permute-start.5
  23.0 1.5 %collective-permute-start.4 = (bf16[8,6272]{1,0:T(8,128)(2,1)S(1)}, bf16[8,6272]{1,0:T(8,128)(2,1)S(1)}, u32[]{:S(2)}, u32[]{:S(2)}) collective-permute-start(bf16[8,6272]{1,0:T(8,128)(2,1)S(1)} %collective-permute-done.refs_1_), channel_id=1, source_target_pairs={{0,2},{2,0},{1,3},{3,1},{4,6},{6,4},{5,7},{7,5},{8,10},{10,8},{9,1... | collective-permute-start | bytes 301064 | tf_op jit(solution)/shard_map/ppermute | solution.py:501
  24.5 0.5 collective-permute-start.10
  25.0 4.7 %shard_map.138 = (bf16[4,192,4096]{2,1,0:T(8,128)(2,1)S(1)}, bf16[4,192,4096]{2,1,0:T(8,128)(2,1)S(1)}) custom-call(bf16[16,192,4096]{2,1,0:T(8,128)(2,1)} %bitcast.12, bf16[16,192,4096]{2,1,0:T(8,128)(2,1)} %bitcast.15, bf16[8,6272]{1,0:T(8,128)(2,1)S(1)} %collective-permute-done.2.refs_2_.refs_3_), custom_call_target="tpu_custom_call" | custom-call | bytes 12582912 | tf_op jit(solution)/shard_map/pallas_call | solution.py:299
  29.8 0.5 collective-permute-start.8
  30.4 0.4 collective-permute-start.12
  30.9 0.4 collective-permute-start.14
  31.3 0.3 collective-permute-done.11.refs_12_
  31.6 0.2 collective-permute-done.12.refs_13_
  31.7 0.4 collective-permute-done.13.refs_14_
  32.2 22.6 %shard_map.139 = (bf16[8,8,6144]{2,1,0:T(8,128)(2,1)}, bf16[8,8,6144]{2,1,0:T(8,128)(2,1)}, bf16[4,192,4096]{2,1,0:T(8,128)(2,1)S(1)}, bf16[4,192,4096]{2,1,0:T(...) custom-call(bf16[8,6272]{1,0:T(8,128)(2,1)S(1)} %copy-done.1, ...), custom_call_target="tpu_custom_call", output_to_operand_aliasing={{2}: (16, {}), {3}: (17, {}), {4}: (18, {}), {5}: (19, {})} | custom-call | flops 14495514624 | bytes 50331648 | tf_op jit(solution)/shard_map/pallas_call | solution.py:441
  54.9 0.4 collective-permute-start.15
  55.3 2.2 %collective-permute-done.15 = bf16[8,8,6144]{2,1,0:T(8,128)(2,1)S(1)} collective-permute-done((bf16[8,8,6144]{2,1,0:T(8,128)(2,1)}, bf16[8,8,6144]{2,1,0:T(8,128)(2,1)S(1)}, u32[]{:S(2)}, u32[]{:S(2)}) %collective-permute-start.15) | collective-permute-done | bytes 786464 | tf_op jit(solution)/shard_map/ppermute | solution.py:508
  57.4 1.3 %add_convert_fusion = bf16[8,8,6144]{2,1,0:T(8,128)(2,1)S(1)} fusion(bf16[8,8,6144]{2,1,0:T(8,128)(2,1)S(1)} %collective-permute-done.15, bf16[8,8,6144]{2,1,0:T(8,128)(2,1)} %get-tuple-element.37), kind=kLoop, calls=%fused_computation | loop fusion | flops 1572864 | bytes 2359296 | tf_op jit(solution)/shard_map/convert_element_type | solution.py:509
  58.8 0.6 collective-permute-start.16
  59.4 10.8 %collective-permute-done.16 = bf16[4,8,6144]{2,1,0:T(8,128)(2,1)S(1)} collective-permute-done((bf16[4,8,6144]{2,1,0:T(8,128)(2,1)S(1)}, bf16[4,8,6144]{2,1,0:T(8,128)(2,1)S(1)}, u32[]{:S(2)}, u32[]{:S(2)}) %collective-permute-start.16) | collective-permute-done | bytes 393248 | tf_op jit(solution)/shard_map/ppermute | solution.py:510
  70.3 0.7 slice_bitcast_fusion
  71.0 0.5 collective-permute-start.19
  71.4 3.7 %collective-permute-start.18 = (bf16[8,6144]{1,0:T(8,128)(2,1)S(1)}, bf16[8,6144]{1,0:T(8,128)(2,1)S(1)}, u32[]{:S(2)}, u32[]{:S(2)}) collective-permute-start(bf16[8,6144]{1,0:T(8,128)(2,1)S(1)} %get-tuple-element.40), channel_id=1, source_target_pairs={{0,12},{4,0},{8,4},{12,8},{1,13},{5,1},{9,5},{13,9},{2,14},{6,2},{... | collective-permute-start | bytes 294920 | tf_op jit(solution)/shard_map/ppermute | solution.py:513
  75.2 0.6 collective-permute-start.17
  75.7 2.8 %collective-permute-done.19.refs_3_ = bf16[8,6144]{1,0:T(8,128)(2,1)S(1)} collective-permute-done((bf16[8,6144]{1,0:T(8,128)(2,1)S(1)}, bf16[8,6144]{1,0:T(8,128)(2,1)S(1)}, u32[]{:S(2)}, u32[]{:S(2)}) %collective-permute-start.19) | collective-permute-done | bytes 98336 | tf_op jit(solution)/shard_map/ppermute | solution.py:513
  78.5 5.5 %collective-permute-done.17.refs_1_ = bf16[8,6144]{1,0:T(8,128)(2,1)S(1)} collective-permute-done((bf16[8,6144]{1,0:T(8,128)(2,1)S(1)}, bf16[8,6144]{1,0:T(8,128)(2,1)S(1)}, u32[]{:S(2)}, u32[]{:S(2)}) %collective-permute-start.17) | collective-permute-done | bytes 98336 | tf_op jit(solution)/shard_map/ppermute | solution.py:513
  84.0 0.6 copy-done.4
  84.6 1.9 %shard_map.140 = bf16[6,2,4096]{2,1,0:T(2,128)(2,1)} custom-call(f32[6,2,4096]{2,1,0:T(2,128)} %get-tuple-element.22.mixed_ref, bf16[8,6144]{1,0:T(8,128)(2,1)} %get-tuple-element.42.refs_0_, bf16[8,6144]{1,0:T(8,128)(2,1)} %copy-done.4, bf16[8,6144]{1,0:T(8,128)(2,1)} %copy-done.3, bf16[8,6144]{1,0:T(8,128)(2,1)} %copy-done.2), custom_call_target="tpu_custom_call" | custom-call | tf_op jit(solution)/shard_map/pallas_call | solution.py:515
  (27 shorter events, 0.6 us)
Async XLA Ops:
  6.6 8.6 %collective-permute-start.2 = (bf16[8,6272]{1,0:T(8,128)(2,1)}, bf16[8,6272]{1,0:T(8,128)(2,1)S(1)}, u32[]{:S(2)}, u32[]{:S(2)}) collective-permute-start(bf16[8,6272]{1,0:T(8,128)(2,1)} %get-tuple-element.23.refs_2_.refs_0_), channel_id=1, source_target_pairs={{0,12},{4,0},{8,4},{12,8},{1,13},{5,1},{9,5},{13,9},{2,14},{6,2},{... | collective-permute-start | bytes 301064 | tf_op jit(solution)/shard_map/ppermute | solution.py:497
  11.7 10.7 %collective-permute-start = (bf16[8,6272]{1,0:T(8,128)(2,1)}, bf16[8,6272]{1,0:T(8,128)(2,1)S(1)}, u32[]{:S(2)}, u32[]{:S(2)}) collective-permute-start(bf16[8,6272]{1,0:T(8,128)(2,1)} %get-tuple-element.23.refs_2_.refs_0_), channel_id=1, source_target_pairs={{0,8},{4,12},{8,0},{12,4},{1,9},{5,13},{9,1},{13,5},{2,10},{6,14},... | collective-permute-start | bytes 301064 | tf_op jit(solution)/shard_map/ppermute | solution.py:497
  11.7 10.7 %collective-permute-start.1 = (bf16[8,6272]{1,0:T(8,128)(2,1)}, bf16[8,6272]{1,0:T(8,128)(2,1)S(1)}, u32[]{:S(2)}, u32[]{:S(2)}) collective-permute-start(bf16[8,6272]{1,0:T(8,128)(2,1)} %get-tuple-element.23.refs_2_.refs_0_), channel_id=1, source_target_pairs={{0,4},{4,8},{8,12},{12,0},{1,5},{5,9},{9,13},{13,1},{2,6},{6,10},{... | collective-permute-start | bytes 301064 | tf_op jit(solution)/shard_map/ppermute | solution.py:497
  12.7 11.8 %collective-permute-start.3 = (bf16[8,6272]{1,0:T(8,128)(2,1)}, bf16[8,6272]{1,0:T(8,128)(2,1)S(1)}, u32[]{:S(2)}, u32[]{:S(2)}) collective-permute-start(bf16[8,6272]{1,0:T(8,128)(2,1)} %get-tuple-element.23.refs_2_.refs_0_), channel_id=1, source_target_pairs={{0,2},{2,0},{1,3},{3,1},{4,6},{6,4},{5,7},{7,5},{8,10},{10,8},{9,1... | collective-permute-start | bytes 301064 | tf_op jit(solution)/shard_map/ppermute | solution.py:501
  15.2 9.8 %collective-permute-start.6 = (bf16[8,6272]{1,0:T(8,128)(2,1)S(1)}, bf16[8,6272]{1,0:T(8,128)(2,1)S(1)}, u32[]{:S(2)}, u32[]{:S(2)}) collective-permute-start(bf16[8,6272]{1,0:T(8,128)(2,1)S(1)} %collective-permute-done.2.refs_2_.refs_3_), channel_id=1, source_target_pairs={{0,2},{2,0},{1,3},{3,1},{4,6},{6,4},{5,7},{7,5},{8,10},{10,8},{9,1... | collective-permute-start | bytes 301064 | tf_op jit(solution)/shard_map/ppermute | solution.py:501
  16.7 0.9 %copy-start = (bf16[8,6272]{1,0:T(8,128)(2,1)S(1)}, bf16[8,6272]{1,0:T(8,128)(2,1)}, u32[]{:S(2)}) copy-start(bf16[8,6272]{1,0:T(8,128)(2,1)} %get-tuple-element.23.refs_2_.refs_0_) | copy-start | bytes 301060
  17.6 6.9 %copy-start.1 = (bf16[8,6272]{1,0:T(8,128)(2,1)S(1)}, bf16[8,6272]{1,0:T(8,128)(2,1)}, u32[]{:S(2)}) copy-start(bf16[8,6272]{1,0:T(8,128)(2,1)} %get-tuple-element.23.refs_2_.refs_0_) | copy-start | bytes 301060
  22.4 7.4 %collective-permute-start.5 = (bf16[8,6272]{1,0:T(8,128)(2,1)S(1)}, bf16[8,6272]{1,0:T(8,128)(2,1)S(1)}, u32[]{:S(2)}, u32[]{:S(2)}) collective-permute-start(bf16[8,6272]{1,0:T(8,128)(2,1)S(1)} %collective-permute-done.1.refs_2_), channel_id=1, source_target_pairs={{0,2},{2,0},{1,3},{3,1},{4,6},{6,4},{5,7},{7,5},{8,10},{10,8},{9,1... | collective-permute-start | bytes 301064 | tf_op jit(solution)/shard_map/ppermute | solution.py:501
  23.0 7.3 %collective-permute-start.4 = (bf16[8,6272]{1,0:T(8,128)(2,1)S(1)}, bf16[8,6272]{1,0:T(8,128)(2,1)S(1)}, u32[]{:S(2)}, u32[]{:S(2)}) collective-permute-start(bf16[8,6272]{1,0:T(8,128)(2,1)S(1)} %collective-permute-done.refs_1_), channel_id=1, source_target_pairs={{0,2},{2,0},{1,3},{3,1},{4,6},{6,4},{5,7},{7,5},{8,10},{10,8},{9,1... | collective-permute-start | bytes 301064 | tf_op jit(solution)/shard_map/ppermute | solution.py:501
  24.4 5.9 %collective-permute-start.7 = (bf16[8,6272]{1,0:T(8,128)(2,1)S(1)}, bf16[8,6272]{1,0:T(8,128)(2,1)S(1)}, u32[]{:S(2)}, u32[]{:S(2)}) collective-permute-start(bf16[8,6272]{1,0:T(8,128)(2,1)S(1)} %copy-done.1), channel_id=1, source_target_pairs={{0,1},{1,0},{2,3},{3,2},{4,5},{5,4},{6,7},{7,6},{8,9},{9,8},{10,11... | collective-permute-start | bytes 301064 | tf_op jit(solution)/shard_map/ppermute | solution.py:506
  24.5 6.3 %collective-permute-start.10 = (bf16[8,6272]{1,0:T(8,128)(2,1)S(1)}, bf16[8,6272]{1,0:T(8,128)(2,1)S(1)}, u32[]{:S(2)}, u32[]{:S(2)}) collective-permute-start(bf16[8,6272]{1,0:T(8,128)(2,1)S(1)} %collective-permute-done.2.refs_2_.refs_3_), channel_id=1, source_target_pairs={{0,1},{1,0},{2,3},{3,2},{4,5},{5,4},{6,7},{7,6},{8,9},{9,8},{10,11... | collective-permute-start | bytes 301064 | tf_op jit(solution)/shard_map/ppermute | solution.py:506
  25.0 5.9 %collective-permute-start.9 = (bf16[8,6272]{1,0:T(8,128)(2,1)S(1)}, bf16[8,6272]{1,0:T(8,128)(2,1)S(1)}, u32[]{:S(2)}, u32[]{:S(2)}) collective-permute-start(bf16[8,6272]{1,0:T(8,128)(2,1)S(1)} %collective-permute-done.1.refs_2_), channel_id=1, source_target_pairs={{0,1},{1,0},{2,3},{3,2},{4,5},{5,4},{6,7},{7,6},{8,9},{9,8},{10,11... | collective-permute-start | bytes 301064 | tf_op jit(solution)/shard_map/ppermute | solution.py:506
  29.8 1.5 %collective-permute-start.8 = (bf16[8,6272]{1,0:T(8,128)(2,1)S(1)}, bf16[8,6272]{1,0:T(8,128)(2,1)S(1)}, u32[]{:S(2)}, u32[]{:S(2)}) collective-permute-start(bf16[8,6272]{1,0:T(8,128)(2,1)S(1)} %collective-permute-done.refs_1_), channel_id=1, source_target_pairs={{0,1},{1,0},{2,3},{3,2},{4,5},{5,4},{6,7},{7,6},{8,9},{9,8},{10,11... | collective-permute-start | bytes 301064 | tf_op jit(solution)/shard_map/ppermute | solution.py:506
  30.3 1.3 %collective-permute-start.11 = (bf16[8,6272]{1,0:T(8,128)(2,1)S(1)}, bf16[8,6272]{1,0:T(8,128)(2,1)S(1)}, u32[]{:S(2)}, u32[]{:S(2)}) collective-permute-start(bf16[8,6272]{1,0:T(8,128)(2,1)S(1)} %collective-permute-done.3.refs_4_), channel_id=1, source_target_pairs={{0,1},{1,0},{2,3},{3,2},{4,5},{5,4},{6,7},{7,6},{8,9},{9,8},{10,11... | collective-permute-start | bytes 301064 | tf_op jit(solution)/shard_map/ppermute | solution.py:506
  30.4 1.4 %collective-permute-start.12 = (bf16[8,6272]{1,0:T(8,128)(2,1)S(1)}, bf16[8,6272]{1,0:T(8,128)(2,1)S(1)}, u32[]{:S(2)}, u32[]{:S(2)}) collective-permute-start(bf16[8,6272]{1,0:T(8,128)(2,1)S(1)} %collective-permute-done.4.refs_5_), channel_id=1, source_target_pairs={{0,1},{1,0},{2,3},{3,2},{4,5},{5,4},{6,7},{7,6},{8,9},{9,8},{10,11... | collective-permute-start | bytes 301064 | tf_op jit(solution)/shard_map/ppermute | solution.py:506
  30.8 1.3 %collective-permute-start.13 = (bf16[8,6272]{1,0:T(8,128)(2,1)S(1)}, bf16[8,6272]{1,0:T(8,128)(2,1)S(1)}, u32[]{:S(2)}, u32[]{:S(2)}) collective-permute-start(bf16[8,6272]{1,0:T(8,128)(2,1)S(1)} %collective-permute-done.5.refs_6_), channel_id=1, source_target_pairs={{0,1},{1,0},{2,3},{3,2},{4,5},{5,4},{6,7},{7,6},{8,9},{9,8},{10,11... | collective-permute-start | bytes 301064 | tf_op jit(solution)/shard_map/ppermute | solution.py:506
  30.9 1.4 %collective-permute-start.14 = (bf16[8,6272]{1,0:T(8,128)(2,1)S(1)}, bf16[8,6272]{1,0:T(8,128)(2,1)S(1)}, u32[]{:S(2)}, u32[]{:S(2)}) collective-permute-start(bf16[8,6272]{1,0:T(8,128)(2,1)S(1)} %collective-permute-done.6.refs_7_), channel_id=1, source_target_pairs={{0,1},{1,0},{2,3},{3,2},{4,5},{5,4},{6,7},{7,6},{8,9},{9,8},{10,11... | collective-permute-start | bytes 301064 | tf_op jit(solution)/shard_map/ppermute | solution.py:506
  54.9 2.6 %collective-permute-start.15 = (bf16[8,8,6144]{2,1,0:T(8,128)(2,1)}, bf16[8,8,6144]{2,1,0:T(8,128)(2,1)S(1)}, u32[]{:S(2)}, u32[]{:S(2)}) collective-permute-start(bf16[8,8,6144]{2,1,0:T(8,128)(2,1)} %get-tuple-element.38), channel_id=1, source_target_pairs={{0,1},{1,0},{2,3},{3,2},{4,5},{5,4},{6,7},{7,6},{8,9},{9,8},{10,11... | collective-permute-start | bytes 2359304 | tf_op jit(solution)/shard_map/ppermute | solution.py:508
  58.8 11.4 %collective-permute-start.16 = (bf16[4,8,6144]{2,1,0:T(8,128)(2,1)S(1)}, bf16[4,8,6144]{2,1,0:T(8,128)(2,1)S(1)}, u32[]{:S(2)}, u32[]{:S(2)}) collective-permute-start(bf16[4,8,6144]{2,1,0:T(8,128)(2,1)S(1)} %slice.25), channel_id=1, source_target_pairs={{0,2},{2,0},{1,3},{3,1},{4,6},{6,4},{5,7},{7,5},{8,10},{10,8},{9,1... | collective-permute-start | bytes 1179656 | tf_op jit(solution)/shard_map/ppermute | solution.py:510
  71.0 7.5 %collective-permute-start.19 = (bf16[8,6144]{1,0:T(8,128)(2,1)S(1)}, bf16[8,6144]{1,0:T(8,128)(2,1)S(1)}, u32[]{:S(2)}, u32[]{:S(2)}) collective-permute-start(bf16[8,6144]{1,0:T(8,128)(2,1)S(1)} %get-tuple-element.39), channel_id=1, source_target_pairs={{0,4},{4,8},{8,12},{12,0},{1,5},{5,9},{9,13},{13,1},{2,6},{6,10},{... | collective-permute-start | bytes 294920 | tf_op jit(solution)/shard_map/ppermute | solution.py:513
  71.4 7.1 %collective-permute-start.18 = (bf16[8,6144]{1,0:T(8,128)(2,1)S(1)}, bf16[8,6144]{1,0:T(8,128)(2,1)S(1)}, u32[]{:S(2)}, u32[]{:S(2)}) collective-permute-start(bf16[8,6144]{1,0:T(8,128)(2,1)S(1)} %get-tuple-element.40), channel_id=1, source_target_pairs={{0,12},{4,0},{8,4},{12,8},{1,13},{5,1},{9,5},{13,9},{2,14},{6,2},{... | collective-permute-start | bytes 294920 | tf_op jit(solution)/shard_map/ppermute | solution.py:513
  75.2 8.8 %collective-permute-start.17 = (bf16[8,6144]{1,0:T(8,128)(2,1)S(1)}, bf16[8,6144]{1,0:T(8,128)(2,1)S(1)}, u32[]{:S(2)}, u32[]{:S(2)}) collective-permute-start(bf16[8,6144]{1,0:T(8,128)(2,1)S(1)} %get-tuple-element.41), channel_id=1, source_target_pairs={{0,8},{4,12},{8,0},{12,4},{1,9},{5,13},{9,1},{13,5},{2,10},{6,14},... | collective-permute-start | bytes 294920 | tf_op jit(solution)/shard_map/ppermute | solution.py:513
  78.5 5.5 %copy-start.2 = (bf16[8,6144]{1,0:T(8,128)(2,1)}, bf16[8,6144]{1,0:T(8,128)(2,1)S(1)}, u32[]{:S(2)}) copy-start(bf16[8,6144]{1,0:T(8,128)(2,1)S(1)} %collective-permute-done.19.refs_3_) | copy-start | bytes 294916
  78.5 5.5 %copy-start.3 = (bf16[8,6144]{1,0:T(8,128)(2,1)}, bf16[8,6144]{1,0:T(8,128)(2,1)S(1)}, u32[]{:S(2)}) copy-start(bf16[8,6144]{1,0:T(8,128)(2,1)S(1)} %collective-permute-done.18.refs_2_) | copy-start | bytes 294916
  84.0 0.6 copy-start.4

commit v4 on v3

--- a/solution.py
+++ b/solution.py
@@ -156,7 +156,7 @@
 VMEM = pl.BlockSpec(memory_space=pltpu.VMEM)
 SMEM = pl.BlockSpec(memory_space=pltpu.SMEM)
 LANES = 128
-VMEM_BYTES = 34 * 2**20
+VMEM_BYTES = 32 * 2**20
 MAIN = 8
 
 
@@ -265,8 +265,8 @@
     return pl.pallas_call(
         front_kernel,
         out_shape=(
-            jax.ShapeDtypeStruct((MAIN, width + width // 2 + LANES), jnp.bfloat16),
-            jax.ShapeDtypeStruct((rows, steps, width), jnp.float32),
+            pltpu.VMEM((MAIN, width + width // 2 + LANES), jnp.bfloat16),
+            pltpu.VMEM((rows, steps, width), jnp.float32),
         ),
         in_specs=[VMEM] * 5 + [SMEM] * 2 + [VMEM] * 4,
         out_specs=(VMEM, VMEM),
@@ -275,6 +275,7 @@
       norm_gain, routes, route_gains)
 
 
+SPLIT = 3584
 GROUP = 4
 CUT = 512
 
@@ -435,7 +436,7 @@
     local, quarter, width = w_down.shape
     tokens = blocks * 12
     packed = width + width // 2
-    half = jax.ShapeDtypeStruct((blocks // 2, MAIN, packed), jnp.bfloat16)
+    half = pltpu.VMEM((blocks // 2, MAIN, packed), jnp.bfloat16)
     place = pl.BlockSpec(memory_space=pl.ANY)
     held = [pltpu.with_memory_space_constraint(a, pltpu.VMEM) for a in (*pays, *early)]
     return pl.pallas_call(
@@ -507,17 +508,25 @@
     near, far = experts(pays, (*pair, *second), gate, up, w_down, "expert")
     far = lax.ppermute(far, "dp", twin)
     near = (near.astype(jnp.float32) + far.astype(jnp.float32)).astype(jnp.bfloat16)
-    peer = lax.ppermute(near[members:], "dp", side)
-    near = (near[:members].astype(jnp.float32) + peer.astype(jnp.float32)).astype(jnp.bfloat16)
-    parts = [near[0]] + [
-        lax.ppermute(near[i + 1], "expert", back[k]) for i, k in enumerate(shifts)
+    own, other = near[:members], near[members:]
+    peer = lax.ppermute(other[1:, :, :SPLIT], "dp", side)
+    lines = [
+        lax.ppermute(other[i + 1, :, SPLIT:], "expert", back[k]) for i, k in enumerate(shifts)
     ]
+    first = own[1:, :, :SPLIT].astype(jnp.float32) + peer.astype(jnp.float32)
+    own_line = stack([first.astype(jnp.bfloat16), own[1:, :, SPLIT:]], axis=2)
+    parts = [own[0]] + [
+        lax.ppermute(own_line[i], "expert", back[k]) for i, k in enumerate(shifts)
+    ]
+    last = other[0, :, SPLIT:].astype(jnp.float32) + sum(p.astype(jnp.float32) for p in lines)
+    crossed = stack([other[0, :, :SPLIT], last.astype(jnp.bfloat16)], axis=1)
+    parts.append(lax.ppermute(crossed, "dp", side))
     return pl.pallas_call(
         final_kernel,
         out_shape=jax.ShapeDtypeStruct(residual.shape, jnp.bfloat16),
-        in_specs=[VMEM] * (1 + members),
+        in_specs=[VMEM] * (1 + len(parts)),
         out_specs=VMEM,
-    )(mixed, *parts)
+    )(*[pltpu.with_memory_space_constraint(a, pltpu.VMEM) for a in (mixed, *parts)])
 
 
 def solution(mesh):

time: 86.8 us -> 77.3 us (0.89)
  waiting for transfers between devices: 23.2 us -> 13.1 us
  starting transfers between devices: 19 us -> 26.1 us
  Pallas kernels: 40.6 us -> 37.6 us
  local copies, waits for them, and re-layouts: 2.22 us -> 0.04 us
  other arithmetic: 1.41 us -> 0.29 us
    ppermute x4 -> x8, waiting for transfers between devices: 19.1 us -> 9.42 us  [the longest x3 5.24 us: gathered(): lax.ppermute(own_line[i], 'expert', back[k])]
    ppermute x4 -> x8, starting transfers between devices: 5.38 us -> 12.3 us  [the longest x3 5.58 us: gathered(): lax.ppermute(other[i + 1, :, SPLIT:], 'expert', back[k])]
    unnamed x10 -> x0, local copies, waits for them, and re-layouts: 1.54 us -> none
    pallas_call x1, Pallas kernels: 22.6 us -> 21.4 us  [experts(): pl.pallas_call(functools.partial(experts_kernel, blocks, axis), out_shape...]
    convert_element_type x1, other arithmetic: 1.31 us -> 0.18 us  [gathered(): (near.astype(jnp.float32) + far.astype(jnp.float32)).astype(jnp.bfloat16)]
    pallas_call x1, Pallas kernels: 1.92 us -> 0.81 us  [gathered(): pl.pallas_call(final_kernel, out_shape=jax.ShapeDtypeStruct(residual.shap...]
  transfers between devices with their start and end apart: 20 -> 24, of which waited for: 9 -> 11; matrix products, arithmetic and copies ran while one was open for 0% -> 0% of each run, Pallas kernels for 11% -> 12%
where the time goes in v4:
time: 77.3 us; the launch traced here: 77.2 us
  Pallas kernels  37.6 us (49%)
  starting transfers between devices  26.1 us (34%)
  waiting for transfers between devices  13.1 us (17%)
    pallas_call x1, Pallas kernels, experts(): pl.pallas_call(functools.partial(experts_kernel, blocks, axis), out_shape...  21.4 us
    pallas_call x2, Pallas kernels, fetch(): pl.pallas_call(functools.partial(fetch_kernel, len(weights), start), out_...  9.4 us
    ppermute x3, starting transfers between devices, gathered(): line = [pay] + [lax.ppermute(pay, 'expert', ahead[k]) for k in shifts]  6.11 us
    pallas_call x1, Pallas kernels, front(): pl.pallas_call(front_kernel, out_shape=(pltpu.VMEM((MAIN, width + width /...  5.95 us
    ppermute x3, starting transfers between devices, gathered(): lax.ppermute(other[i + 1, :, SPLIT:], 'expert', back[k])  5.58 us
    ppermute x3, waiting for transfers between devices, gathered(): lax.ppermute(own_line[i], 'expert', back[k])  5.24 us
    ppermute x4, starting transfers between devices, gathered(): pays = line + [lax.ppermute(p, 'dp', side) for p in line]  5.07 us
    ppermute x3, starting transfers between devices, gathered(): lax.ppermute(own_line[i], 'expert', back[k])  4.55 us
  transfers between devices with their start and end apart: 24, of which 11 were waited for; matrix products, arithmetic and copies ran while one was open for 0% of the time, Pallas kernels for 12%

profile of v4, /device:TPU:0, one launch (start us, length us, event | category | flops | bytes accessed | tf_op | source)
XLA Modules:
  0.0 77.2 jit_solution(8503560532561385264)
XLA Ops:
  0.0 5.9 %shard_map.136 = (bf16[8,6272]{1,0:T(8,128)(2,1)S(1)}, f32[6,2,4096]{2,1,0:T(2,128)S(1)}) custom-call(bf16[6,2,4096]{2,1,0:T(2,128)(2,1)} %q_ref.1, bf16[6,2,256]{2,1,0:T(2,128)(2,1)} %nk_ref.1, bf16[6,2,256]{2,1,0:T(2,128)(2,1)} %nv_ref.1, bf16[6,32,256]{2,1,0:T(8,128)(2,1)} %ck_ref.1, bf16[6,32,256]{2,1,0:T(8,128)(2,1)} %cv_ref.1, s32[6]{0:T(128)} %len_ref.1, ...), custom_call_target="tpu_custom_call" | custom-call | flops 10000000 | bytes 1000000 | tf_op jit(solution)/shard_map/pallas_call | solution.py:265
  6.0 5.1 %collective-permute-start.2 = (bf16[8,6272]{1,0:T(8,128)(2,1)S(1)}, bf16[8,6272]{1,0:T(8,128)(2,1)S(1)}, u32[]{:S(2)}, u32[]{:S(2)}) collective-permute-start(bf16[8,6272]{1,0:T(8,128)(2,1)S(1)} %get-tuple-element.23.refs_2_.refs_0_), channel_id=1, source_target_pairs={{0,12},{4,0},{8,4},{12,8},{1,13},{5,1},{9,5},{13,9},{2,14},{6,2},{... | collective-permute-start | bytes 301064 | tf_op jit(solution)/shard_map/ppermute | solution.py:498
  11.1 1.0 %collective-permute-start.1 = (bf16[8,6272]{1,0:T(8,128)(2,1)S(1)}, bf16[8,6272]{1,0:T(8,128)(2,1)S(1)}, u32[]{:S(2)}, u32[]{:S(2)}) collective-permute-start(bf16[8,6272]{1,0:T(8,128)(2,1)S(1)} %get-tuple-element.23.refs_2_.refs_0_), channel_id=1, source_target_pairs={{0,4},{4,8},{8,12},{12,0},{1,5},{5,9},{9,13},{13,1},{2,6},{6,10},{... | collective-permute-start | bytes 301064 | tf_op jit(solution)/shard_map/ppermute | solution.py:498
  12.1 1.5 %collective-permute-start.3 = (bf16[8,6272]{1,0:T(8,128)(2,1)S(1)}, bf16[8,6272]{1,0:T(8,128)(2,1)S(1)}, u32[]{:S(2)}, u32[]{:S(2)}) collective-permute-start(bf16[8,6272]{1,0:T(8,128)(2,1)S(1)} %get-tuple-element.23.refs_2_.refs_0_), channel_id=1, source_target_pairs={{0,2},{2,0},{1,3},{3,1},{4,6},{6,4},{5,7},{7,5},{8,10},{10,8},{9,1... | collective-permute-start | bytes 301064 | tf_op jit(solution)/shard_map/ppermute | solution.py:502
  13.6 0.7 collective-permute-done.2.refs_2_.refs_3_
  14.3 1.5 %collective-permute-start.6 = (bf16[8,6272]{1,0:T(8,128)(2,1)S(1)}, bf16[8,6272]{1,0:T(8,128)(2,1)S(1)}, u32[]{:S(2)}, u32[]{:S(2)}) collective-permute-start(bf16[8,6272]{1,0:T(8,128)(2,1)S(1)} %collective-permute-done.2.refs_2_.refs_3_), channel_id=1, source_target_pairs={{0,2},{2,0},{1,3},{3,1},{4,6},{6,4},{5,7},{7,5},{8,10},{10,8},{9,1... | collective-permute-start | bytes 301064 | tf_op jit(solution)/shard_map/ppermute | solution.py:502
  15.8 4.7 %shard_map.137 = (bf16[4,192,4096]{2,1,0:T(8,128)(2,1)S(1)}, bf16[4,192,4096]{2,1,0:T(8,128)(2,1)S(1)}) custom-call(bf16[16,192,4096]{2,1,0:T(8,128)(2,1)} %bitcast.24, bf16[16,192,4096]{2,1,0:T(8,128)(2,1)} %bitcast.27, bf16[8,6272]{1,0:T(8,128)(2,1)S(1)} %get-tuple-element.23.refs_2_.refs_0_), custom_call_target="tpu_custom_call" | custom-call | bytes 12582912 | tf_op jit(solution)/shard_map/pallas_call | solution.py:300
  20.5 0.9 %collective-permute-start.5 = (bf16[8,6272]{1,0:T(8,128)(2,1)S(1)}, bf16[8,6272]{1,0:T(8,128)(2,1)S(1)}, u32[]{:S(2)}, u32[]{:S(2)}) collective-permute-start(bf16[8,6272]{1,0:T(8,128)(2,1)S(1)} %collective-permute-done.1.refs_2_), channel_id=1, source_target_pairs={{0,2},{2,0},{1,3},{3,1},{4,6},{6,4},{5,7},{7,5},{8,10},{10,8},{9,1... | collective-permute-start | bytes 301064 | tf_op jit(solution)/shard_map/ppermute | solution.py:502
  21.5 1.2 %collective-permute-start.4 = (bf16[8,6272]{1,0:T(8,128)(2,1)S(1)}, bf16[8,6272]{1,0:T(8,128)(2,1)S(1)}, u32[]{:S(2)}, u32[]{:S(2)}) collective-permute-start(bf16[8,6272]{1,0:T(8,128)(2,1)S(1)} %collective-permute-done.refs_1_), channel_id=1, source_target_pairs={{0,2},{2,0},{1,3},{3,1},{4,6},{6,4},{5,7},{7,5},{8,10},{10,8},{9,1... | collective-permute-start | bytes 301064 | tf_op jit(solution)/shard_map/ppermute | solution.py:502
  22.6 0.5 collective-permute-start.10
  23.2 4.7 %shard_map.138 = (bf16[4,192,4096]{2,1,0:T(8,128)(2,1)S(1)}, bf16[4,192,4096]{2,1,0:T(8,128)(2,1)S(1)}) custom-call(bf16[16,192,4096]{2,1,0:T(8,128)(2,1)} %bitcast.25, bf16[16,192,4096]{2,1,0:T(8,128)(2,1)} %bitcast.28, bf16[8,6272]{1,0:T(8,128)(2,1)S(1)} %collective-permute-done.2.refs_2_.refs_3_), custom_call_target="tpu_custom_call" | custom-call | bytes 12582912 | tf_op jit(solution)/shard_map/pallas_call | solution.py:300
  27.9 0.5 collective-permute-start.8
  28.5 0.4 collective-permute-start.12
  29.0 0.4 collective-permute-start.14
  29.5 0.3 collective-permute-done.11.refs_12_
  29.9 0.4 collective-permute-done.13.refs_14_
  30.4 21.4 %shard_map.139 = (bf16[8,8,6144]{2,1,0:T(8,128)(2,1)S(1)}, bf16[8,8,6144]{2,1,0:T(8,128)(2,1)S(1)}, bf16[4,192,4096]{2,1,0:T(8,128)(2,1)S(1)}, bf16[4,192,4096]{...) custom-call(bf16[8,6272]{1,0:T(8,128)(2,1)S(1)} %get-tuple-element.2, ...), custom_call_target="tpu_custom_call", output_to_operand_aliasing={{2}: (16, {}), {3}: (17, {}), {4}: (18, {}), {5}: (19, {})} | custom-call | flops 14495514624 | bytes 50331648 | tf_op jit(solution)/shard_map/pallas_call | solution.py:442
  51.8 0.4 collective-permute-start.15
  52.3 1.9 %collective-permute-done.15 = bf16[8,8,6144]{2,1,0:T(8,128)(2,1)S(1)} collective-permute-done((bf16[8,8,6144]{2,1,0:T(8,128)(2,1)S(1)}, bf16[8,8,6144]{2,1,0:T(8,128)(2,1)S(1)}, u32[]{:S(2)}, u32[]{:S(2)}) %collective-permute-start.15) | collective-permute-done | bytes 786464 | tf_op jit(solution)/shard_map/ppermute | solution.py:509
  54.4 1.8 %collective-permute-start.20 = (bf16[8,2560]{1,0:T(8,128)(2,1)S(1)}, bf16[8,2560]{1,0:T(8,128)(2,1)S(1)}, u32[]{:S(2)}, u32[]{:S(2)}) collective-permute-start(bf16[8,2560]{1,0:T(8,128)(2,1)S(1)} %get-tuple-element.39), channel_id=1, source_target_pairs={{0,8},{4,12},{8,0},{12,4},{1,9},{5,13},{9,1},{13,5},{2,10},{6,14},... | collective-permute-start | bytes 122888 | tf_op jit(solution)/shard_map/ppermute | solution.py:514
  56.1 3.2 %collective-permute-start.22 = (bf16[8,2560]{1,0:T(8,128)(2,1)S(1)}, bf16[8,2560]{1,0:T(8,128)(2,1)S(1)}, u32[]{:S(2)}, u32[]{:S(2)}) collective-permute-start(bf16[8,2560]{1,0:T(8,128)(2,1)S(1)} %get-tuple-element.40), channel_id=1, source_target_pairs={{0,4},{4,8},{8,12},{12,0},{1,5},{5,9},{9,13},{13,1},{2,6},{6,10},{... | collective-permute-start | bytes 122888 | tf_op jit(solution)/shard_map/ppermute | solution.py:514
  59.3 0.6 collective-permute-start.21
  60.0 1.5 %collective-permute-start.16 = (bf16[3,8,3584]{2,1,0:T(8,128)(2,1)S(1)}, bf16[3,8,3584]{2,1,0:T(8,128)(2,1)S(1)}, u32[]{:S(2)}, u32[]{:S(2)}) collective-permute-start(bf16[3,8,3584]{2,1,0:T(8,128)(2,1)S(1)} %slice.61), channel_id=1, source_target_pairs={{0,2},{2,0},{1,3},{3,1},{4,6},{6,4},{5,7},{7,5},{8,10},{10,8},{9,1... | collective-permute-start | bytes 516104 | tf_op jit(solution)/shard_map/ppermute | solution.py:512
  61.6 0.8 %collective-permute-done.22 = bf16[8,2560]{1,0:T(8,128)(2,1)S(1)} collective-permute-done((bf16[8,2560]{1,0:T(8,128)(2,1)S(1)}, bf16[8,2560]{1,0:T(8,128)(2,1)S(1)}, u32[]{:S(2)}, u32[]{:S(2)}) %collective-permute-start.22) | collective-permute-done | bytes 40992 | tf_op jit(solution)/shard_map/ppermute | solution.py:514
  62.4 1.0 %collective-permute-done.21 = bf16[8,2560]{1,0:T(8,128)(2,1)S(1)} collective-permute-done((bf16[8,2560]{1,0:T(8,128)(2,1)S(1)}, bf16[8,2560]{1,0:T(8,128)(2,1)S(1)}, u32[]{:S(2)}, u32[]{:S(2)}) %collective-permute-start.21) | collective-permute-done | bytes 40992 | tf_op jit(solution)/shard_map/ppermute | solution.py:514
  63.4 0.7 collective-permute-start.23
  64.1 2.4 %collective-permute-done.16 = bf16[3,8,3584]{2,1,0:T(8,128)(2,1)S(1)} collective-permute-done((bf16[3,8,3584]{2,1,0:T(8,128)(2,1)S(1)}, bf16[3,8,3584]{2,1,0:T(8,128)(2,1)S(1)}, u32[]{:S(2)}, u32[]{:S(2)}) %collective-permute-start.16) | collective-permute-done | bytes 172064 | tf_op jit(solution)/shard_map/ppermute | solution.py:512
  66.5 1.9 %collective-permute-start.19 = (bf16[8,6144]{1,0:T(8,128)(2,1)S(1)}, bf16[8,6144]{1,0:T(8,128)(2,1)S(1)}, u32[]{:S(2)}, u32[]{:S(2)}) collective-permute-start(bf16[8,6144]{1,0:T(8,128)(2,1)S(1)} %get-tuple-element.42), channel_id=1, source_target_pairs={{0,4},{4,8},{8,12},{12,0},{1,5},{5,9},{9,13},{13,1},{2,6},{6,10},{... | collective-permute-start | bytes 294920 | tf_op jit(solution)/shard_map/ppermute | solution.py:519
  68.4 2.6 %collective-permute-start.18 = (bf16[8,6144]{1,0:T(8,128)(2,1)S(1)}, bf16[8,6144]{1,0:T(8,128)(2,1)S(1)}, u32[]{:S(2)}, u32[]{:S(2)}) collective-permute-start(bf16[8,6144]{1,0:T(8,128)(2,1)S(1)} %get-tuple-element.44), channel_id=1, source_target_pairs={{0,12},{4,0},{8,4},{12,8},{1,13},{5,1},{9,5},{13,9},{2,14},{6,2},{... | collective-permute-start | bytes 294920 | tf_op jit(solution)/shard_map/ppermute | solution.py:519
  71.1 2.3 %collective-permute-done.19.refs_3_ = bf16[8,6144]{1,0:T(8,128)(2,1)S(1)} collective-permute-done((bf16[8,6144]{1,0:T(8,128)(2,1)S(1)}, bf16[8,6144]{1,0:T(8,128)(2,1)S(1)}, u32[]{:S(2)}, u32[]{:S(2)}) %collective-permute-start.19) | collective-permute-done | bytes 98336 | tf_op jit(solution)/shard_map/ppermute | solution.py:519
  73.4 2.9 %collective-permute-done.17.refs_1_ = bf16[8,6144]{1,0:T(8,128)(2,1)S(1)} collective-permute-done((bf16[8,6144]{1,0:T(8,128)(2,1)S(1)}, bf16[8,6144]{1,0:T(8,128)(2,1)S(1)}, u32[]{:S(2)}, u32[]{:S(2)}) %collective-permute-start.17) | collective-permute-done | bytes 98336 | tf_op jit(solution)/shard_map/ppermute | solution.py:519
  76.3 0.8 %shard_map.140 = bf16[6,2,4096]{2,1,0:T(2,128)(2,1)} custom-call(f32[6,2,4096]{2,1,0:T(2,128)S(1)} %get-tuple-element.22.mixed_ref, bf16[8,6144]{1,0:T(8,128)(2,1)S(1)} %slice_bitcast_fusion.refs_0_, bf16[8,6144]{1,0:T(8,128)(2,1)S(1)} %collective-permute-done.17.refs_1_, bf16[8,6144]{1,0:T(8,128)(2,1)S(1)} %collective-permute-done.18.refs_2_, ...), custom_call_target="tpu_custom_call" | custom-call | tf_op jit(solution)/shard_map/pallas_call | solution.py:524
  (31 shorter events, 0.9 us)
Async XLA Ops:
  6.0 8.3 %collective-permute-start.2 = (bf16[8,6272]{1,0:T(8,128)(2,1)S(1)}, bf16[8,6272]{1,0:T(8,128)(2,1)S(1)}, u32[]{:S(2)}, u32[]{:S(2)}) collective-permute-start(bf16[8,6272]{1,0:T(8,128)(2,1)S(1)} %get-tuple-element.23.refs_2_.refs_0_), channel_id=1, source_target_pairs={{0,12},{4,0},{8,4},{12,8},{1,13},{5,1},{9,5},{13,9},{2,14},{6,2},{... | collective-permute-start | bytes 301064 | tf_op jit(solution)/shard_map/ppermute | solution.py:498
  11.1 9.4 %collective-permute-start = (bf16[8,6272]{1,0:T(8,128)(2,1)S(1)}, bf16[8,6272]{1,0:T(8,128)(2,1)S(1)}, u32[]{:S(2)}, u32[]{:S(2)}) collective-permute-start(bf16[8,6272]{1,0:T(8,128)(2,1)S(1)} %get-tuple-element.23.refs_2_.refs_0_), channel_id=1, source_target_pairs={{0,8},{4,12},{8,0},{12,4},{1,9},{5,13},{9,1},{13,5},{2,10},{6,14},... | collective-permute-start | bytes 301064 | tf_op jit(solution)/shard_map/ppermute | solution.py:498
  11.1 9.5 %collective-permute-start.1 = (bf16[8,6272]{1,0:T(8,128)(2,1)S(1)}, bf16[8,6272]{1,0:T(8,128)(2,1)S(1)}, u32[]{:S(2)}, u32[]{:S(2)}) collective-permute-start(bf16[8,6272]{1,0:T(8,128)(2,1)S(1)} %get-tuple-element.23.refs_2_.refs_0_), channel_id=1, source_target_pairs={{0,4},{4,8},{8,12},{12,0},{1,5},{5,9},{9,13},{13,1},{2,6},{6,10},{... | collective-permute-start | bytes 301064 | tf_op jit(solution)/shard_map/ppermute | solution.py:498
  12.1 10.5 %collective-permute-start.3 = (bf16[8,6272]{1,0:T(8,128)(2,1)S(1)}, bf16[8,6272]{1,0:T(8,128)(2,1)S(1)}, u32[]{:S(2)}, u32[]{:S(2)}) collective-permute-start(bf16[8,6272]{1,0:T(8,128)(2,1)S(1)} %get-tuple-element.23.refs_2_.refs_0_), channel_id=1, source_target_pairs={{0,2},{2,0},{1,3},{3,1},{4,6},{6,4},{5,7},{7,5},{8,10},{10,8},{9,1... | collective-permute-start | bytes 301064 | tf_op jit(solution)/shard_map/ppermute | solution.py:502
  14.3 8.8 %collective-permute-start.6 = (bf16[8,6272]{1,0:T(8,128)(2,1)S(1)}, bf16[8,6272]{1,0:T(8,128)(2,1)S(1)}, u32[]{:S(2)}, u32[]{:S(2)}) collective-permute-start(bf16[8,6272]{1,0:T(8,128)(2,1)S(1)} %collective-permute-done.2.refs_2_.refs_3_), channel_id=1, source_target_pairs={{0,2},{2,0},{1,3},{3,1},{4,6},{6,4},{5,7},{7,5},{8,10},{10,8},{9,1... | collective-permute-start | bytes 301064 | tf_op jit(solution)/shard_map/ppermute | solution.py:502
  20.5 7.4 %collective-permute-start.5 = (bf16[8,6272]{1,0:T(8,128)(2,1)S(1)}, bf16[8,6272]{1,0:T(8,128)(2,1)S(1)}, u32[]{:S(2)}, u32[]{:S(2)}) collective-permute-start(bf16[8,6272]{1,0:T(8,128)(2,1)S(1)} %collective-permute-done.1.refs_2_), channel_id=1, source_target_pairs={{0,2},{2,0},{1,3},{3,1},{4,6},{6,4},{5,7},{7,5},{8,10},{10,8},{9,1... | collective-permute-start | bytes 301064 | tf_op jit(solution)/shard_map/ppermute | solution.py:502
  21.5 7.0 %collective-permute-start.4 = (bf16[8,6272]{1,0:T(8,128)(2,1)S(1)}, bf16[8,6272]{1,0:T(8,128)(2,1)S(1)}, u32[]{:S(2)}, u32[]{:S(2)}) collective-permute-start(bf16[8,6272]{1,0:T(8,128)(2,1)S(1)} %collective-permute-done.refs_1_), channel_id=1, source_target_pairs={{0,2},{2,0},{1,3},{3,1},{4,6},{6,4},{5,7},{7,5},{8,10},{10,8},{9,1... | collective-permute-start | bytes 301064 | tf_op jit(solution)/shard_map/ppermute | solution.py:502
  22.6 5.9 %collective-permute-start.7 = (bf16[8,6272]{1,0:T(8,128)(2,1)S(1)}, bf16[8,6272]{1,0:T(8,128)(2,1)S(1)}, u32[]{:S(2)}, u32[]{:S(2)}) collective-permute-start(bf16[8,6272]{1,0:T(8,128)(2,1)S(1)} %get-tuple-element.23.refs_2_.refs_0_), channel_id=1, source_target_pairs={{0,1},{1,0},{2,3},{3,2},{4,5},{5,4},{6,7},{7,6},{8,9},{9,8},{10,11... | collective-permute-start | bytes 301064 | tf_op jit(solution)/shard_map/ppermute | solution.py:507
  22.6 6.3 %collective-permute-start.10 = (bf16[8,6272]{1,0:T(8,128)(2,1)S(1)}, bf16[8,6272]{1,0:T(8,128)(2,1)S(1)}, u32[]{:S(2)}, u32[]{:S(2)}) collective-permute-start(bf16[8,6272]{1,0:T(8,128)(2,1)S(1)} %collective-permute-done.2.refs_2_.refs_3_), channel_id=1, source_target_pairs={{0,1},{1,0},{2,3},{3,2},{4,5},{5,4},{6,7},{7,6},{8,9},{9,8},{10,11... | collective-permute-start | bytes 301064 | tf_op jit(solution)/shard_map/ppermute | solution.py:507
  23.1 5.9 %collective-permute-start.9 = (bf16[8,6272]{1,0:T(8,128)(2,1)S(1)}, bf16[8,6272]{1,0:T(8,128)(2,1)S(1)}, u32[]{:S(2)}, u32[]{:S(2)}) collective-permute-start(bf16[8,6272]{1,0:T(8,128)(2,1)S(1)} %collective-permute-done.1.refs_2_), channel_id=1, source_target_pairs={{0,1},{1,0},{2,3},{3,2},{4,5},{5,4},{6,7},{7,6},{8,9},{9,8},{10,11... | collective-permute-start | bytes 301064 | tf_op jit(solution)/shard_map/ppermute | solution.py:507
  27.9 1.5 %collective-permute-start.8 = (bf16[8,6272]{1,0:T(8,128)(2,1)S(1)}, bf16[8,6272]{1,0:T(8,128)(2,1)S(1)}, u32[]{:S(2)}, u32[]{:S(2)}) collective-permute-start(bf16[8,6272]{1,0:T(8,128)(2,1)S(1)} %collective-permute-done.refs_1_), channel_id=1, source_target_pairs={{0,1},{1,0},{2,3},{3,2},{4,5},{5,4},{6,7},{7,6},{8,9},{9,8},{10,11... | collective-permute-start | bytes 301064 | tf_op jit(solution)/shard_map/ppermute | solution.py:507
  28.4 1.3 %collective-permute-start.11 = (bf16[8,6272]{1,0:T(8,128)(2,1)S(1)}, bf16[8,6272]{1,0:T(8,128)(2,1)S(1)}, u32[]{:S(2)}, u32[]{:S(2)}) collective-permute-start(bf16[8,6272]{1,0:T(8,128)(2,1)S(1)} %collective-permute-done.3.refs_4_), channel_id=1, source_target_pairs={{0,1},{1,0},{2,3},{3,2},{4,5},{5,4},{6,7},{7,6},{8,9},{9,8},{10,11... | collective-permute-start | bytes 301064 | tf_op jit(solution)/shard_map/ppermute | solution.py:507
  28.5 1.4 %collective-permute-start.12 = (bf16[8,6272]{1,0:T(8,128)(2,1)S(1)}, bf16[8,6272]{1,0:T(8,128)(2,1)S(1)}, u32[]{:S(2)}, u32[]{:S(2)}) collective-permute-start(bf16[8,6272]{1,0:T(8,128)(2,1)S(1)} %collective-permute-done.4.refs_5_), channel_id=1, source_target_pairs={{0,1},{1,0},{2,3},{3,2},{4,5},{5,4},{6,7},{7,6},{8,9},{9,8},{10,11... | collective-permute-start | bytes 301064 | tf_op jit(solution)/shard_map/ppermute | solution.py:507
  28.9 1.3 %collective-permute-start.13 = (bf16[8,6272]{1,0:T(8,128)(2,1)S(1)}, bf16[8,6272]{1,0:T(8,128)(2,1)S(1)}, u32[]{:S(2)}, u32[]{:S(2)}) collective-permute-start(bf16[8,6272]{1,0:T(8,128)(2,1)S(1)} %collective-permute-done.5.refs_6_), channel_id=1, source_target_pairs={{0,1},{1,0},{2,3},{3,2},{4,5},{5,4},{6,7},{7,6},{8,9},{9,8},{10,11... | collective-permute-start | bytes 301064 | tf_op jit(solution)/shard_map/ppermute | solution.py:507
  29.0 1.4 %collective-permute-start.14 = (bf16[8,6272]{1,0:T(8,128)(2,1)S(1)}, bf16[8,6272]{1,0:T(8,128)(2,1)S(1)}, u32[]{:S(2)}, u32[]{:S(2)}) collective-permute-start(bf16[8,6272]{1,0:T(8,128)(2,1)S(1)} %collective-permute-done.6.refs_7_), channel_id=1, source_target_pairs={{0,1},{1,0},{2,3},{3,2},{4,5},{5,4},{6,7},{7,6},{8,9},{9,8},{10,11... | collective-permute-start | bytes 301064 | tf_op jit(solution)/shard_map/ppermute | solution.py:507
  51.8 2.4 %collective-permute-start.15 = (bf16[8,8,6144]{2,1,0:T(8,128)(2,1)S(1)}, bf16[8,8,6144]{2,1,0:T(8,128)(2,1)S(1)}, u32[]{:S(2)}, u32[]{:S(2)}) collective-permute-start(bf16[8,8,6144]{2,1,0:T(8,128)(2,1)S(1)} %get-tuple-element.38), channel_id=1, source_target_pairs={{0,1},{1,0},{2,3},{3,2},{4,5},{5,4},{6,7},{7,6},{8,9},{9,8},{10,11... | collective-permute-start | bytes 2359304 | tf_op jit(solution)/shard_map/ppermute | solution.py:509
  54.4 7.2 %collective-permute-start.20 = (bf16[8,2560]{1,0:T(8,128)(2,1)S(1)}, bf16[8,2560]{1,0:T(8,128)(2,1)S(1)}, u32[]{:S(2)}, u32[]{:S(2)}) collective-permute-start(bf16[8,2560]{1,0:T(8,128)(2,1)S(1)} %get-tuple-element.39), channel_id=1, source_target_pairs={{0,8},{4,12},{8,0},{12,4},{1,9},{5,13},{9,1},{13,5},{2,10},{6,14},... | collective-permute-start | bytes 122888 | tf_op jit(solution)/shard_map/ppermute | solution.py:514
  56.1 6.2 %collective-permute-start.22 = (bf16[8,2560]{1,0:T(8,128)(2,1)S(1)}, bf16[8,2560]{1,0:T(8,128)(2,1)S(1)}, u32[]{:S(2)}, u32[]{:S(2)}) collective-permute-start(bf16[8,2560]{1,0:T(8,128)(2,1)S(1)} %get-tuple-element.40), channel_id=1, source_target_pairs={{0,4},{4,8},{8,12},{12,0},{1,5},{5,9},{9,13},{13,1},{2,6},{6,10},{... | collective-permute-start | bytes 122888 | tf_op jit(solution)/shard_map/ppermute | solution.py:514
  59.3 4.0 %collective-permute-start.21 = (bf16[8,2560]{1,0:T(8,128)(2,1)S(1)}, bf16[8,2560]{1,0:T(8,128)(2,1)S(1)}, u32[]{:S(2)}, u32[]{:S(2)}) collective-permute-start(bf16[8,2560]{1,0:T(8,128)(2,1)S(1)} %get-tuple-element.41), channel_id=1, source_target_pairs={{0,12},{4,0},{8,4},{12,8},{1,13},{5,1},{9,5},{13,9},{2,14},{6,2},{... | collective-permute-start | bytes 122888 | tf_op jit(solution)/shard_map/ppermute | solution.py:514
  60.0 6.4 %collective-permute-start.16 = (bf16[3,8,3584]{2,1,0:T(8,128)(2,1)S(1)}, bf16[3,8,3584]{2,1,0:T(8,128)(2,1)S(1)}, u32[]{:S(2)}, u32[]{:S(2)}) collective-permute-start(bf16[3,8,3584]{2,1,0:T(8,128)(2,1)S(1)} %slice.61), channel_id=1, source_target_pairs={{0,2},{2,0},{1,3},{3,1},{4,6},{6,4},{5,7},{7,5},{8,10},{10,8},{9,1... | collective-permute-start | bytes 516104 | tf_op jit(solution)/shard_map/ppermute | solution.py:512
  63.4 7.7 %collective-permute-start.23 = (bf16[8,6144]{1,0:T(8,128)(2,1)S(1)}, bf16[8,6144]{1,0:T(8,128)(2,1)S(1)}, u32[]{:S(2)}, u32[]{:S(2)}) collective-permute-start(bf16[8,6144]{1,0:T(8,128)(2,1)S(1)} %pad_maximum_fusion.1), channel_id=1, source_target_pairs={{0,2},{2,0},{1,3},{3,1},{4,6},{6,4},{5,7},{7,5},{8,10},{10,8},{9,1... | collective-permute-start | bytes 294920 | tf_op jit(solution)/shard_map/ppermute | solution.py:523
  66.5 6.9 %collective-permute-start.19 = (bf16[8,6144]{1,0:T(8,128)(2,1)S(1)}, bf16[8,6144]{1,0:T(8,128)(2,1)S(1)}, u32[]{:S(2)}, u32[]{:S(2)}) collective-permute-start(bf16[8,6144]{1,0:T(8,128)(2,1)S(1)} %get-tuple-element.42), channel_id=1, source_target_pairs={{0,4},{4,8},{8,12},{12,0},{1,5},{5,9},{9,13},{13,1},{2,6},{6,10},{... | collective-permute-start | bytes 294920 | tf_op jit(solution)/shard_map/ppermute | solution.py:519
  68.4 7.9 %collective-permute-start.17 = (bf16[8,6144]{1,0:T(8,128)(2,1)S(1)}, bf16[8,6144]{1,0:T(8,128)(2,1)S(1)}, u32[]{:S(2)}, u32[]{:S(2)}) collective-permute-start(bf16[8,6144]{1,0:T(8,128)(2,1)S(1)} %get-tuple-element.43), channel_id=1, source_target_pairs={{0,8},{4,12},{8,0},{12,4},{1,9},{5,13},{9,1},{13,5},{2,10},{6,14},... | collective-permute-start | bytes 294920 | tf_op jit(solution)/shard_map/ppermute | solution.py:519
  68.4 7.9 %collective-permute-start.18 = (bf16[8,6144]{1,0:T(8,128)(2,1)S(1)}, bf16[8,6144]{1,0:T(8,128)(2,1)S(1)}, u32[]{:S(2)}, u32[]{:S(2)}) collective-permute-start(bf16[8,6144]{1,0:T(8,128)(2,1)S(1)} %get-tuple-element.44), channel_id=1, source_target_pairs={{0,12},{4,0},{8,4},{12,8},{1,13},{5,1},{9,5},{13,9},{2,14},{6,2},{... | collective-permute-start | bytes 294920 | tf_op jit(solution)/shard_map/ppermute | solution.py:519

commit v5 on v4

--- a/solution.py
+++ b/solution.py
@@ -275,7 +275,7 @@
       norm_gain, routes, route_gains)
 
 
-SPLIT = 3584
+SPLIT = 3072
 GROUP = 4
 CUT = 512
 

time: 77.3 us -> 76.2 us (0.986)
  waiting for transfers between devices: 13.1 us -> 12.2 us
    ppermute x3, waiting for transfers between devices: 1.79 us -> 4.22 us  [gathered(): lax.ppermute(other[i + 1, :, SPLIT:], 'expert', back[k])]
    ppermute x1, waiting for transfers between devices: 2.39 us -> 0.13 us  [gathered(): peer = lax.ppermute(other[1:, :, :SPLIT], 'dp', side)]
    ppermute x3, starting transfers between devices: 4.55 us -> 5.9 us  [gathered(): lax.ppermute(own_line[i], 'expert', back[k])]
    ppermute x3, waiting for transfers between devices: 5.24 us -> 4.26 us  [gathered(): lax.ppermute(own_line[i], 'expert', back[k])]
    ppermute x1, starting transfers between devices: 1.55 us -> 0.59 us  [gathered(): peer = lax.ppermute(other[1:, :, :SPLIT], 'dp', side)]
where the time goes in v5:
time: 76.2 us; the launch traced here: 76 us
  Pallas kernels  37.6 us (49%)
  starting transfers between devices  25.8 us (34%)
  waiting for transfers between devices  12.2 us (16%)
    pallas_call x1, Pallas kernels, experts(): pl.pallas_call(functools.partial(experts_kernel, blocks, axis), out_shape...  21.4 us
    pallas_call x2, Pallas kernels, fetch(): pl.pallas_call(functools.partial(fetch_kernel, len(weights), start), out_...  9.4 us
    ppermute x3, starting transfers between devices, gathered(): line = [pay] + [lax.ppermute(pay, 'expert', ahead[k]) for k in shifts]  6.11 us
    pallas_call x1, Pallas kernels, front(): pl.pallas_call(front_kernel, out_shape=(pltpu.VMEM((MAIN, width + width /...  5.95 us
    ppermute x3, starting transfers between devices, gathered(): lax.ppermute(own_line[i], 'expert', back[k])  5.9 us
    ppermute x4, starting transfers between devices, gathered(): pays = line + [lax.ppermute(p, 'dp', side) for p in line]  5.07 us
    ppermute x3, starting transfers between devices, gathered(): lax.ppermute(other[i + 1, :, SPLIT:], 'expert', back[k])  4.94 us
    ppermute x3, waiting for transfers between devices, gathered(): lax.ppermute(own_line[i], 'expert', back[k])  4.26 us
  transfers between devices with their start and end apart: 24, of which 11 were waited for; matrix products, arithmetic and copies ran while one was open for 0% of the time, Pallas kernels for 12%

profile of v5, /device:TPU:0, one launch (start us, length us, event | category | flops | bytes accessed | tf_op | source)
XLA Modules:
  0.0 76.0 jit_solution(10743845441682175784)
XLA Ops:
  0.0 5.9 %shard_map.136 = (bf16[8,6272]{1,0:T(8,128)(2,1)S(1)}, f32[6,2,4096]{2,1,0:T(2,128)S(1)}) custom-call(bf16[6,2,4096]{2,1,0:T(2,128)(2,1)} %q_ref.1, bf16[6,2,256]{2,1,0:T(2,128)(2,1)} %nk_ref.1, bf16[6,2,256]{2,1,0:T(2,128)(2,1)} %nv_ref.1, bf16[6,32,256]{2,1,0:T(8,128)(2,1)} %ck_ref.1, bf16[6,32,256]{2,1,0:T(8,128)(2,1)} %cv_ref.1, s32[6]{0:T(128)} %len_ref.1, ...), custom_call_target="tpu_custom_call" | custom-call | flops 10000000 | bytes 1000000 | tf_op jit(solution)/shard_map/pallas_call | solution.py:265
  6.0 5.1 %collective-permute-start.2 = (bf16[8,6272]{1,0:T(8,128)(2,1)S(1)}, bf16[8,6272]{1,0:T(8,128)(2,1)S(1)}, u32[]{:S(2)}, u32[]{:S(2)}) collective-permute-start(bf16[8,6272]{1,0:T(8,128)(2,1)S(1)} %get-tuple-element.23.refs_2_.refs_0_), channel_id=1, source_target_pairs={{0,12},{4,0},{8,4},{12,8},{1,13},{5,1},{9,5},{13,9},{2,14},{6,2},{... | collective-permute-start | bytes 301064 | tf_op jit(solution)/shard_map/ppermute | solution.py:498
  11.1 1.0 %collective-permute-start.1 = (bf16[8,6272]{1,0:T(8,128)(2,1)S(1)}, bf16[8,6272]{1,0:T(8,128)(2,1)S(1)}, u32[]{:S(2)}, u32[]{:S(2)}) collective-permute-start(bf16[8,6272]{1,0:T(8,128)(2,1)S(1)} %get-tuple-element.23.refs_2_.refs_0_), channel_id=1, source_target_pairs={{0,4},{4,8},{8,12},{12,0},{1,5},{5,9},{9,13},{13,1},{2,6},{6,10},{... | collective-permute-start | bytes 301064 | tf_op jit(solution)/shard_map/ppermute | solution.py:498
  12.1 1.5 %collective-permute-start.3 = (bf16[8,6272]{1,0:T(8,128)(2,1)S(1)}, bf16[8,6272]{1,0:T(8,128)(2,1)S(1)}, u32[]{:S(2)}, u32[]{:S(2)}) collective-permute-start(bf16[8,6272]{1,0:T(8,128)(2,1)S(1)} %get-tuple-element.23.refs_2_.refs_0_), channel_id=1, source_target_pairs={{0,2},{2,0},{1,3},{3,1},{4,6},{6,4},{5,7},{7,5},{8,10},{10,8},{9,1... | collective-permute-start | bytes 301064 | tf_op jit(solution)/shard_map/ppermute | solution.py:502
  13.6 0.7 collective-permute-done.2.refs_2_.refs_3_
  14.3 1.5 %collective-permute-start.6 = (bf16[8,6272]{1,0:T(8,128)(2,1)S(1)}, bf16[8,6272]{1,0:T(8,128)(2,1)S(1)}, u32[]{:S(2)}, u32[]{:S(2)}) collective-permute-start(bf16[8,6272]{1,0:T(8,128)(2,1)S(1)} %collective-permute-done.2.refs_2_.refs_3_), channel_id=1, source_target_pairs={{0,2},{2,0},{1,3},{3,1},{4,6},{6,4},{5,7},{7,5},{8,10},{10,8},{9,1... | collective-permute-start | bytes 301064 | tf_op jit(solution)/shard_map/ppermute | solution.py:502
  15.8 4.7 %shard_map.137 = (bf16[4,192,4096]{2,1,0:T(8,128)(2,1)S(1)}, bf16[4,192,4096]{2,1,0:T(8,128)(2,1)S(1)}) custom-call(bf16[16,192,4096]{2,1,0:T(8,128)(2,1)} %bitcast.24, bf16[16,192,4096]{2,1,0:T(8,128)(2,1)} %bitcast.27, bf16[8,6272]{1,0:T(8,128)(2,1)S(1)} %get-tuple-element.23.refs_2_.refs_0_), custom_call_target="tpu_custom_call" | custom-call | bytes 12582912 | tf_op jit(solution)/shard_map/pallas_call | solution.py:300
  20.5 0.9 %collective-permute-start.5 = (bf16[8,6272]{1,0:T(8,128)(2,1)S(1)}, bf16[8,6272]{1,0:T(8,128)(2,1)S(1)}, u32[]{:S(2)}, u32[]{:S(2)}) collective-permute-start(bf16[8,6272]{1,0:T(8,128)(2,1)S(1)} %collective-permute-done.1.refs_2_), channel_id=1, source_target_pairs={{0,2},{2,0},{1,3},{3,1},{4,6},{6,4},{5,7},{7,5},{8,10},{10,8},{9,1... | collective-permute-start | bytes 301064 | tf_op jit(solution)/shard_map/ppermute | solution.py:502
  21.5 1.2 %collective-permute-start.4 = (bf16[8,6272]{1,0:T(8,128)(2,1)S(1)}, bf16[8,6272]{1,0:T(8,128)(2,1)S(1)}, u32[]{:S(2)}, u32[]{:S(2)}) collective-permute-start(bf16[8,6272]{1,0:T(8,128)(2,1)S(1)} %collective-permute-done.refs_1_), channel_id=1, source_target_pairs={{0,2},{2,0},{1,3},{3,1},{4,6},{6,4},{5,7},{7,5},{8,10},{10,8},{9,1... | collective-permute-start | bytes 301064 | tf_op jit(solution)/shard_map/ppermute | solution.py:502
  22.6 0.5 collective-permute-start.10
  23.2 4.7 %shard_map.138 = (bf16[4,192,4096]{2,1,0:T(8,128)(2,1)S(1)}, bf16[4,192,4096]{2,1,0:T(8,128)(2,1)S(1)}) custom-call(bf16[16,192,4096]{2,1,0:T(8,128)(2,1)} %bitcast.25, bf16[16,192,4096]{2,1,0:T(8,128)(2,1)} %bitcast.28, bf16[8,6272]{1,0:T(8,128)(2,1)S(1)} %collective-permute-done.2.refs_2_.refs_3_), custom_call_target="tpu_custom_call" | custom-call | bytes 12582912 | tf_op jit(solution)/shard_map/pallas_call | solution.py:300
  27.9 0.5 collective-permute-start.8
  28.5 0.4 collective-permute-start.12
  29.0 0.4 collective-permute-start.14
  29.5 0.3 collective-permute-done.11.refs_12_
  29.9 0.4 collective-permute-done.13.refs_14_
  30.4 21.4 %shard_map.139 = (bf16[8,8,6144]{2,1,0:T(8,128)(2,1)S(1)}, bf16[8,8,6144]{2,1,0:T(8,128)(2,1)S(1)}, bf16[4,192,4096]{2,1,0:T(8,128)(2,1)S(1)}, bf16[4,192,4096]{...) custom-call(bf16[8,6272]{1,0:T(8,128)(2,1)S(1)} %get-tuple-element.2, ...), custom_call_target="tpu_custom_call", output_to_operand_aliasing={{2}: (16, {}), {3}: (17, {}), {4}: (18, {}), {5}: (19, {})} | custom-call | flops 14495514624 | bytes 50331648 | tf_op jit(solution)/shard_map/pallas_call | solution.py:442
  51.8 0.4 collective-permute-start.15
  52.3 1.9 %collective-permute-done.15 = bf16[8,8,6144]{2,1,0:T(8,128)(2,1)S(1)} collective-permute-done((bf16[8,8,6144]{2,1,0:T(8,128)(2,1)S(1)}, bf16[8,8,6144]{2,1,0:T(8,128)(2,1)S(1)}, u32[]{:S(2)}, u32[]{:S(2)}) %collective-permute-start.15) | collective-permute-done | bytes 786464 | tf_op jit(solution)/shard_map/ppermute | solution.py:509
  54.4 0.9 %collective-permute-start.22 = (bf16[8,3072]{1,0:T(8,128)(2,1)S(1)}, bf16[8,3072]{1,0:T(8,128)(2,1)S(1)}, u32[]{:S(2)}, u32[]{:S(2)}) collective-permute-start(bf16[8,3072]{1,0:T(8,128)(2,1)S(1)} %get-tuple-element.40), channel_id=1, source_target_pairs={{0,4},{4,8},{8,12},{12,0},{1,5},{5,9},{9,13},{13,1},{2,6},{6,10},{... | collective-permute-start | bytes 147464 | tf_op jit(solution)/shard_map/ppermute | solution.py:514
  55.2 3.6 %collective-permute-start.21 = (bf16[8,3072]{1,0:T(8,128)(2,1)S(1)}, bf16[8,3072]{1,0:T(8,128)(2,1)S(1)}, u32[]{:S(2)}, u32[]{:S(2)}) collective-permute-start(bf16[8,3072]{1,0:T(8,128)(2,1)S(1)} %get-tuple-element.41), channel_id=1, source_target_pairs={{0,12},{4,0},{8,4},{12,8},{1,13},{5,1},{9,5},{13,9},{2,14},{6,2},{... | collective-permute-start | bytes 147464 | tf_op jit(solution)/shard_map/ppermute | solution.py:514
  58.8 0.5 collective-permute-start.20
  59.4 0.6 collective-permute-start.16
  60.0 1.1 %collective-permute-done.22 = bf16[8,3072]{1,0:T(8,128)(2,1)S(1)} collective-permute-done((bf16[8,3072]{1,0:T(8,128)(2,1)S(1)}, bf16[8,3072]{1,0:T(8,128)(2,1)S(1)}, u32[]{:S(2)}, u32[]{:S(2)}) %collective-permute-start.22) | collective-permute-done | bytes 49184 | tf_op jit(solution)/shard_map/ppermute | solution.py:514
  61.1 3.1 %collective-permute-done.20 = bf16[8,3072]{1,0:T(8,128)(2,1)S(1)} collective-permute-done((bf16[8,3072]{1,0:T(8,128)(2,1)S(1)}, bf16[8,3072]{1,0:T(8,128)(2,1)S(1)}, u32[]{:S(2)}, u32[]{:S(2)}) %collective-permute-start.20) | collective-permute-done | bytes 49184 | tf_op jit(solution)/shard_map/ppermute | solution.py:514
  64.2 0.6 collective-permute-start.23
  65.0 1.8 %collective-permute-start.19 = (bf16[8,6144]{1,0:T(8,128)(2,1)S(1)}, bf16[8,6144]{1,0:T(8,128)(2,1)S(1)}, u32[]{:S(2)}, u32[]{:S(2)}) collective-permute-start(bf16[8,6144]{1,0:T(8,128)(2,1)S(1)} %get-tuple-element.45), channel_id=1, source_target_pairs={{0,4},{4,8},{8,12},{12,0},{1,5},{5,9},{9,13},{13,1},{2,6},{6,10},{... | collective-permute-start | bytes 294920 | tf_op jit(solution)/shard_map/ppermute | solution.py:519
  66.8 1.3 %collective-permute-start.17 = (bf16[8,6144]{1,0:T(8,128)(2,1)S(1)}, bf16[8,6144]{1,0:T(8,128)(2,1)S(1)}, u32[]{:S(2)}, u32[]{:S(2)}) collective-permute-start(bf16[8,6144]{1,0:T(8,128)(2,1)S(1)} %get-tuple-element.46), channel_id=1, source_target_pairs={{0,8},{4,12},{8,0},{12,4},{1,9},{5,13},{9,1},{13,5},{2,10},{6,14},... | collective-permute-start | bytes 294920 | tf_op jit(solution)/shard_map/ppermute | solution.py:519
  68.1 2.8 %collective-permute-start.18 = (bf16[8,6144]{1,0:T(8,128)(2,1)S(1)}, bf16[8,6144]{1,0:T(8,128)(2,1)S(1)}, u32[]{:S(2)}, u32[]{:S(2)}) collective-permute-start(bf16[8,6144]{1,0:T(8,128)(2,1)S(1)} %get-tuple-element.47), channel_id=1, source_target_pairs={{0,12},{4,0},{8,4},{12,8},{1,13},{5,1},{9,5},{13,9},{2,14},{6,2},{... | collective-permute-start | bytes 294920 | tf_op jit(solution)/shard_map/ppermute | solution.py:519
  70.9 1.8 %collective-permute-done.19.refs_3_ = bf16[8,6144]{1,0:T(8,128)(2,1)S(1)} collective-permute-done((bf16[8,6144]{1,0:T(8,128)(2,1)S(1)}, bf16[8,6144]{1,0:T(8,128)(2,1)S(1)}, u32[]{:S(2)}, u32[]{:S(2)}) %collective-permute-start.19) | collective-permute-done | bytes 98336 | tf_op jit(solution)/shard_map/ppermute | solution.py:519
  72.7 2.5 %collective-permute-done.17.refs_1_ = bf16[8,6144]{1,0:T(8,128)(2,1)S(1)} collective-permute-done((bf16[8,6144]{1,0:T(8,128)(2,1)S(1)}, bf16[8,6144]{1,0:T(8,128)(2,1)S(1)}, u32[]{:S(2)}, u32[]{:S(2)}) %collective-permute-start.17) | collective-permute-done | bytes 98336 | tf_op jit(solution)/shard_map/ppermute | solution.py:519
  75.2 0.8 %shard_map.140 = bf16[6,2,4096]{2,1,0:T(2,128)(2,1)} custom-call(f32[6,2,4096]{2,1,0:T(2,128)S(1)} %get-tuple-element.22.mixed_ref, bf16[8,6144]{1,0:T(8,128)(2,1)S(1)} %slice_bitcast_fusion.refs_0_, bf16[8,6144]{1,0:T(8,128)(2,1)S(1)} %collective-permute-done.17.refs_1_, bf16[8,6144]{1,0:T(8,128)(2,1)S(1)} %collective-permute-done.18.refs_2_, ...), custom_call_target="tpu_custom_call" | custom-call | tf_op jit(solution)/shard_map/pallas_call | solution.py:524
  (29 shorter events, 1.0 us)
Async XLA Ops:
  6.0 8.3 %collective-permute-start.2 = (bf16[8,6272]{1,0:T(8,128)(2,1)S(1)}, bf16[8,6272]{1,0:T(8,128)(2,1)S(1)}, u32[]{:S(2)}, u32[]{:S(2)}) collective-permute-start(bf16[8,6272]{1,0:T(8,128)(2,1)S(1)} %get-tuple-element.23.refs_2_.refs_0_), channel_id=1, source_target_pairs={{0,12},{4,0},{8,4},{12,8},{1,13},{5,1},{9,5},{13,9},{2,14},{6,2},{... | collective-permute-start | bytes 301064 | tf_op jit(solution)/shard_map/ppermute | solution.py:498
  11.1 9.4 %collective-permute-start = (bf16[8,6272]{1,0:T(8,128)(2,1)S(1)}, bf16[8,6272]{1,0:T(8,128)(2,1)S(1)}, u32[]{:S(2)}, u32[]{:S(2)}) collective-permute-start(bf16[8,6272]{1,0:T(8,128)(2,1)S(1)} %get-tuple-element.23.refs_2_.refs_0_), channel_id=1, source_target_pairs={{0,8},{4,12},{8,0},{12,4},{1,9},{5,13},{9,1},{13,5},{2,10},{6,14},... | collective-permute-start | bytes 301064 | tf_op jit(solution)/shard_map/ppermute | solution.py:498
  11.1 9.5 %collective-permute-start.1 = (bf16[8,6272]{1,0:T(8,128)(2,1)S(1)}, bf16[8,6272]{1,0:T(8,128)(2,1)S(1)}, u32[]{:S(2)}, u32[]{:S(2)}) collective-permute-start(bf16[8,6272]{1,0:T(8,128)(2,1)S(1)} %get-tuple-element.23.refs_2_.refs_0_), channel_id=1, source_target_pairs={{0,4},{4,8},{8,12},{12,0},{1,5},{5,9},{9,13},{13,1},{2,6},{6,10},{... | collective-permute-start | bytes 301064 | tf_op jit(solution)/shard_map/ppermute | solution.py:498
  12.1 10.5 %collective-permute-start.3 = (bf16[8,6272]{1,0:T(8,128)(2,1)S(1)}, bf16[8,6272]{1,0:T(8,128)(2,1)S(1)}, u32[]{:S(2)}, u32[]{:S(2)}) collective-permute-start(bf16[8,6272]{1,0:T(8,128)(2,1)S(1)} %get-tuple-element.23.refs_2_.refs_0_), channel_id=1, source_target_pairs={{0,2},{2,0},{1,3},{3,1},{4,6},{6,4},{5,7},{7,5},{8,10},{10,8},{9,1... | collective-permute-start | bytes 301064 | tf_op jit(solution)/shard_map/ppermute | solution.py:502
  14.3 8.8 %collective-permute-start.6 = (bf16[8,6272]{1,0:T(8,128)(2,1)S(1)}, bf16[8,6272]{1,0:T(8,128)(2,1)S(1)}, u32[]{:S(2)}, u32[]{:S(2)}) collective-permute-start(bf16[8,6272]{1,0:T(8,128)(2,1)S(1)} %collective-permute-done.2.refs_2_.refs_3_), channel_id=1, source_target_pairs={{0,2},{2,0},{1,3},{3,1},{4,6},{6,4},{5,7},{7,5},{8,10},{10,8},{9,1... | collective-permute-start | bytes 301064 | tf_op jit(solution)/shard_map/ppermute | solution.py:502
  20.5 7.4 %collective-permute-start.5 = (bf16[8,6272]{1,0:T(8,128)(2,1)S(1)}, bf16[8,6272]{1,0:T(8,128)(2,1)S(1)}, u32[]{:S(2)}, u32[]{:S(2)}) collective-permute-start(bf16[8,6272]{1,0:T(8,128)(2,1)S(1)} %collective-permute-done.1.refs_2_), channel_id=1, source_target_pairs={{0,2},{2,0},{1,3},{3,1},{4,6},{6,4},{5,7},{7,5},{8,10},{10,8},{9,1... | collective-permute-start | bytes 301064 | tf_op jit(solution)/shard_map/ppermute | solution.py:502
  21.5 7.0 %collective-permute-start.4 = (bf16[8,6272]{1,0:T(8,128)(2,1)S(1)}, bf16[8,6272]{1,0:T(8,128)(2,1)S(1)}, u32[]{:S(2)}, u32[]{:S(2)}) collective-permute-start(bf16[8,6272]{1,0:T(8,128)(2,1)S(1)} %collective-permute-done.refs_1_), channel_id=1, source_target_pairs={{0,2},{2,0},{1,3},{3,1},{4,6},{6,4},{5,7},{7,5},{8,10},{10,8},{9,1... | collective-permute-start | bytes 301064 | tf_op jit(solution)/shard_map/ppermute | solution.py:502
  22.6 5.9 %collective-permute-start.7 = (bf16[8,6272]{1,0:T(8,128)(2,1)S(1)}, bf16[8,6272]{1,0:T(8,128)(2,1)S(1)}, u32[]{:S(2)}, u32[]{:S(2)}) collective-permute-start(bf16[8,6272]{1,0:T(8,128)(2,1)S(1)} %get-tuple-element.23.refs_2_.refs_0_), channel_id=1, source_target_pairs={{0,1},{1,0},{2,3},{3,2},{4,5},{5,4},{6,7},{7,6},{8,9},{9,8},{10,11... | collective-permute-start | bytes 301064 | tf_op jit(solution)/shard_map/ppermute | solution.py:507
  22.6 6.3 %collective-permute-start.10 = (bf16[8,6272]{1,0:T(8,128)(2,1)S(1)}, bf16[8,6272]{1,0:T(8,128)(2,1)S(1)}, u32[]{:S(2)}, u32[]{:S(2)}) collective-permute-start(bf16[8,6272]{1,0:T(8,128)(2,1)S(1)} %collective-permute-done.2.refs_2_.refs_3_), channel_id=1, source_target_pairs={{0,1},{1,0},{2,3},{3,2},{4,5},{5,4},{6,7},{7,6},{8,9},{9,8},{10,11... | collective-permute-start | bytes 301064 | tf_op jit(solution)/shard_map/ppermute | solution.py:507
  23.1 5.9 %collective-permute-start.9 = (bf16[8,6272]{1,0:T(8,128)(2,1)S(1)}, bf16[8,6272]{1,0:T(8,128)(2,1)S(1)}, u32[]{:S(2)}, u32[]{:S(2)}) collective-permute-start(bf16[8,6272]{1,0:T(8,128)(2,1)S(1)} %collective-permute-done.1.refs_2_), channel_id=1, source_target_pairs={{0,1},{1,0},{2,3},{3,2},{4,5},{5,4},{6,7},{7,6},{8,9},{9,8},{10,11... | collective-permute-start | bytes 301064 | tf_op jit(solution)/shard_map/ppermute | solution.py:507
  27.9 1.5 %collective-permute-start.8 = (bf16[8,6272]{1,0:T(8,128)(2,1)S(1)}, bf16[8,6272]{1,0:T(8,128)(2,1)S(1)}, u32[]{:S(2)}, u32[]{:S(2)}) collective-permute-start(bf16[8,6272]{1,0:T(8,128)(2,1)S(1)} %collective-permute-done.refs_1_), channel_id=1, source_target_pairs={{0,1},{1,0},{2,3},{3,2},{4,5},{5,4},{6,7},{7,6},{8,9},{9,8},{10,11... | collective-permute-start | bytes 301064 | tf_op jit(solution)/shard_map/ppermute | solution.py:507
  28.4 1.3 %collective-permute-start.11 = (bf16[8,6272]{1,0:T(8,128)(2,1)S(1)}, bf16[8,6272]{1,0:T(8,128)(2,1)S(1)}, u32[]{:S(2)}, u32[]{:S(2)}) collective-permute-start(bf16[8,6272]{1,0:T(8,128)(2,1)S(1)} %collective-permute-done.3.refs_4_), channel_id=1, source_target_pairs={{0,1},{1,0},{2,3},{3,2},{4,5},{5,4},{6,7},{7,6},{8,9},{9,8},{10,11... | collective-permute-start | bytes 301064 | tf_op jit(solution)/shard_map/ppermute | solution.py:507
  28.5 1.4 %collective-permute-start.12 = (bf16[8,6272]{1,0:T(8,128)(2,1)S(1)}, bf16[8,6272]{1,0:T(8,128)(2,1)S(1)}, u32[]{:S(2)}, u32[]{:S(2)}) collective-permute-start(bf16[8,6272]{1,0:T(8,128)(2,1)S(1)} %collective-permute-done.4.refs_5_), channel_id=1, source_target_pairs={{0,1},{1,0},{2,3},{3,2},{4,5},{5,4},{6,7},{7,6},{8,9},{9,8},{10,11... | collective-permute-start | bytes 301064 | tf_op jit(solution)/shard_map/ppermute | solution.py:507
  28.9 1.3 %collective-permute-start.13 = (bf16[8,6272]{1,0:T(8,128)(2,1)S(1)}, bf16[8,6272]{1,0:T(8,128)(2,1)S(1)}, u32[]{:S(2)}, u32[]{:S(2)}) collective-permute-start(bf16[8,6272]{1,0:T(8,128)(2,1)S(1)} %collective-permute-done.5.refs_6_), channel_id=1, source_target_pairs={{0,1},{1,0},{2,3},{3,2},{4,5},{5,4},{6,7},{7,6},{8,9},{9,8},{10,11... | collective-permute-start | bytes 301064 | tf_op jit(solution)/shard_map/ppermute | solution.py:507
  29.0 1.4 %collective-permute-start.14 = (bf16[8,6272]{1,0:T(8,128)(2,1)S(1)}, bf16[8,6272]{1,0:T(8,128)(2,1)S(1)}, u32[]{:S(2)}, u32[]{:S(2)}) collective-permute-start(bf16[8,6272]{1,0:T(8,128)(2,1)S(1)} %collective-permute-done.6.refs_7_), channel_id=1, source_target_pairs={{0,1},{1,0},{2,3},{3,2},{4,5},{5,4},{6,7},{7,6},{8,9},{9,8},{10,11... | collective-permute-start | bytes 301064 | tf_op jit(solution)/shard_map/ppermute | solution.py:507
  51.8 2.4 %collective-permute-start.15 = (bf16[8,8,6144]{2,1,0:T(8,128)(2,1)S(1)}, bf16[8,8,6144]{2,1,0:T(8,128)(2,1)S(1)}, u32[]{:S(2)}, u32[]{:S(2)}) collective-permute-start(bf16[8,8,6144]{2,1,0:T(8,128)(2,1)S(1)} %get-tuple-element.38), channel_id=1, source_target_pairs={{0,1},{1,0},{2,3},{3,2},{4,5},{5,4},{6,7},{7,6},{8,9},{9,8},{10,11... | collective-permute-start | bytes 2359304 | tf_op jit(solution)/shard_map/ppermute | solution.py:509
  54.4 6.7 %collective-permute-start.22 = (bf16[8,3072]{1,0:T(8,128)(2,1)S(1)}, bf16[8,3072]{1,0:T(8,128)(2,1)S(1)}, u32[]{:S(2)}, u32[]{:S(2)}) collective-permute-start(bf16[8,3072]{1,0:T(8,128)(2,1)S(1)} %get-tuple-element.40), channel_id=1, source_target_pairs={{0,4},{4,8},{8,12},{12,0},{1,5},{5,9},{9,13},{13,1},{2,6},{6,10},{... | collective-permute-start | bytes 147464 | tf_op jit(solution)/shard_map/ppermute | solution.py:514
  55.2 5.9 %collective-permute-start.21 = (bf16[8,3072]{1,0:T(8,128)(2,1)S(1)}, bf16[8,3072]{1,0:T(8,128)(2,1)S(1)}, u32[]{:S(2)}, u32[]{:S(2)}) collective-permute-start(bf16[8,3072]{1,0:T(8,128)(2,1)S(1)} %get-tuple-element.41), channel_id=1, source_target_pairs={{0,12},{4,0},{8,4},{12,8},{1,13},{5,1},{9,5},{13,9},{2,14},{6,2},{... | collective-permute-start | bytes 147464 | tf_op jit(solution)/shard_map/ppermute | solution.py:514
  58.8 5.3 %collective-permute-start.20 = (bf16[8,3072]{1,0:T(8,128)(2,1)S(1)}, bf16[8,3072]{1,0:T(8,128)(2,1)S(1)}, u32[]{:S(2)}, u32[]{:S(2)}) collective-permute-start(bf16[8,3072]{1,0:T(8,128)(2,1)S(1)} %get-tuple-element.42), channel_id=1, source_target_pairs={{0,8},{4,12},{8,0},{12,4},{1,9},{5,13},{9,1},{13,5},{2,10},{6,14},... | collective-permute-start | bytes 147464 | tf_op jit(solution)/shard_map/ppermute | solution.py:514
  59.4 5.6 %collective-permute-start.16 = (bf16[3,8,3072]{2,1,0:T(8,128)(2,1)S(1)}, bf16[3,8,3072]{2,1,0:T(8,128)(2,1)S(1)}, u32[]{:S(2)}, u32[]{:S(2)}) collective-permute-start(bf16[3,8,3072]{2,1,0:T(8,128)(2,1)S(1)} %get-tuple-element.44), channel_id=1, source_target_pairs={{0,2},{2,0},{1,3},{3,1},{4,6},{6,4},{5,7},{7,5},{8,10},{10,8},{9,1... | collective-permute-start | bytes 442376 | tf_op jit(solution)/shard_map/ppermute | solution.py:512
  64.2 6.7 %collective-permute-start.23 = (bf16[8,6144]{1,0:T(8,128)(2,1)S(1)}, bf16[8,6144]{1,0:T(8,128)(2,1)S(1)}, u32[]{:S(2)}, u32[]{:S(2)}) collective-permute-start(bf16[8,6144]{1,0:T(8,128)(2,1)S(1)} %pad_maximum_fusion.1), channel_id=1, source_target_pairs={{0,2},{2,0},{1,3},{3,1},{4,6},{6,4},{5,7},{7,5},{8,10},{10,8},{9,1... | collective-permute-start | bytes 294920 | tf_op jit(solution)/shard_map/ppermute | solution.py:523
  65.0 7.7 %collective-permute-start.19 = (bf16[8,6144]{1,0:T(8,128)(2,1)S(1)}, bf16[8,6144]{1,0:T(8,128)(2,1)S(1)}, u32[]{:S(2)}, u32[]{:S(2)}) collective-permute-start(bf16[8,6144]{1,0:T(8,128)(2,1)S(1)} %get-tuple-element.45), channel_id=1, source_target_pairs={{0,4},{4,8},{8,12},{12,0},{1,5},{5,9},{9,13},{13,1},{2,6},{6,10},{... | collective-permute-start | bytes 294920 | tf_op jit(solution)/shard_map/ppermute | solution.py:519
  66.8 8.4 %collective-permute-start.17 = (bf16[8,6144]{1,0:T(8,128)(2,1)S(1)}, bf16[8,6144]{1,0:T(8,128)(2,1)S(1)}, u32[]{:S(2)}, u32[]{:S(2)}) collective-permute-start(bf16[8,6144]{1,0:T(8,128)(2,1)S(1)} %get-tuple-element.46), channel_id=1, source_target_pairs={{0,8},{4,12},{8,0},{12,4},{1,9},{5,13},{9,1},{13,5},{2,10},{6,14},... | collective-permute-start | bytes 294920 | tf_op jit(solution)/shard_map/ppermute | solution.py:519
  68.1 7.1 %collective-permute-start.18 = (bf16[8,6144]{1,0:T(8,128)(2,1)S(1)}, bf16[8,6144]{1,0:T(8,128)(2,1)S(1)}, u32[]{:S(2)}, u32[]{:S(2)}) collective-permute-start(bf16[8,6144]{1,0:T(8,128)(2,1)S(1)} %get-tuple-element.47), channel_id=1, source_target_pairs={{0,12},{4,0},{8,4},{12,8},{1,13},{5,1},{9,5},{13,9},{2,14},{6,2},{... | collective-permute-start | bytes 294920 | tf_op jit(solution)/shard_map/ppermute | solution.py:519
